TPU v7x, 512 devices: a whole 4x8x8 slice. The times are simulated.
512 devices in a mesh: tile: 64 (over x, y, core), mem: 8 (over z).
Axes of the slice: x: 4, y: 8, z: 8, core: 2. Of those that a mesh axis runs over, the one named last changes fastest.
Arguments:
- perturb: bfloat16 [48, 2, 16, 8192], P('mem', None, None, 'tile'), may hold values from -6 to 6
- control: float32 [48, 2, 16, 8192], P('mem', None, None, 'tile'), may hold values from -6 to 6
- obs_cell: int32 [64, 64, 16], P('tile'), may hold values from 0 to 3966, as said below
- obs_count: int32 [64, 64], P('tile'), may hold values from 0 to 16, as said below
- obs_frac: float32 [64, 2, 64, 16], P('tile'), may hold values from 0 to 1
- obs_innov: float32 [64, 64, 16], P('tile'), may hold values from -6 to 6
- obs_prec: float32 [64, 64, 16], P('tile'), may hold values from 1 to 10
Outputs:
- gradient: float32 [48, 2, 16, 8192], P('mem', None, None, 'tile')
Inputs may be any that keep to these rules, and one draw needn't show every extreme that they name: `obs_count`: in every draw some owner tile receives 16 live slots from every holder tile. `obs_cell`: each corner has row below 15 and column below 127, so its stencil lies in the owner tile.
All inputs are finite; a program needn't handle non-finite values.
Results may differ from a plain program's by a relative error of at most 0.0003.
Values may be sent and summed in bfloat16 or wider, within the bound.
No kernel may reach another device: no remote copies, remote signals or barrier semaphores. Data moves between devices by JAX's collectives and lax.ppermute only.
A program may use at most 64 MiB of HBM per device.

v0:
```python
import math

import jax
import jax.numpy as jnp
from jax import lax
from jax.sharding import PartitionSpec as P

YSCALE = 1


EXACT_MODE = lax.Precision.HIGHEST


def padded(cells, sides, width):
    for axis, dim in sides:
        count = lax.axis_size(axis)
        head = lax.slice_in_dim(cells, 0, width, axis=dim)
        tail = lax.slice_in_dim(cells, cells.shape[dim] - width, cells.shape[dim], axis=dim)
        cells = jnp.concatenate(
            [
                lax.ppermute(tail, axis, [(i, (i + 1) % count) for i in range(count)]),
                cells,
                lax.ppermute(head, axis, [((i + 1) % count, i) for i in range(count)]),
            ],
            axis=dim,
        )
    return cells


def band_table(col_count):
    source_pos = jnp.arange(3 * col_count) - col_count
    target_pos = jnp.arange(col_count)
    offset = source_pos[:, None] - target_pos[None, :]
    distance = offset.astype(jnp.float32)
    weights = jnp.exp(-0.5 * distance * distance / (col_count * col_count))
    return jnp.where(jnp.abs(offset) <= col_count, weights, jnp.zeros_like(weights))


def row_table(row_count, scale):
    offset = (jnp.arange(row_count)[:, None] - jnp.arange(row_count)[None, :]).astype(jnp.float32)
    return jnp.exp(-0.5 * offset * offset / (scale * scale))


def norm_factor(col_count, row_count, scale):
    along_x = jnp.arange(-col_count, col_count + 1).astype(jnp.float32)
    along_y = jnp.arange(-(row_count - 1), row_count).astype(jnp.float32)
    total_x = jnp.sum(jnp.exp(-along_x * along_x / (col_count * col_count)))
    total_y = jnp.sum(jnp.exp(-along_y * along_y / (scale * scale)))
    return 1.0 / jnp.sqrt(total_x * total_y)


def per_device(perturb, control, obs_cell, obs_count, obs_frac, obs_innov, obs_prec):
    mem_local, levels, row_count, col_count = perturb.shape
    members = mem_local * lax.axis_size("mem")
    spread = 1.0 / math.sqrt(members - 1)
    band = band_table(col_count)
    rowmat = row_table(row_count, YSCALE)
    factor = norm_factor(col_count, row_count, YSCALE)

    def across(extended):
        swept = jnp.einsum("mlyk,kc->mlyc", extended, band, precision=EXACT_MODE)
        mixed = jnp.einsum("iy,mlyc->mlic", rowmat, swept, precision=EXACT_MODE)
        return factor * mixed

    control_ext = padded(control, (("tile", 3),), col_count)
    localized = across(control_ext)
    partial_value = spread * jnp.sum(perturb.astype(jnp.float32) * localized, axis=0)
    increment = lax.psum(partial_value, "mem")
    slot_count = obs_cell.shape[2]
    live_mask = (jnp.arange(slot_count)[None, :] < obs_count[0][:, None]).astype(jnp.float32)
    packed = jnp.stack([obs_frac[0, 0], obs_frac[0, 1], obs_innov[0], obs_prec[0] * live_mask])
    arrived, arrived_cells = (
        lax.all_to_all(packed, "tile", split_axis=1, concat_axis=1, tiled=True),
        lax.all_to_all(obs_cell, "tile", split_axis=1, concat_axis=1, tiled=True),
    )
    frac_x = arrived[0]
    frac_y = arrived[1]
    innov_recv = arrived[2]
    prec_live = arrived[3]
    corner = arrived_cells[0]
    flat_inc = increment.reshape(-1)
    weight_aa = (1.0 - frac_x) * (1.0 - frac_y)
    weight_ab = frac_x * (1.0 - frac_y)
    weight_ba = (1.0 - frac_x) * frac_y
    weight_bb = frac_x * frac_y
    value = weight_aa * jnp.take(flat_inc, corner) + weight_ab * jnp.take(flat_inc, corner + 1)
    value = value + weight_ba * jnp.take(flat_inc, corner + col_count)
    value = value + weight_bb * jnp.take(flat_inc, corner + col_count + 1)
    weighted = prec_live * (value - innov_recv)
    adjoint = jnp.zeros(flat_inc.shape, jnp.float32)
    adjoint = adjoint.at[corner].add(weighted * weight_aa)
    adjoint = adjoint.at[corner + 1].add(weighted * weight_ab)
    adjoint = adjoint.at[corner + col_count].add(weighted * weight_ba)
    adjoint = adjoint.at[corner + col_count + 1].add(weighted * weight_bb)
    adjoint = adjoint.reshape(levels, row_count, col_count)
    product = perturb.astype(jnp.float32) * adjoint[None]
    product_ext = padded(product, (("tile", 3),), col_count)
    return control + spread * across(product_ext)


def solution(mesh):
    return jax.shard_map(
        per_device,
        mesh=mesh,
        in_specs=(
            P("mem", None, None, "tile"),
            P("mem", None, None, "tile"),
            P("tile", None, None),
            P("tile", None),
            P("tile", None, None, None),
            P("tile", None, None),
            P("tile", None, None),
        ),
        out_specs=P("mem", None, None, "tile"),
        check_vma=False,
    )
```

profile of v0, /device:TPU:1, one launch (start us, length us, event | category | flops | bytes accessed | tf_op | source)
XLA Modules:
  0.0 142.7 jit_solution(14518659161094015812)
XLA Ops:
  0.0 4.6 %collective-permute-start = (f32[6,2,16,128]{3,2,1,0:T(8,128)}, f32[6,2,16,128]{3,2,1,0:T(8,128)S(1)}, u32[]{:S(2)}, u32[]{:S(2)}) collective-permute-start(f32[6,2,16,128]{3,2,1,0:T(8,128)} %param.10), channel_id=1, source_target_pairs={{0,8},{8,16},{16,24},{24,32},{32,40},{40,48},{48,56},{56,64},{64,7... | collective-permute-start | bytes 294920 | tf_op jit(solution)/shard_map/ppermute | solution.py:21
  4.6 6.1 %collective-permute-start.1 = (f32[6,2,16,128]{3,2,1,0:T(8,128)}, f32[6,2,16,128]{3,2,1,0:T(8,128)S(1)}, u32[]{:S(2)}, u32[]{:S(2)}) collective-permute-start(f32[6,2,16,128]{3,2,1,0:T(8,128)} %param.10), channel_id=1, source_target_pairs={{8,0},{16,8},{24,16},{32,24},{40,32},{48,40},{56,48},{64,56},{72,6... | collective-permute-start | bytes 294920 | tf_op jit(solution)/shard_map/ppermute | solution.py:23
  10.7 1.4 copy.13
  12.1 9.2 %all-to-all-start = ((s32[1,64,16]{2,0,1:T(1,128)}), s32[1,64,16]{2,0,1:T(1,128)S(1)}, u32[]{:S(2)}, u32[]{:S(2)}) async-start(s32[1,64,16]{2,0,1:T(1,128)} %copy.13), calls=%async_computation | async-start | bytes 65536 | tf_op jit(solution)/shard_map/all_to_all | solution.py:74
  21.4 0.7 copy-done.3
  22.1 0.7 copy-done.4
  22.8 0.6 fusion.55
  23.4 0.7 fusion.53
  25.4 0.7 copy.14
  26.1 4.6 %all-to-all-done = s32[1,64,16]{2,0,1:T(1,128)S(1)} async-done(((s32[1,64,16]{2,0,1:T(1,128)}), s32[1,64,16]{2,0,1:T(1,128)S(1)}, u32[]{:S(2)}, u32[]{:S(2)}) %all-to-all-start) | async-done | bytes 4128 | tf_op jit(solution)/shard_map/all_to_all | solution.py:74
  30.7 5.9 %all-to-all-start.1 = ((f32[4,64,16]{2,0,1:T(4,128)}), f32[4,64,16]{2,0,1:T(4,128)S(1)}, u32[]{:S(2)}, u32[]{:S(2)}) async-start(f32[4,64,16]{2,0,1:T(4,128)} %copy.14), calls=%async_computation.1 | async-start | bytes 262144 | tf_op jit(solution)/shard_map/all_to_all | solution.py:73
  36.6 0.1 reshape.228
  36.9 0.1 reshape.186
  37.2 9.7 %all-to-all-done.1 = f32[4,64,16]{2,0,1:T(4,128)S(1)} async-done(((f32[4,64,16]{2,0,1:T(4,128)}), f32[4,64,16]{2,0,1:T(4,128)S(1)}, u32[]{:S(2)}, u32[]{:S(2)}) %all-to-all-start.1) | async-done | bytes 16416 | tf_op jit(solution)/shard_map/all_to_all | solution.py:73
  46.9 0.1 fusion.69
  47.0 0.6 fusion.6
  47.6 0.2 copy-done
  47.8 0.2 fusion.5
  48.1 27.2 %psum.7 = f32[4096]{0:T(1024)S(1)} all-reduce(f32[4096]{0:T(1024)S(1)} %bitcast.63), channel_id=1, replica_groups=mesh['tile'=64,'mem'=8] {'mem'}, use_global_device_ids=true, to_apply=%region_3.4 | all-reduce | flops 4096 | bytes 32768 | tf_op jit(solution)/shard_map/psum | solution.py:68
  75.3 6.1 %gather_fusion = f32[1024]{0:T(1024)S(1)} fusion(f32[4096]{0:T(1024)S(1)} %psum.7, s32[1024]{0:T(1024)S(1)} %broadcast_clamp_fusion.3), kind=kCustom, calls=%fused_computation.clone | custom fusion | bytes 12288 | tf_op jit(solution)/shard_map/jit(_take)/gather | solution.py:86
  81.5 6.1 %gather_fusion.1 = f32[1024]{0:T(1024)S(1)} fusion(f32[4096]{0:T(1024)S(1)} %psum.7, s32[1024]{0:T(1024)S(1)} %broadcast_clamp_fusion.2), kind=kCustom, calls=%fused_computation.1.clone | custom fusion | bytes 12288 | tf_op jit(solution)/shard_map/jit(_take)/gather | solution.py:86
  87.7 6.1 %gather_fusion.2 = f32[1024]{0:T(1024)S(1)} fusion(f32[4096]{0:T(1024)S(1)} %psum.7, s32[1024]{0:T(1024)S(1)} %broadcast_clamp_fusion.1), kind=kCustom, calls=%fused_computation.2.clone | custom fusion | bytes 12288 | tf_op jit(solution)/shard_map/jit(_take)/gather | solution.py:87
  93.9 6.1 %gather_fusion.3 = f32[1024]{0:T(1024)S(1)} fusion(f32[4096]{0:T(1024)S(1)} %psum.7, s32[1024]{0:T(1024)S(1)} %broadcast_clamp_fusion), kind=kCustom, calls=%fused_computation.3.clone | custom fusion | bytes 12288 | tf_op jit(solution)/shard_map/jit(_take)/gather | solution.py:88
  100.6 5.9 %scatter_custom_fusion = f32[4096]{0:T(1024)S(1)} fusion(s32[1024]{0:T(1024)S(1)} %reshape.186, f32[1024]{0:T(1024)S(1)} %reshape.188, f32[]{:T(128)} %constant.25.clone.1), kind=kCustom, calls=%fused_computation.77 | custom fusion | flops 1024 | bytes 16388 | tf_op jit(solution)/shard_map/scatter-add | solution.py:91
  106.5 6.1 %scatter_fusion = f32[4096]{0:T(1024)S(1)} fusion(f32[4096]{0:T(1024)S(1)} %scatter_custom_fusion, s32[1024]{0:T(1024)S(1)} %reshape.194, f32[1024]{0:T(1024)S(1)} %reshape.196), kind=kCustom, calls=%fused_computation.5 | custom fusion | flops 1024 | bytes 16384 | tf_op jit(solution)/shard_map/scatter-add | solution.py:92
  112.6 6.1 %scatter_fusion.1 = f32[4096]{0:T(1024)S(1)} fusion(f32[4096]{0:T(1024)S(1)} %scatter_fusion, s32[1024]{0:T(1024)S(1)} %reshape.202, f32[1024]{0:T(1024)S(1)} %reshape.204), kind=kCustom, calls=%fused_computation.6 | custom fusion | flops 1024 | bytes 16384 | tf_op jit(solution)/shard_map/scatter-add | solution.py:93
  118.6 6.1 %scatter_fusion.2 = f32[4096]{0:T(1024)S(1)} fusion(f32[4096]{0:T(1024)S(1)} %scatter_fusion.1, s32[1024]{0:T(1024)S(1)} %reshape.210, f32[1024]{0:T(1024)S(1)} %reshape.212), kind=kCustom, calls=%fused_computation.7 | custom fusion | flops 1024 | bytes 16384 | tf_op jit(solution)/shard_map/scatter-add | solution.py:94
  124.7 10.4 %collective-permute-start.2 = (f32[6,2,16,128]{3,2,1,0:T(8,128)S(1)}, f32[6,2,16,128]{3,2,1,0:T(8,128)S(1)}, u32[]{:S(2)}, u32[]{:S(2)}) collective-permute-start(f32[6,2,16,128]{3,2,1,0:T(8,128)S(1)} %convert_multiply_fusion), channel_id=1, source_target_pairs={{0,8},{8,16},{16,24},{24,32},{32,40},{40,48},{48,56},{56,64},{64,7... | collective-permute-start | bytes 294920 | tf_op jit(solution)/shard_map/ppermute | solution.py:21
  135.2 1.9 %collective-permute-start.3 = (f32[6,2,16,128]{3,2,1,0:T(8,128)S(1)}, f32[6,2,16,128]{3,2,1,0:T(8,128)S(1)}, u32[]{:S(2)}, u32[]{:S(2)}) collective-permute-start(f32[6,2,16,128]{3,2,1,0:T(8,128)S(1)} %convert_multiply_fusion), channel_id=1, source_target_pairs={{8,0},{16,8},{24,16},{32,24},{40,32},{48,40},{56,48},{64,56},{72,6... | collective-permute-start | bytes 294920 | tf_op jit(solution)/shard_map/ppermute | solution.py:23
  137.1 4.1 %collective-permute-done.3 = f32[6,2,16,128]{3,2,1,0:T(8,128)S(1)} collective-permute-done((f32[6,2,16,128]{3,2,1,0:T(8,128)S(1)}, f32[6,2,16,128]{3,2,1,0:T(8,128)S(1)}, u32[]{:S(2)}, u32[]{:S(2)}) %collective-permute-start.3) | collective-permute-done | bytes 98336 | tf_op jit(solution)/shard_map/ppermute | solution.py:23
  141.2 0.6 fusion.12
  141.8 0.9 fusion.4
  (40 shorter events, 1.2 us)
Async XLA Ops:
  0.0 47.0 %collective-permute-start = (f32[6,2,16,128]{3,2,1,0:T(8,128)}, f32[6,2,16,128]{3,2,1,0:T(8,128)S(1)}, u32[]{:S(2)}, u32[]{:S(2)}) collective-permute-start(f32[6,2,16,128]{3,2,1,0:T(8,128)} %param.10), channel_id=1, source_target_pairs={{0,8},{8,16},{16,24},{24,32},{32,40},{40,48},{48,56},{56,64},{64,7... | collective-permute-start | bytes 294920 | tf_op jit(solution)/shard_map/ppermute | solution.py:21
  4.6 42.4 %collective-permute-start.1 = (f32[6,2,16,128]{3,2,1,0:T(8,128)}, f32[6,2,16,128]{3,2,1,0:T(8,128)S(1)}, u32[]{:S(2)}, u32[]{:S(2)}) collective-permute-start(f32[6,2,16,128]{3,2,1,0:T(8,128)} %param.10), channel_id=1, source_target_pairs={{8,0},{16,8},{24,16},{32,24},{40,32},{48,40},{56,48},{64,56},{72,6... | collective-permute-start | bytes 294920 | tf_op jit(solution)/shard_map/ppermute | solution.py:23
  12.1 9.2 %copy-start.2 = (f32[1,2,64,16]{2,3,1,0:T(8,128)S(1)}, f32[1,2,64,16]{2,3,1,0:T(8,128)}, u32[]{:S(2)}) copy-start(f32[1,2,64,16]{2,3,1,0:T(8,128)} %param.13) | copy-start | bytes 24580
  12.1 18.5 %all-to-all-start = ((s32[1,64,16]{2,0,1:T(1,128)}), s32[1,64,16]{2,0,1:T(1,128)S(1)}, u32[]{:S(2)}, u32[]{:S(2)}) async-start(s32[1,64,16]{2,0,1:T(1,128)} %copy.13), calls=%async_computation | async-start | bytes 65536 | tf_op jit(solution)/shard_map/all_to_all | solution.py:74
  21.3 0.7 copy-start.3
  21.4 0.7 copy-start.5
  22.0 0.7 copy-start.4
  30.7 16.2 %all-to-all-start.1 = ((f32[4,64,16]{2,0,1:T(4,128)}), f32[4,64,16]{2,0,1:T(4,128)S(1)}, u32[]{:S(2)}, u32[]{:S(2)}) async-start(f32[4,64,16]{2,0,1:T(4,128)} %copy.14), calls=%async_computation.1 | async-start | bytes 262144 | tf_op jit(solution)/shard_map/all_to_all | solution.py:73
  37.2 9.8 %copy-start.1 = (f32[6,2,16,128]{3,2,1,0:T(8,128)S(1)}, f32[6,2,16,128]{3,2,1,0:T(8,128)}, u32[]{:S(2)}) copy-start(f32[6,2,16,128]{3,2,1,0:T(8,128)} %param.10) | copy-start | bytes 294916
  47.0 0.8 copy-start
  124.7 12.4 %collective-permute-start.2 = (f32[6,2,16,128]{3,2,1,0:T(8,128)S(1)}, f32[6,2,16,128]{3,2,1,0:T(8,128)S(1)}, u32[]{:S(2)}, u32[]{:S(2)}) collective-permute-start(f32[6,2,16,128]{3,2,1,0:T(8,128)S(1)} %convert_multiply_fusion), channel_id=1, source_target_pairs={{0,8},{8,16},{16,24},{24,32},{32,40},{40,48},{48,56},{56,64},{64,7... | collective-permute-start | bytes 294920 | tf_op jit(solution)/shard_map/ppermute | solution.py:21
  135.2 6.0 %collective-permute-start.3 = (f32[6,2,16,128]{3,2,1,0:T(8,128)S(1)}, f32[6,2,16,128]{3,2,1,0:T(8,128)S(1)}, u32[]{:S(2)}, u32[]{:S(2)}) collective-permute-start(f32[6,2,16,128]{3,2,1,0:T(8,128)S(1)} %convert_multiply_fusion), channel_id=1, source_target_pairs={{8,0},{16,8},{24,16},{32,24},{40,32},{48,40},{56,48},{64,56},{72,6... | collective-permute-start | bytes 294920 | tf_op jit(solution)/shard_map/ppermute | solution.py:23
where the time goes:
time: 144 us; the launch traced here: 143 us
  starting transfers between devices  38.2 us (27%)
  local copies, waits for them, and re-layouts  29.6 us (21%)
  blocking collectives  27.2 us (19%)
  other arithmetic  25.6 us (18%)
  waiting for transfers between devices  18.3 us (13%)
  matrix products  2.23 us (2%)
  between operations  1.58 us (1%)
    psum x1, blocking collectives, per_device(): increment = lax.psum(partial_value, 'mem')  27.2 us
    ppermute x2, starting transfers between devices, padded(): lax.ppermute(tail, axis, [(i, (i + 1) % count) for i in range(count)])  15 us
    all_to_all x1, waiting for transfers between devices, per_device(): lax.all_to_all(packed, 'tile', split_axis=1, concat_axis=1, tiled=True)  9.66 us
    all_to_all x1, starting transfers between devices, per_device(): lax.all_to_all(obs_cell, 'tile', split_axis=1, concat_axis=1, tiled=True)  9.21 us
    ppermute x2, starting transfers between devices, padded(): lax.ppermute(head, axis, [((i + 1) % count, i) for i in range(count)])  8.04 us
    gather x2, local copies, waits for them, and re-layouts, per_device(): jnp.take(flat_inc, corner + 1)  6.22 us
    gather x2, local copies, waits for them, and re-layouts, per_device(): value = value + weight_ba * jnp.take(flat_inc, corner + col_count)  6.22 us
    gather x2, local copies, waits for them, and re-layouts, per_device(): value = value + weight_bb * jnp.take(flat_inc, corner + col_count + 1)  6.22 us
  transfers between devices with their start and end apart: 6, of which 3 were waited for; matrix products, arithmetic and copies ran while one was open for 3% of the time, Pallas kernels for 0%

commit v1 on v0

v1 whole, which is shorter than its diff:
```python
import math

import jax
import jax.numpy as jnp
import ml_dtypes
import numpy as np
from jax import lax
from jax.experimental import pallas as pl
from jax.experimental.pallas import tpu as pltpu
from jax.sharding import PartitionSpec as P

YSCALE = 1
F32 = jnp.float32
BF16 = jnp.bfloat16


def halves(table):
    high = table.astype(np.float32).astype(ml_dtypes.bfloat16)
    low = (table.astype(np.float32) - high.astype(np.float32)).astype(ml_dtypes.bfloat16)
    return high, low


def tables(col_count, row_count, scale, copies):
    offset = (np.arange(3 * col_count) - col_count)[:, None] - np.arange(col_count)[None, :]
    band = np.where(np.abs(offset) <= col_count, np.exp(-0.5 * (offset / col_count) ** 2), 0.0)
    row_offset = np.arange(row_count)[:, None] - np.arange(row_count)[None, :]
    rows = np.exp(-0.5 * (row_offset / scale) ** 2)
    along_x = np.arange(-col_count, col_count + 1)
    along_y = np.arange(-(row_count - 1), row_count)
    total = np.sum(np.exp(-((along_x / col_count) ** 2))) * np.sum(np.exp(-((along_y / scale) ** 2)))
    mixed = np.kron(np.eye(copies), rows) / np.sqrt(total)
    band_high, band_low = halves(band)
    mixed_high, mixed_low = halves(mixed)
    return (
        np.concatenate([band_high, band_high, band_low], axis=0),
        np.concatenate([mixed_high, mixed_high, mixed_low], axis=1),
    )


def split(values):
    high = values.astype(BF16)
    return high, (values - high.astype(F32)).astype(BF16)


def localize(extended, band, mixed):
    high, low = split(extended)
    swept = jnp.dot(jnp.concatenate([high, low, high], axis=1), band, preferred_element_type=F32)
    high, low = split(swept)
    return jnp.dot(mixed, jnp.concatenate([high, low, high], axis=0), preferred_element_type=F32)


def extend(even, own, near, far):
    left = jnp.where(even, far, near)
    right = jnp.where(even, near, far)
    return jnp.concatenate([left, own, right], axis=1)


def pack_kernel(cell_ref, count_ref, frac_ref, innov_ref, prec_ref, out_ref):
    tiles, slots = innov_ref.shape
    row = lax.broadcasted_iota(jnp.int32, (tiles, tiles), 0)
    col = lax.broadcasted_iota(jnp.int32, (tiles, tiles), 1)
    counts = jnp.where(row == col, jnp.broadcast_to(count_ref[...], (tiles, tiles)), 0)
    counts = jnp.sum(counts.astype(F32), axis=1, keepdims=True)
    slot = lax.broadcasted_iota(jnp.int32, (tiles, slots), 1).astype(F32)
    live = jnp.where(slot < counts, 1.0, 0.0)
    out_ref[...] = jnp.concatenate(
        [
            frac_ref[0],
            frac_ref[1],
            innov_ref[...],
            prec_ref[...] * live,
            cell_ref[...].astype(F32),
            jnp.zeros((tiles, 128 - 5 * slots), F32),
        ],
        axis=1,
    )


def partial_kernel(spread, even_ref, own_ref, near_ref, far_ref, perturb_ref, band_ref, mixed_ref, out_ref):
    even = even_ref[0] == 1
    rows = out_ref.shape[1]
    extended = extend(even, own_ref[...], near_ref[...], far_ref[...])
    localized = localize(extended, band_ref[...], mixed_ref[...])
    product = perturb_ref[...].astype(F32) * localized
    total = product[:rows]
    for start in range(rows, product.shape[0], rows):
        total = total + product[start : start + rows]
    total = spread * total
    for copy in range(out_ref.shape[0]):
        out_ref[copy] = total


def obs_kernel(slots, row_count, partial_ref, obs_ref, perturb_ref, out_ref):
    field = partial_ref[0]
    for member in range(1, partial_ref.shape[0]):
        field = field + partial_ref[member]
    rows, cols = field.shape
    turned = jnp.transpose(obs_ref[...])
    half = slots // 2

    def quantity(index):
        first = turned[index * slots : index * slots + half]
        second = turned[index * slots + half : (index + 1) * slots]
        return jnp.concatenate([first, second], axis=1)

    frac_x, frac_y, innov, prec, cell = (quantity(i) for i in range(5))
    cell = (cell + 0.5).astype(jnp.int32)
    corner_row = cell // cols
    corner_col = cell - corner_row * cols
    lanes = frac_x.shape[1]
    row_at = lax.broadcasted_iota(jnp.int32, (rows, lanes), 0)
    col_at = lax.broadcasted_iota(jnp.int32, (cols, lanes), 0)
    row_parts, col_parts = [], []
    for k in range(half):
        r, x = corner_row[k : k + 1], corner_col[k : k + 1]
        fy, fx = frac_y[k : k + 1], frac_x[k : k + 1]
        row_parts.append(jnp.where(row_at == r, 1.0 - fy, jnp.where(row_at == r + 1, fy, 0.0)))
        col_parts.append(jnp.where(col_at == x, 1.0 - fx, jnp.where(col_at == x + 1, fx, 0.0)))
    row_all = jnp.concatenate(row_parts, axis=1)
    row_high, row_low = split(row_all)
    field_high, field_low = split(jnp.transpose(field))
    picked = jnp.dot(
        jnp.concatenate([field_high, field_low, field_high], axis=1),
        jnp.concatenate([row_high, row_high, row_low], axis=0),
        preferred_element_type=F32,
    )
    weighted = []
    for k in range(half):
        value = jnp.sum(picked[:, k * lanes : (k + 1) * lanes] * col_parts[k], axis=0, keepdims=True)
        weighted.append(prec[k : k + 1] * (value - innov[k : k + 1]))
    weighted = jnp.concatenate(weighted, axis=1)
    rows_high, rows_low = split(row_all * weighted)
    cols_high, cols_low = split(jnp.concatenate(col_parts, axis=1))
    adjoint = lax.dot_general(
        jnp.concatenate([rows_high, rows_low, rows_high], axis=1),
        jnp.concatenate([cols_high, cols_high, cols_low], axis=1),
        (((1,), (1,)), ((), ())),
        preferred_element_type=F32,
    )
    for start in range(0, out_ref.shape[0], rows):
        out_ref[start : start + rows] = perturb_ref[start : start + rows].astype(F32) * adjoint


def final_kernel(spread, even_ref, control_ref, own_ref, near_ref, far_ref, band_ref, mixed_ref, out_ref):
    even = even_ref[0] == 1
    extended = extend(even, own_ref[...], near_ref[...], far_ref[...])
    out_ref[...] = control_ref[...] + spread * localize(extended, band_ref[...], mixed_ref[...])


def call(kernel, out_shape, scalars, arrays):
    specs = [pl.BlockSpec(memory_space=pltpu.SMEM)] * scalars + [pl.BlockSpec(memory_space=pltpu.VMEM)] * arrays
    return pl.pallas_call(
        kernel,
        out_shape=jax.ShapeDtypeStruct(out_shape, F32),
        in_specs=specs,
        out_specs=pl.BlockSpec(memory_space=pltpu.VMEM),
        compiler_params=pltpu.CompilerParams(vmem_limit_bytes=24 * 1024 * 1024),
    )


def per_device(perturb, control, obs_cell, obs_count, obs_frac, obs_innov, obs_prec):
    mem_local, levels, row_count, col_count = perturb.shape
    members = lax.axis_size("mem")
    tiles = lax.axis_size("tile")
    spread = 1.0 / math.sqrt(mem_local * members - 1)
    slots = obs_cell.shape[2]
    rows = levels * row_count
    band, mixed = tables(col_count, row_count, YSCALE, mem_local * levels)
    band, mixed = jnp.asarray(band), jnp.asarray(mixed)
    even = (1 - lax.axis_index("tile") % 2).astype(jnp.int32).reshape(1)
    near_pairs = [(i, i ^ 1) for i in range(tiles)]
    far_pairs = [(i, (i + 1) % tiles if i % 2 else (i - 1) % tiles) for i in range(tiles)]

    def neighbours(own):
        far = lax.ppermute(own, "tile", far_pairs)
        near = lax.ppermute(own, "tile", near_pairs)
        return near, far

    flat = mem_local * rows
    own = control.reshape(flat, col_count)
    weights = perturb.reshape(flat, col_count)

    near, far = neighbours(own)
    packed = call(pack_kernel, (tiles, 128), 0, 5)(
        obs_cell[0], obs_count, obs_frac[0], obs_innov[0], obs_prec[0]
    )
    arrived = lax.all_to_all(packed.reshape(tiles, 1, 128), "tile", split_axis=0, concat_axis=0, tiled=True)
    partials = call(lambda *refs: partial_kernel(spread, *refs), (members, rows, col_count), 1, 6)(
        even, own, near, far, weights, band, mixed
    )
    partials = lax.all_to_all(partials, "mem", split_axis=0, concat_axis=0, tiled=True)
    product = call(lambda *refs: obs_kernel(slots, row_count, *refs), (flat, col_count), 0, 3)(
        partials, arrived.reshape(tiles, 128), weights
    )
    near, far = neighbours(product)
    gradient = call(lambda *refs: final_kernel(spread, *refs), (flat, col_count), 1, 6)(
        even, own, product, near, far, band, mixed
    )
    return gradient.reshape(control.shape)


def solution(mesh):
    return jax.shard_map(
        per_device,
        mesh=mesh,
        in_specs=(
            P("mem", None, None, "tile"),
            P("mem", None, None, "tile"),
            P("tile", None, None),
            P("tile", None),
            P("tile", None, None, None),
            P("tile", None, None),
            P("tile", None, None),
        ),
        out_specs=P("mem", None, None, "tile"),
        check_vma=False,
    )
```

time: 144 us -> 58.5 us (0.41)
  other arithmetic: 25.6 us -> 0 us
  local copies, waits for them, and re-layouts: 29.6 us -> 4.75 us
  starting transfers between devices: 38.2 us -> 24.6 us
  blocking collectives: 27.2 us -> 15.8 us
  waiting for transfers between devices: 18.3 us -> 8.96 us
  Pallas kernels: 0 us -> 3.31 us
  matrix products: 2.23 us -> 0 us
  between operations: 1.58 us -> 0.13 us
    psum x1 -> x0, blocking collectives: 27.2 us -> none  [per_device(): increment = lax.psum(partial_value, 'mem')]
    gather x8 -> x0, local copies, waits for them, and re-layouts: 24.9 us -> none  [the longest x2 6.22 us: per_device(): jnp.take(flat_inc, corner + 1)]
    scatter-add x4 -> x0, other arithmetic: 24.1 us -> none  [the longest x1 6.07 us: per_device(): adjoint = adjoint.at[corner + 1].add(weighted * weight_ab)]
    all_to_all x0 -> x1, blocking collectives: none -> 15.8 us  [per_device(): lax.all_to_all(partials, 'mem', split_axis=0, concat_axis=0, tiled=True)]
    all_to_all x2 -> x1, starting transfers between devices: 15.1 us -> 7.41 us  [per_device(): lax.all_to_all(packed.reshape(tiles, 1, 128), 'tile', split_axis=0, conca...]
    all_to_all x2 -> x1, waiting for transfers between devices: 14.2 us -> 7.68 us  [per_device(): lax.all_to_all(packed.reshape(tiles, 1, 128), 'tile', split_axis=0, conca...]
    ppermute x4, starting transfers between devices: 23.1 us -> 17.2 us  [the longest x2 9.15 us: neighbours(): far = lax.ppermute(own, 'tile', far_pairs)]
    pallas_call x0 -> x4, Pallas kernels: none -> 3.31 us  [the longest x1 1.15 us: per_device(): call(lambda *refs: final_kernel(spread, *refs), (flat, col_count), 1, 6)]
  transfers between devices with their start and end apart: 6 -> 5, of which waited for: 3 -> 3; matrix products, arithmetic and copies ran while one was open for 3% -> 5% of each run, Pallas kernels for 0% -> 2%
where the time goes in v1:
time: 58.5 us; the launch traced here: 57.6 us
  starting transfers between devices  24.6 us (42%)
  blocking collectives  15.8 us (27%)
  waiting for transfers between devices  8.96 us (15%)
  local copies, waits for them, and re-layouts  4.75 us (8%)
  Pallas kernels  3.31 us (6%)
    all_to_all x1, blocking collectives, per_device(): lax.all_to_all(partials, 'mem', split_axis=0, concat_axis=0, tiled=True)  15.8 us
    ppermute x2, starting transfers between devices, neighbours(): far = lax.ppermute(own, 'tile', far_pairs)  9.15 us
    ppermute x2, starting transfers between devices, neighbours(): near = lax.ppermute(own, 'tile', near_pairs)  8.04 us
    all_to_all x1, waiting for transfers between devices, per_device(): lax.all_to_all(packed.reshape(tiles, 1, 128), 'tile', split_axis=0, conca...  7.68 us
    all_to_all x1, starting transfers between devices, per_device(): lax.all_to_all(packed.reshape(tiles, 1, 128), 'tile', split_axis=0, conca...  7.41 us
    unnamed x16, local copies, waits for them, and re-layouts  4.75 us
  transfers between devices with their start and end apart: 5, of which 3 were waited for; matrix products, arithmetic and copies ran while one was open for 5% of the time, Pallas kernels for 2%

profile of v1, /device:TPU:1, one launch (start us, length us, event | category | flops | bytes accessed | tf_op | source)
XLA Modules:
  0.0 57.6 jit_solution(18104387281283436089)
XLA Ops:
  0.0 0.0 copy-start
  0.0 4.7 %collective-permute-start.1 = (f32[192,128]{1,0:T(8,128)}, f32[192,128]{1,0:T(8,128)S(1)}, u32[]{:S(2)}, u32[]{:S(2)}) collective-permute-start(f32[192,128]{1,0:T(8,128)} %bitcast.12), channel_id=1, source_target_pairs={{0,504},{8,16},{16,8},{24,32},{32,24},{40,48},{48,40},{56,64},{64,... | collective-permute-start | bytes 294920 | tf_op jit(solution)/shard_map/ppermute | solution.py:175
  4.7 6.1 %collective-permute-start = (f32[192,128]{1,0:T(8,128)}, f32[192,128]{1,0:T(8,128)S(1)}, u32[]{:S(2)}, u32[]{:S(2)}) collective-permute-start(f32[192,128]{1,0:T(8,128)} %bitcast.13), channel_id=1, source_target_pairs={{0,8},{8,0},{16,24},{24,16},{32,40},{40,32},{48,56},{56,48},{64,72... | collective-permute-start | bytes 294920 | tf_op jit(solution)/shard_map/ppermute | solution.py:176
  10.8 0.8 %copy.14 = s32[1,64,16]{2,1,0:T(8,128)S(1)} copy(s32[1,64,16]{1,2,0:T(8,128)} %param.11) | data formatting | bytes 8192 | tf_op args[2]
  11.6 0.8 %copy.16 = f32[1,64,16]{2,1,0:T(8,128)S(1)} copy(f32[1,64,16]{1,2,0:T(8,128)} %param.14) | data formatting | bytes 8192 | tf_op args[5]
  12.4 0.8 %copy.17 = f32[1,64,16]{2,1,0:T(8,128)S(1)} copy(f32[1,64,16]{1,2,0:T(8,128)} %param.15) | data formatting | bytes 8192 | tf_op args[6]
  13.2 0.8 %copy.15 = f32[1,2,64,16]{3,2,1,0:T(8,128)S(1)} copy(f32[1,2,64,16]{2,3,1,0:T(8,128)} %param.13) | data formatting | bytes 16384 | tf_op args[4]
  14.0 0.0 copy-start.5
  14.0 0.7 %copy-done.5 = s32[1,64]{1,0:T(1,128)S(1)} copy-done((s32[1,64]{1,0:T(1,128)S(1)}, s32[1,64]{1,0:T(1,128)}, u32[]{:S(2)}) %copy-start.5) | copy-done | bytes 280
  14.6 0.0 copy-start.4
  14.6 0.8 %shard_map.92 = f32[64,128]{1,0:T(8,128)} custom-call(s32[64,16]{1,0:T(8,128)S(1)} %bitcast.20, s32[1,64]{1,0:T(1,128)S(1)} %copy-done.5, f32[2,64,16]{2,1,0:T(8,128)S(1)} %bitcast.16, f32[64,16]{1,0:T(8,128)S(1)} %bitcast.21, f32[64,16]{1,0:T(8,128)S(1)} %bitcast.22), custom_call_target="tpu_custom_call" | custom-call | tf_op jit(solution)/shard_map/pallas_call | solution.py:184
  15.4 0.0 copy-start.3
  15.4 7.4 %all-to-all-start.1 = ((f32[64,1,128]{2,1,0:T(1,128)}), f32[64,1,128]{2,1,0:T(1,128)S(1)}, u32[]{:S(2)}, u32[]{:S(2)}) async-start(f32[64,1,128]{2,1,0:T(1,128)} %bitcast.8), calls=%async_computation.1 | async-start | bytes 65536 | tf_op jit(solution)/shard_map/all_to_all | solution.py:187
  22.9 0.0 collective-permute-done.1.refs_3_
  22.9 0.0 collective-permute-done.refs_2_
  22.9 0.0 copy-done
  22.9 0.0 copy-done.4
  22.9 0.0 copy-done.3
  22.9 0.0 copy-start.1
  22.9 0.9 %copy-done.1 = bf16[192,576]{1,0:T(8,128)(2,1)S(1)} copy-done((bf16[192,576]{1,0:T(8,128)(2,1)S(1)}, bf16[192,576]{1,0:T(8,128)(2,1)}, u32[]{:S(2)}) %copy-start.1) | copy-done | bytes 221208
  23.9 0.5 shard_map.91
  24.4 0.0 copy-start.2
  24.4 7.7 %all-to-all-done.1 = f32[64,1,128]{2,1,0:T(1,128)S(1)} async-done(((f32[64,1,128]{2,1,0:T(1,128)}), f32[64,1,128]{2,1,0:T(1,128)S(1)}, u32[]{:S(2)}, u32[]{:S(2)}) %all-to-all-start.1) | async-done | bytes 32800 | tf_op jit(solution)/shard_map/all_to_all | solution.py:187
  32.1 15.8 %all_to_all.10.refs_0_ = f32[8,32,128]{2,1,0:T(8,128)S(1)} all-to-all(f32[8,32,128]{2,1,0:T(8,128)S(1)} %shard_map.91), channel_id=1, replica_groups=mesh['tile'=64,'mem'=8] {'mem'}, dimensions={0} | all-to-all | bytes 262144 | tf_op jit(solution)/shard_map/all_to_all | solution.py:191
  47.9 0.9 %shard_map.93.refs_2_ = f32[192,128]{1,0:T(8,128)S(1)} custom-call(f32[8,32,128]{2,1,0:T(8,128)S(1)} %all_to_all.10.refs_0_, f32[64,128]{1,0:T(8,128)S(1)} %bitcast.19, bf16[192,128]{1,0:T(8,128)(2,1)S(1)} %bitcast.18), custom_call_target="tpu_custom_call" | custom-call | tf_op jit(solution)/shard_map/pallas_call | solution.py:192
  48.8 4.4 %collective-permute-start.3 = (f32[192,128]{1,0:T(8,128)S(1)}, f32[192,128]{1,0:T(8,128)S(1)}, u32[]{:S(2)}, u32[]{:S(2)}) collective-permute-start(f32[192,128]{1,0:T(8,128)S(1)} %shard_map.93.refs_2_), channel_id=1, source_target_pairs={{0,504},{8,16},{16,8},{24,32},{32,24},{40,48},{48,40},{56,64},{64,... | collective-permute-start | bytes 294920 | tf_op jit(solution)/shard_map/ppermute | solution.py:175
  53.2 1.9 %collective-permute-start.2 = (f32[192,128]{1,0:T(8,128)S(1)}, f32[192,128]{1,0:T(8,128)S(1)}, u32[]{:S(2)}, u32[]{:S(2)}) collective-permute-start(f32[192,128]{1,0:T(8,128)S(1)} %shard_map.93.refs_2_), channel_id=1, source_target_pairs={{0,8},{8,0},{16,24},{24,16},{32,40},{40,32},{48,56},{56,48},{64,72... | collective-permute-start | bytes 294920 | tf_op jit(solution)/shard_map/ppermute | solution.py:176
  55.2 0.4 collective-permute-done.3.refs_4_
  55.5 0.9 %collective-permute-done.2.refs_3_ = f32[192,128]{1,0:T(8,128)S(1)} collective-permute-done((f32[192,128]{1,0:T(8,128)S(1)}, f32[192,128]{1,0:T(8,128)S(1)}, u32[]{:S(2)}, u32[]{:S(2)}) %collective-permute-start.2) | collective-permute-done | bytes 98336 | tf_op jit(solution)/shard_map/ppermute | solution.py:176
  56.4 0.0 copy-done.2
  56.4 1.1 %shard_map.94 = f32[192,128]{1,0:T(8,128)} custom-call(s32[1]{0:T(128)} %bitcast.refs_0_, f32[192,128]{1,0:T(8,128)S(1)} %bitcast.15, f32[192,128]{1,0:T(8,128)S(1)} %shard_map.93.refs_2_, f32[192,128]{1,0:T(8,128)S(1)} %collective-permute-done.2.refs_3_, f32[192,128]{1,0:T(8,128)S(1)} %collective-permute-done.3.refs_4_, bf16[1152,128]{1,0:T(8,128)(2,1)S(1)} %copy-done, ...), custom_call_target="tpu_custom_call" | custom-call | tf_op jit(solution)/shard_map/pallas_call | solution.py:196
Async XLA Ops:
  0.0 22.9 %copy-start = (bf16[1152,128]{1,0:T(8,128)(2,1)S(1)}, bf16[1152,128]{1,0:T(8,128)(2,1)}, u32[]{:S(2)}) copy-start(bf16[1152,128]{1,0:T(8,128)(2,1)} %constant.24.clone.refs_5_) | copy-start | bytes 884740
  0.0 22.9 %collective-permute-start.1 = (f32[192,128]{1,0:T(8,128)}, f32[192,128]{1,0:T(8,128)S(1)}, u32[]{:S(2)}, u32[]{:S(2)}) collective-permute-start(f32[192,128]{1,0:T(8,128)} %bitcast.12), channel_id=1, source_target_pairs={{0,504},{8,16},{16,8},{24,32},{32,24},{40,48},{48,40},{56,64},{64,... | collective-permute-start | bytes 294920 | tf_op jit(solution)/shard_map/ppermute | solution.py:175
  4.7 18.1 %collective-permute-start = (f32[192,128]{1,0:T(8,128)}, f32[192,128]{1,0:T(8,128)S(1)}, u32[]{:S(2)}, u32[]{:S(2)}) collective-permute-start(f32[192,128]{1,0:T(8,128)} %bitcast.13), channel_id=1, source_target_pairs={{0,8},{8,0},{16,24},{24,16},{32,40},{40,32},{48,56},{56,48},{64,72... | collective-permute-start | bytes 294920 | tf_op jit(solution)/shard_map/ppermute | solution.py:176
  14.0 0.7 %copy-start.5 = (s32[1,64]{1,0:T(1,128)S(1)}, s32[1,64]{1,0:T(1,128)}, u32[]{:S(2)}) copy-start(s32[1,64]{1,0:T(1,128)} %count_ref.1) | copy-start | bytes 772
  14.6 8.2 %copy-start.4 = (bf16[6,2,16,128]{3,2,1,0:T(8,128)(2,1)S(1)}, bf16[6,2,16,128]{3,2,1,0:T(8,128)(2,1)}, u32[]{:S(2)}) copy-start(bf16[6,2,16,128]{3,2,1,0:T(8,128)(2,1)} %param.9) | copy-start | bytes 147460
  15.4 7.5 %copy-start.3 = (f32[6,2,16,128]{3,2,1,0:T(8,128)S(1)}, f32[6,2,16,128]{3,2,1,0:T(8,128)}, u32[]{:S(2)}) copy-start(f32[6,2,16,128]{3,2,1,0:T(8,128)} %param.10) | copy-start | bytes 294916
  15.4 16.6 %all-to-all-start.1 = ((f32[64,1,128]{2,1,0:T(1,128)}), f32[64,1,128]{2,1,0:T(1,128)S(1)}, u32[]{:S(2)}, u32[]{:S(2)}) async-start(f32[64,1,128]{2,1,0:T(1,128)} %bitcast.8), calls=%async_computation.1 | async-start | bytes 65536 | tf_op jit(solution)/shard_map/all_to_all | solution.py:187
  22.9 0.9 %copy-start.1 = (bf16[192,576]{1,0:T(8,128)(2,1)S(1)}, bf16[192,576]{1,0:T(8,128)(2,1)}, u32[]{:S(2)}) copy-start(bf16[192,576]{1,0:T(8,128)(2,1)} %constant.25.clone.refs_6_) | copy-start | bytes 663556
  24.4 32.1 %copy-start.2 = (bf16[192,576]{1,0:T(8,128)(2,1)S(1)}, bf16[192,576]{1,0:T(8,128)(2,1)}, u32[]{:S(2)}) copy-start(bf16[192,576]{1,0:T(8,128)(2,1)} %constant.25.clone.refs_6_) | copy-start | bytes 663556
  48.8 6.7 %collective-permute-start.3 = (f32[192,128]{1,0:T(8,128)S(1)}, f32[192,128]{1,0:T(8,128)S(1)}, u32[]{:S(2)}, u32[]{:S(2)}) collective-permute-start(f32[192,128]{1,0:T(8,128)S(1)} %shard_map.93.refs_2_), channel_id=1, source_target_pairs={{0,504},{8,16},{16,8},{24,32},{32,24},{40,48},{48,40},{56,64},{64,... | collective-permute-start | bytes 294920 | tf_op jit(solution)/shard_map/ppermute | solution.py:175
  53.2 3.2 %collective-permute-start.2 = (f32[192,128]{1,0:T(8,128)S(1)}, f32[192,128]{1,0:T(8,128)S(1)}, u32[]{:S(2)}, u32[]{:S(2)}) collective-permute-start(f32[192,128]{1,0:T(8,128)S(1)} %shard_map.93.refs_2_), channel_id=1, source_target_pairs={{0,8},{8,0},{16,24},{24,16},{32,40},{40,32},{48,56},{56,48},{64,72... | collective-permute-start | bytes 294920 | tf_op jit(solution)/shard_map/ppermute | solution.py:176

commit v2 on v1

v2 whole, which is shorter than its diff:
```python
import math

import jax
import jax.numpy as jnp
import ml_dtypes
import numpy as np
from jax import lax
from jax.experimental import pallas as pl
from jax.experimental.pallas import tpu as pltpu
from jax.sharding import PartitionSpec as P

YSCALE = 1
F32 = jnp.float32
BF16 = jnp.bfloat16


def halves(table):
    high = table.astype(np.float32).astype(ml_dtypes.bfloat16)
    low = (table.astype(np.float32) - high.astype(np.float32)).astype(ml_dtypes.bfloat16)
    return high, low


def tables(col_count, row_count, scale, levels):
    offset = (np.arange(3 * col_count) - col_count)[:, None] - np.arange(col_count)[None, :]
    band = np.where(np.abs(offset) <= col_count, np.exp(-0.5 * (offset / col_count) ** 2), 0.0)
    row_offset = np.arange(row_count)[:, None] - np.arange(row_count)[None, :]
    rows = np.exp(-0.5 * (row_offset / scale) ** 2)
    along_x = np.arange(-col_count, col_count + 1)
    along_y = np.arange(-(row_count - 1), row_count)
    total = np.sum(np.exp(-((along_x / col_count) ** 2))) * np.sum(np.exp(-((along_y / scale) ** 2)))
    mixed = np.kron(np.eye(levels), rows) / np.sqrt(total)
    band_high, band_low = halves(band)
    mixed_high, mixed_low = halves(mixed)
    mixed = np.concatenate([mixed_high, mixed_high, mixed_low], axis=1)
    mixed = np.pad(mixed, ((0, 0), (0, col_count - mixed.shape[1])))
    return np.concatenate([band_high, band_low, mixed], axis=0)


def split(values):
    high = values.astype(BF16)
    return high, (values - high.astype(F32)).astype(BF16)


def localize(extended, table_ref, rows):
    depth, cols = extended.shape[1], table_ref.shape[1]
    band_high, band_low = table_ref[:depth], table_ref[depth : 2 * depth]
    mixed = table_ref[2 * depth :, : 3 * rows]
    high, low = split(extended)
    swept = jnp.dot(
        jnp.concatenate([high, low, high], axis=1),
        jnp.concatenate([band_high, band_high, band_low], axis=0),
        preferred_element_type=F32,
    )
    swept = jnp.concatenate([swept[start : start + rows] for start in range(0, swept.shape[0], rows)], axis=1)
    high, low = split(swept)
    return jnp.dot(mixed, jnp.concatenate([high, low, high], axis=0), preferred_element_type=F32)


def extend(even, own, near, far):
    left = jnp.where(even, far, near)
    right = jnp.where(even, near, far)
    return jnp.concatenate([left, own, right], axis=1)


def pack_kernel(cell_ref, count_ref, frac_ref, innov_ref, prec_ref, out_ref):
    slots, tiles = innov_ref.shape
    cols = out_ref.shape[1]
    slot = lax.broadcasted_iota(jnp.int32, (slots, tiles), 0)
    live = jnp.where(slot < count_ref[...], 1.0, 0.0)
    cell = cell_ref[...]
    corner_row = cell // cols
    corner_col = cell - corner_row * cols
    packed = jnp.concatenate(
        [
            corner_col.astype(F32) + frac_ref[0],
            corner_row.astype(F32) + frac_ref[1],
            innov_ref[...],
            prec_ref[...] * live,
            jnp.zeros((out_ref.shape[1] - 4 * slots, tiles), F32),
        ],
        axis=0,
    )
    out_ref[...] = jnp.transpose(packed)


def partial_kernel(
    spread, slots, place_ref, own_ref, near_ref, far_ref, perturb_ref, obs_ref, table_ref, out_ref
):
    even = place_ref[0] == 1
    copies, cols = out_ref.shape[0], out_ref.shape[2]
    rows = table_ref.shape[0] - 6 * cols
    extended = extend(even, own_ref[...], near_ref[...], far_ref[...])
    localized = localize(extended, table_ref, rows)
    total = jnp.zeros((rows, cols), F32)
    for member in range(own_ref.shape[0] // rows):
        weights = perturb_ref[member * rows : (member + 1) * rows].astype(F32)
        total = total + weights * localized[:, member * cols : (member + 1) * cols]
    total = spread * total
    for copy in range(copies):
        out_ref[copy, :rows] = total

    @pl.when(place_ref[1] == 0)
    def _():
        turned = jnp.transpose(obs_ref[...])
        half = slots // 2
        for index in range(4):
            first = turned[index * slots : index * slots + half]
            second = turned[index * slots + half : (index + 1) * slots]
            quantity = jnp.concatenate([first, second], axis=1)
            for copy in range(copies):
                out_ref[copy, rows + index * half : rows + (index + 1) * half] = quantity

    @pl.when(place_ref[1] != 0)
    def _():
        for copy in range(copies):
            out_ref[copy, rows:] = jnp.zeros((out_ref.shape[1] - rows, cols), F32)


def obs_kernel(half, partial_ref, perturb_ref, out_ref):
    rows = partial_ref.shape[1] - 4 * half
    field = partial_ref[0, :rows]
    for member in range(1, partial_ref.shape[0]):
        field = field + partial_ref[member, :rows]
    cols = field.shape[1]
    at_x, at_y, innov, prec = (partial_ref[0, rows + i * half : rows + (i + 1) * half] for i in range(4))
    corner_col, corner_row = at_x.astype(jnp.int32), at_y.astype(jnp.int32)
    frac_x, frac_y = at_x - corner_col.astype(F32), at_y - corner_row.astype(F32)
    lanes = at_x.shape[1]
    row_at = lax.broadcasted_iota(jnp.int32, (rows, lanes), 0)
    col_at = lax.broadcasted_iota(jnp.int32, (cols, lanes), 0)
    row_parts, col_parts = [], []
    for k in range(half):
        r, x = corner_row[k : k + 1], corner_col[k : k + 1]
        fy, fx = frac_y[k : k + 1], frac_x[k : k + 1]
        row_parts.append(jnp.where(row_at == r, 1.0 - fy, jnp.where(row_at == r + 1, fy, 0.0)))
        col_parts.append(jnp.where(col_at == x, 1.0 - fx, jnp.where(col_at == x + 1, fx, 0.0)))
    row_all = jnp.concatenate(row_parts, axis=1)
    row_high, row_low = split(row_all)
    field_high, field_low = split(jnp.transpose(field))
    picked = jnp.dot(
        jnp.concatenate([field_high, field_low, field_high], axis=1),
        jnp.concatenate([row_high, row_high, row_low], axis=0),
        preferred_element_type=F32,
    )
    weighted = []
    for k in range(half):
        value = jnp.sum(picked[:, k * lanes : (k + 1) * lanes] * col_parts[k], axis=0, keepdims=True)
        weighted.append(prec[k : k + 1] * (value - innov[k : k + 1]))
    weighted = jnp.concatenate(weighted, axis=1)
    rows_high, rows_low = split(row_all * weighted)
    cols_high, cols_low = split(jnp.concatenate(col_parts, axis=1))
    adjoint = lax.dot_general(
        jnp.concatenate([rows_high, rows_low, rows_high], axis=1),
        jnp.concatenate([cols_high, cols_high, cols_low], axis=1),
        (((1,), (1,)), ((), ())),
        preferred_element_type=F32,
    )
    for start in range(0, out_ref.shape[0], rows):
        out_ref[start : start + rows] = perturb_ref[start : start + rows].astype(F32) * adjoint


def final_kernel(spread, place_ref, control_ref, own_ref, near_ref, far_ref, table_ref, out_ref):
    even = place_ref[0] == 1
    cols = out_ref.shape[1]
    rows = table_ref.shape[0] - 6 * cols
    extended = extend(even, own_ref[...], near_ref[...], far_ref[...])
    localized = localize(extended, table_ref, rows)
    for member in range(out_ref.shape[0] // rows):
        part = slice(member * rows, (member + 1) * rows)
        out_ref[part] = control_ref[part] + spread * localized[:, member * cols : (member + 1) * cols]


def call(kernel, out_shape, scalars, arrays):
    specs = [pl.BlockSpec(memory_space=pltpu.SMEM)] * scalars + [pl.BlockSpec(memory_space=pltpu.VMEM)] * arrays
    return pl.pallas_call(
        kernel,
        out_shape=jax.ShapeDtypeStruct(out_shape, F32),
        in_specs=specs,
        out_specs=pl.BlockSpec(memory_space=pltpu.VMEM),
        compiler_params=pltpu.CompilerParams(vmem_limit_bytes=24 * 1024 * 1024),
    )


def per_device(perturb, control, obs_cell, obs_count, obs_frac, obs_innov, obs_prec):
    mem_local, levels, row_count, col_count = perturb.shape
    members = lax.axis_size("mem")
    tiles = lax.axis_size("tile")
    spread = 1.0 / math.sqrt(mem_local * members - 1)
    slots = obs_cell.shape[2]
    rows = levels * row_count
    table = jnp.asarray(tables(col_count, row_count, YSCALE, levels))
    even = 1 - lax.axis_index("tile") % 2
    plane = lax.axis_index("mem")
    place = jnp.stack([even, plane]).astype(jnp.int32)
    near_pairs = [(i, i ^ 1) for i in range(tiles)]
    far_pairs = [(i, (i + 1) % tiles if i % 2 else (i - 1) % tiles) for i in range(tiles)]

    def neighbours(own):
        far = lax.ppermute(own, "tile", far_pairs)
        near = lax.ppermute(own, "tile", near_pairs)
        return near, far

    def route(cell, count, frac, innov, prec):
        packed = call(pack_kernel, (tiles, col_count), 0, 5)(
            cell[0].T, count, frac[0].transpose(0, 2, 1), innov[0].T, prec[0].T
        )
        packed = packed.reshape(tiles, 1, col_count)
        arrived = lax.all_to_all(packed, "tile", split_axis=0, concat_axis=0, tiled=True)
        return arrived.reshape(tiles, col_count)

    def skip(cell, count, frac, innov, prec):
        return jnp.zeros((tiles, col_count), F32)

    flat = mem_local * rows
    own = control.reshape(flat, col_count)
    weights = perturb.reshape(flat, col_count)

    near, far = neighbours(own)
    arrived = lax.cond(plane == 0, route, skip, obs_cell, obs_count, obs_frac, obs_innov, obs_prec)
    partials = call(lambda *refs: partial_kernel(spread, slots, *refs), (members, rows + 2 * slots, col_count), 1, 6)(
        place, own, near, far, weights, arrived, table
    )
    partials = lax.all_to_all(partials, "mem", split_axis=0, concat_axis=0, tiled=True)
    product = call(lambda *refs: obs_kernel(slots // 2, *refs), (flat, col_count), 0, 2)(partials, weights)
    near, far = neighbours(product)
    gradient = call(lambda *refs: final_kernel(spread, *refs), (flat, col_count), 1, 5)(
        place, own, product, near, far, table
    )
    return gradient.reshape(control.shape)


def solution(mesh):
    return jax.shard_map(
        per_device,
        mesh=mesh,
        in_specs=(
            P("mem", None, None, "tile"),
            P("mem", None, None, "tile"),
            P("tile", None, None),
            P("tile", None),
            P("tile", None, None, None),
            P("tile", None, None),
            P("tile", None, None),
        ),
        out_specs=P("mem", None, None, "tile"),
        check_vma=False,
    )
```

time: 58.5 us -> 54.1 us (0.925)
  blocking collectives: 15.8 us -> 29.8 us
  starting transfers between devices: 24.6 us -> 16.8 us
  waiting for transfers between devices: 8.96 us -> 1.27 us
  local copies, waits for them, and re-layouts: 4.75 us -> 0.9 us
  Pallas kernels: 3.31 us -> 4.3 us
    all_to_all x0 -> x1, blocking collectives: none -> 16.4 us  [route(): lax.all_to_all(packed, 'tile', split_axis=0, concat_axis=0, tiled=True)]
    all_to_all x1 -> x0, waiting for transfers between devices: 7.68 us -> none  [per_device(): lax.all_to_all(packed.reshape(tiles, 1, 128), 'tile', split_axis=0, conca...]
    all_to_all x1 -> x0, starting transfers between devices: 7.41 us -> none  [per_device(): lax.all_to_all(packed.reshape(tiles, 1, 128), 'tile', split_axis=0, conca...]
    unnamed x16 -> x8, local copies, waits for them, and re-layouts: 4.75 us -> 0.9 us
    all_to_all x1, blocking collectives: 15.8 us -> 13.4 us  [per_device(): lax.all_to_all(partials, 'mem', split_axis=0, concat_axis=0, tiled=True)]
    pallas_call x4, Pallas kernels: 3.31 us -> 4.3 us  [the longest x1 1.61 us: per_device(): call(lambda *refs: final_kernel(spread, *refs), (flat, col_count), 1, 5)]
  transfers between devices with their start and end apart: 5 -> 4, of which waited for: 3 -> 2; matrix products, arithmetic and copies ran while one was open for 5% -> 0% of each run, Pallas kernels for 2% -> 2%
where the time goes in v2:
time: 54.1 us; the launch traced here: 53.2 us
  blocking collectives  29.8 us (55%)
  starting transfers between devices  16.8 us (31%)
  Pallas kernels  4.3 us (8%)
  waiting for transfers between devices  1.27 us (2%)
  local copies, waits for them, and re-layouts  0.9 us (2%)
    all_to_all x1, blocking collectives, route(): lax.all_to_all(packed, 'tile', split_axis=0, concat_axis=0, tiled=True)  16.4 us
    all_to_all x1, blocking collectives, per_device(): lax.all_to_all(partials, 'mem', split_axis=0, concat_axis=0, tiled=True)  13.4 us
    ppermute x2, starting transfers between devices, neighbours(): far = lax.ppermute(own, 'tile', far_pairs)  8.72 us
    ppermute x2, starting transfers between devices, neighbours(): near = lax.ppermute(own, 'tile', near_pairs)  8.04 us
    pallas_call x1, Pallas kernels, per_device(): call(lambda *refs: final_kernel(spread, *refs), (flat, col_count), 1, 5)  1.61 us
    pallas_call x1, Pallas kernels, per_device(): call(lambda *refs: partial_kernel(spread, slots, *refs), (members, rows +...  1.1 us
  transfers between devices with their start and end apart: 4, of which 2 were waited for; matrix products, arithmetic and copies ran while one was open for 0% of the time, Pallas kernels for 2%

profile of v2, /device:TPU:1, one launch (start us, length us, event | category | flops | bytes accessed | tf_op | source)
XLA Modules:
  0.0 53.2 jit_solution(10422358835450613925)
XLA Ops:
  0.0 0.0 copy-start
  0.0 4.7 %collective-permute-start.1 = (f32[192,128]{1,0:T(8,128)}, f32[192,128]{1,0:T(8,128)S(1)}, u32[]{:S(2)}, u32[]{:S(2)}) collective-permute-start(f32[192,128]{1,0:T(8,128)} %bitcast.21), channel_id=1, source_target_pairs={{0,504},{8,16},{16,8},{24,32},{32,24},{40,48},{48,40},{56,64},{64,... | collective-permute-start | bytes 294920 | tf_op jit(solution)/shard_map/ppermute | solution.py:199
  4.7 6.1 %collective-permute-start = (f32[192,128]{1,0:T(8,128)}, f32[192,128]{1,0:T(8,128)S(1)}, u32[]{:S(2)}, u32[]{:S(2)}) collective-permute-start(f32[192,128]{1,0:T(8,128)} %bitcast.22), channel_id=1, source_target_pairs={{0,8},{8,0},{16,24},{24,16},{32,40},{40,32},{48,56},{56,48},{64,72... | collective-permute-start | bytes 294920 | tf_op jit(solution)/shard_map/ppermute | solution.py:200
  10.9 0.0 copy-start.3
  10.9 17.2 %conditional.1 = (f32[64,128]{1,0:T(8,128)S(1)}) conditional(s32[]{:T(128)} %convert_element_type.3, () %tuple.11, (s32[1,64,16]{1,2,0:T(8,128)}, f32[1,2,64,16]{2,3,1,0:T(8,128)}, f32[1,64,16]{1,2,0:T(8,128)}, f32[1,64,16]{1,2,0:T(8,128)}, s32[1,64]{1,0:T(1,128)}) %tuple.12), branch_computations={%region_0.1_spmd, %region_1.2_spmd} | conditional | bytes 65544 | solution.py:219
  10.9 0.9 %branch_1_fun.1 = f32[64,128]{1,0:T(8,128)S(1)} custom-call(s32[16,64]{1,0:T(8,128)} %bitcast.30, s32[1,64]{1,0:T(1,128)} %get-tuple-element.32.count_ref, f32[2,16,64]{2,1,0:T(8,128)} %bitcast.29, f32[16,64]{1,0:T(8,128)} %bitcast.31, f32[16,64]{1,0:T(8,128)} %bitcast.32), custom_call_target="tpu_custom_call" | custom-call | tf_op jit(solution)/shard_map/cond/branch_1_fun/pallas_call | solution.py:204
  11.8 16.4 %all_to_all.9 = f32[64,1,128]{2,1,0:T(1,128)S(1)} all-to-all(f32[64,1,128]{2,1,0:T(1,128)S(1)} %bitcast.27), channel_id=1, replica_groups=mesh['tile'=64,'mem'=8] {'tile'}, dimensions={0} | all-to-all | bytes 65536 | tf_op jit(solution)/shard_map/cond/branch_1_fun/all_to_all | solution.py:208
  28.1 0.1 pad_add_fusion.refs_0_
  28.2 0.0 collective-permute-done.1.refs_3_
  28.2 0.0 collective-permute-done.refs_2_
  28.2 0.0 copy-done
  28.2 0.0 copy-done.3
  28.2 0.0 copy-start.1
  28.2 0.9 %copy-done.1 = f32[6,2,16,128]{3,2,1,0:T(8,128)S(1)} copy-done((f32[6,2,16,128]{3,2,1,0:T(8,128)S(1)}, f32[6,2,16,128]{3,2,1,0:T(8,128)}, u32[]{:S(2)}) %copy-start.1) | copy-done | bytes 98328
  29.1 1.1 %shard_map.87 = f32[8,64,128]{2,1,0:T(8,128)S(1)} custom-call(s32[2]{0:T(128)S(1)} %pad_add_fusion.refs_0_, f32[192,128]{1,0:T(8,128)S(1)} %bitcast.23, f32[192,128]{1,0:T(8,128)S(1)} %collective-permute-done.refs_2_, f32[192,128]{1,0:T(8,128)S(1)} %collective-permute-done.1.refs_3_, bf16[192,128]{1,0:T(8,128)(2,1)S(1)} %bitcast.25, ...), custom_call_target="tpu_custom_call" | custom-call | tf_op jit(solution)/shard_map/pallas_call | solution.py:220
  30.2 13.4 %all_to_all.10.refs_0_ = f32[8,64,128]{2,1,0:T(8,128)S(1)} all-to-all(f32[8,64,128]{2,1,0:T(8,128)S(1)} %shard_map.87), channel_id=1, replica_groups=mesh['tile'=64,'mem'=8] {'mem'}, dimensions={0} | all-to-all | bytes 524288 | tf_op jit(solution)/shard_map/all_to_all | solution.py:223
  43.6 0.0 copy-start.2
  43.6 0.7 %shard_map.88.refs_2_ = f32[192,128]{1,0:T(8,128)S(1)} custom-call(f32[8,64,128]{2,1,0:T(8,128)S(1)} %all_to_all.10.refs_0_, bf16[192,128]{1,0:T(8,128)(2,1)S(1)} %bitcast.26), custom_call_target="tpu_custom_call" | custom-call | tf_op jit(solution)/shard_map/pallas_call | solution.py:224
  44.4 4.0 %collective-permute-start.3 = (f32[192,128]{1,0:T(8,128)S(1)}, f32[192,128]{1,0:T(8,128)S(1)}, u32[]{:S(2)}, u32[]{:S(2)}) collective-permute-start(f32[192,128]{1,0:T(8,128)S(1)} %shard_map.88.refs_2_), channel_id=1, source_target_pairs={{0,504},{8,16},{16,8},{24,32},{32,24},{40,48},{48,40},{56,64},{64,... | collective-permute-start | bytes 294920 | tf_op jit(solution)/shard_map/ppermute | solution.py:199
  48.4 1.9 %collective-permute-start.2 = (f32[192,128]{1,0:T(8,128)S(1)}, f32[192,128]{1,0:T(8,128)S(1)}, u32[]{:S(2)}, u32[]{:S(2)}) collective-permute-start(f32[192,128]{1,0:T(8,128)S(1)} %shard_map.88.refs_2_), channel_id=1, source_target_pairs={{0,8},{8,0},{16,24},{24,16},{32,40},{40,32},{48,56},{56,48},{64,72... | collective-permute-start | bytes 294920 | tf_op jit(solution)/shard_map/ppermute | solution.py:200
  50.3 0.4 collective-permute-done.3.refs_4_
  50.7 0.9 %collective-permute-done.2.refs_3_ = f32[192,128]{1,0:T(8,128)S(1)} collective-permute-done((f32[192,128]{1,0:T(8,128)S(1)}, f32[192,128]{1,0:T(8,128)S(1)}, u32[]{:S(2)}, u32[]{:S(2)}) %collective-permute-start.2) | collective-permute-done | bytes 98336 | tf_op jit(solution)/shard_map/ppermute | solution.py:200
  51.6 0.0 copy-done.2
  51.6 1.6 %shard_map.89 = f32[192,128]{1,0:T(8,128)} custom-call(s32[2]{0:T(128)S(1)} %pad_add_fusion.refs_0_, f32[192,128]{1,0:T(8,128)S(1)} %bitcast.24, f32[192,128]{1,0:T(8,128)S(1)} %shard_map.88.refs_2_, f32[192,128]{1,0:T(8,128)S(1)} %collective-permute-done.2.refs_3_, f32[192,128]{1,0:T(8,128)S(1)} %collective-permute-done.3.refs_4_, bf16[800,128]{1,0:T(8,128)(2,1)S(1)} %copy-done), custom_call_target="tpu_custom_call" | custom-call | tf_op jit(solution)/shard_map/pallas_call | solution.py:226
Async XLA Ops:
  0.0 28.2 %copy-start = (bf16[800,128]{1,0:T(8,128)(2,1)S(1)}, bf16[800,128]{1,0:T(8,128)(2,1)}, u32[]{:S(2)}) copy-start(bf16[800,128]{1,0:T(8,128)(2,1)} %constant.28.clone.refs_6_.refs_5_) | copy-start | bytes 614404
  0.0 28.2 %collective-permute-start.1 = (f32[192,128]{1,0:T(8,128)}, f32[192,128]{1,0:T(8,128)S(1)}, u32[]{:S(2)}, u32[]{:S(2)}) collective-permute-start(f32[192,128]{1,0:T(8,128)} %bitcast.21), channel_id=1, source_target_pairs={{0,504},{8,16},{16,8},{24,32},{32,24},{40,48},{48,40},{56,64},{64,... | collective-permute-start | bytes 294920 | tf_op jit(solution)/shard_map/ppermute | solution.py:199
  4.7 23.5 %collective-permute-start = (f32[192,128]{1,0:T(8,128)}, f32[192,128]{1,0:T(8,128)S(1)}, u32[]{:S(2)}, u32[]{:S(2)}) collective-permute-start(f32[192,128]{1,0:T(8,128)} %bitcast.22), channel_id=1, source_target_pairs={{0,8},{8,0},{16,24},{24,16},{32,40},{40,32},{48,56},{56,48},{64,72... | collective-permute-start | bytes 294920 | tf_op jit(solution)/shard_map/ppermute | solution.py:200
  10.9 17.3 %copy-start.3 = (bf16[6,2,16,128]{3,2,1,0:T(8,128)(2,1)S(1)}, bf16[6,2,16,128]{3,2,1,0:T(8,128)(2,1)}, u32[]{:S(2)}) copy-start(bf16[6,2,16,128]{3,2,1,0:T(8,128)(2,1)} %param.10) | copy-start | bytes 147460
  28.2 0.9 %copy-start.1 = (f32[6,2,16,128]{3,2,1,0:T(8,128)S(1)}, f32[6,2,16,128]{3,2,1,0:T(8,128)}, u32[]{:S(2)}) copy-start(f32[6,2,16,128]{3,2,1,0:T(8,128)} %param.11) | copy-start | bytes 294916
  43.6 8.0 %copy-start.2 = (f32[6,2,16,128]{3,2,1,0:T(8,128)S(1)}, f32[6,2,16,128]{3,2,1,0:T(8,128)}, u32[]{:S(2)}) copy-start(f32[6,2,16,128]{3,2,1,0:T(8,128)} %param.11) | copy-start | bytes 294916
  44.4 6.3 %collective-permute-start.3 = (f32[192,128]{1,0:T(8,128)S(1)}, f32[192,128]{1,0:T(8,128)S(1)}, u32[]{:S(2)}, u32[]{:S(2)}) collective-permute-start(f32[192,128]{1,0:T(8,128)S(1)} %shard_map.88.refs_2_), channel_id=1, source_target_pairs={{0,504},{8,16},{16,8},{24,32},{32,24},{40,48},{48,40},{56,64},{64,... | collective-permute-start | bytes 294920 | tf_op jit(solution)/shard_map/ppermute | solution.py:199
  48.4 3.2 %collective-permute-start.2 = (f32[192,128]{1,0:T(8,128)S(1)}, f32[192,128]{1,0:T(8,128)S(1)}, u32[]{:S(2)}, u32[]{:S(2)}) collective-permute-start(f32[192,128]{1,0:T(8,128)S(1)} %shard_map.88.refs_2_), channel_id=1, source_target_pairs={{0,8},{8,0},{16,24},{24,16},{32,40},{40,32},{48,56},{56,48},{64,72... | collective-permute-start | bytes 294920 | tf_op jit(solution)/shard_map/ppermute | solution.py:200

commit v3 on v2

v3 whole, which is shorter than its diff:
```python
import math

import jax
import jax.numpy as jnp
import ml_dtypes
import numpy as np
from jax import lax
from jax.experimental import pallas as pl
from jax.experimental.pallas import tpu as pltpu
from jax.sharding import PartitionSpec as P

YSCALE = 1
F32 = jnp.float32
BF16 = jnp.bfloat16
ROUTING_PLANE = 1
MEMBER_LEAD = 6
TILE_LEAD = 40


def halves(table):
    high = table.astype(np.float32).astype(ml_dtypes.bfloat16)
    low = (table.astype(np.float32) - high.astype(np.float32)).astype(ml_dtypes.bfloat16)
    return high, low


def tables(col_count, row_count, scale, levels):
    offset = (np.arange(3 * col_count) - col_count)[:, None] - np.arange(col_count)[None, :]
    band = np.where(np.abs(offset) <= col_count, np.exp(-0.5 * (offset / col_count) ** 2), 0.0)
    row_offset = np.arange(row_count)[:, None] - np.arange(row_count)[None, :]
    rows = np.exp(-0.5 * (row_offset / scale) ** 2)
    along_x = np.arange(-col_count, col_count + 1)
    along_y = np.arange(-(row_count - 1), row_count)
    total = np.sum(np.exp(-((along_x / col_count) ** 2))) * np.sum(np.exp(-((along_y / scale) ** 2)))
    mixed = np.kron(np.eye(levels), rows) / np.sqrt(total)
    mixed = np.tile(mixed, (1, col_count // mixed.shape[1]))
    return np.concatenate([*halves(band), *halves(mixed)], axis=0)


def split(values):
    high = values.astype(BF16)
    return high, (values - high.astype(F32)).astype(BF16)


def localize(extended, table_ref, rows):
    flat, depth = extended.shape
    cols = table_ref.shape[1]
    row_block = lax.broadcasted_iota(jnp.int32, (flat, flat), 0) // rows
    same = row_block == lax.broadcasted_iota(jnp.int32, (flat, flat), 1) // rows

    def mixing(start):
        strip = table_ref[start : start + rows].astype(F32)
        strip = jnp.concatenate([strip] * pl.cdiv(flat, cols), axis=1)[:, :flat]
        return jnp.where(same, jnp.concatenate([strip] * (flat // rows), axis=0), 0.0).astype(BF16)

    mixed_high, mixed_low = mixing(2 * depth), mixing(2 * depth + rows)
    band_high, band_low = table_ref[:depth], table_ref[depth : 2 * depth]
    high, low = split(extended)
    swept = jnp.dot(
        jnp.concatenate([high, low, high], axis=1),
        jnp.concatenate([band_high, band_high, band_low], axis=0),
        preferred_element_type=F32,
    )
    high, low = split(swept)
    both = jnp.dot(mixed_high, jnp.concatenate([high, low], axis=1), preferred_element_type=F32)
    return both[:, :cols] + both[:, cols:] + jnp.dot(mixed_low, high, preferred_element_type=F32)


def extend(even, own, near, far):
    left = jnp.where(even, far, near)
    right = jnp.where(even, near, far)
    return jnp.concatenate([left, own, right], axis=1)


def pack_kernel(lead, cell_ref, count_ref, frac_ref, innov_ref, prec_ref, out_ref):
    slots, tiles = innov_ref.shape
    cols = out_ref.shape[1]
    slot = lax.broadcasted_iota(jnp.int32, (slots, tiles), 0)
    live = jnp.where(slot < count_ref[...], 1.0, 0.0)
    cell = cell_ref[...]
    corner_row = cell // cols
    corner_col = cell - corner_row * cols
    packed = jnp.concatenate(
        [
            corner_col.astype(F32) + frac_ref[0],
            corner_row.astype(F32) + frac_ref[1],
            innov_ref[...],
            prec_ref[...] * live,
            jnp.zeros((out_ref.shape[1] - 4 * slots, tiles), F32),
        ],
        axis=0,
    )
    turned = jnp.transpose(packed)
    out_ref[: tiles - lead] = turned[lead:]
    out_ref[tiles - lead :] = turned[:lead]


def partial_sum(spread, rows, even, own_ref, near_ref, far_ref, perturb_ref, table_ref):
    extended = extend(even, own_ref[...], near_ref[...], far_ref[...])
    product = perturb_ref[...].astype(F32) * localize(extended, table_ref, rows)
    total = product[:rows]
    for start in range(rows, product.shape[0], rows):
        total = total + product[start : start + rows]
    return spread * total


def partial_kernel(spread, even_ref, own_ref, near_ref, far_ref, perturb_ref, table_ref, out_ref):
    even = even_ref[0] == 1
    out_ref[...] = partial_sum(spread, out_ref.shape[0], even, own_ref, near_ref, far_ref, perturb_ref, table_ref)


def partial_copies_kernel(spread, rows, even_ref, own_ref, near_ref, far_ref, perturb_ref, table_ref, out_ref):
    even = even_ref[0] == 1
    total = partial_sum(spread, rows, even, own_ref, near_ref, far_ref, perturb_ref, table_ref)
    for copy in range(out_ref.shape[0]):
        out_ref[copy, :rows] = total
        out_ref[copy, rows:] = jnp.zeros((out_ref.shape[1] - rows, out_ref.shape[2]), F32)


def join_kernel(slots, partial_ref, obs_ref, out_ref):
    rows = partial_ref.shape[0]
    total = partial_ref[...]
    turned = jnp.transpose(obs_ref[...])
    half = slots // 2
    quantities = []
    for index in range(4):
        first = turned[index * slots : index * slots + half]
        second = turned[index * slots + half : (index + 1) * slots]
        quantities.append(jnp.concatenate([first, second], axis=1))
    for copy in range(out_ref.shape[0]):
        out_ref[copy, :rows] = total
        for index, quantity in enumerate(quantities):
            out_ref[copy, rows + index * half : rows + (index + 1) * half] = quantity


def obs_kernel(half, source, partial_ref, perturb_ref, out_ref):
    rows = partial_ref.shape[1] - 4 * half
    field = partial_ref[0, :rows]
    for member in range(1, partial_ref.shape[0]):
        field = field + partial_ref[member, :rows]
    cols = field.shape[1]
    at_x, at_y, innov, prec = (partial_ref[source, rows + i * half : rows + (i + 1) * half] for i in range(4))
    corner_col, corner_row = at_x.astype(jnp.int32), at_y.astype(jnp.int32)
    frac_x, frac_y = at_x - corner_col.astype(F32), at_y - corner_row.astype(F32)
    lanes = at_x.shape[1]
    row_at = lax.broadcasted_iota(jnp.int32, (rows, lanes), 0)
    col_at = lax.broadcasted_iota(jnp.int32, (cols, lanes), 0)
    row_parts, col_parts = [], []
    for k in range(half):
        r, x = corner_row[k : k + 1], corner_col[k : k + 1]
        fy, fx = frac_y[k : k + 1], frac_x[k : k + 1]
        row_parts.append(jnp.where(row_at == r, 1.0 - fy, jnp.where(row_at == r + 1, fy, 0.0)))
        col_parts.append(jnp.where(col_at == x, 1.0 - fx, jnp.where(col_at == x + 1, fx, 0.0)))
    row_all = jnp.concatenate(row_parts, axis=1)
    row_high, row_low = split(row_all)
    field_high, field_low = split(jnp.transpose(field))
    picked = jnp.dot(
        jnp.concatenate([field_high, field_low, field_high], axis=1),
        jnp.concatenate([row_high, row_high, row_low], axis=0),
        preferred_element_type=F32,
    )
    weighted = []
    for k in range(half):
        value = jnp.sum(picked[:, k * lanes : (k + 1) * lanes] * col_parts[k], axis=0, keepdims=True)
        weighted.append(prec[k : k + 1] * (value - innov[k : k + 1]))
    weighted = jnp.concatenate(weighted, axis=1)
    rows_high, rows_low = split(row_all * weighted)
    cols_high, cols_low = split(jnp.concatenate(col_parts, axis=1))
    adjoint = lax.dot_general(
        jnp.concatenate([rows_high, rows_low, rows_high], axis=1),
        jnp.concatenate([cols_high, cols_high, cols_low], axis=1),
        (((1,), (1,)), ((), ())),
        preferred_element_type=F32,
    )
    for start in range(0, out_ref.shape[0], rows):
        out_ref[start : start + rows] = perturb_ref[start : start + rows].astype(F32) * adjoint


def final_kernel(spread, rows, even_ref, control_ref, own_ref, near_ref, far_ref, table_ref, out_ref):
    even = even_ref[0] == 1
    extended = extend(even, own_ref[...], near_ref[...], far_ref[...])
    out_ref[...] = control_ref[...] + spread * localize(extended, table_ref, rows)


def call(kernel, out_shape, scalars, arrays):
    specs = [pl.BlockSpec(memory_space=pltpu.SMEM)] * scalars + [pl.BlockSpec(memory_space=pltpu.VMEM)] * arrays
    return pl.pallas_call(
        kernel,
        out_shape=jax.ShapeDtypeStruct(out_shape, F32),
        in_specs=specs,
        out_specs=pl.BlockSpec(memory_space=pltpu.VMEM),
        compiler_params=pltpu.CompilerParams(vmem_limit_bytes=24 * 1024 * 1024),
    )


def per_device(perturb, control, obs_cell, obs_count, obs_frac, obs_innov, obs_prec):
    mem_local, levels, row_count, col_count = perturb.shape
    members = lax.axis_size("mem")
    tiles = lax.axis_size("tile")
    spread = 1.0 / math.sqrt(mem_local * members - 1)
    slots = obs_cell.shape[2]
    rows = levels * row_count
    table = jnp.asarray(tables(col_count, row_count, YSCALE, levels))
    even = (1 - lax.axis_index("tile") % 2).astype(jnp.int32).reshape(1)
    tile_lead = TILE_LEAD
    tile_order = [[(i + tile_lead) % tiles for i in range(tiles)]]
    member_order = [[(i + MEMBER_LEAD) % members for i in range(members)]]
    near_pairs = [(i, i ^ 1) for i in range(tiles)]
    far_pairs = [(i, (i + 1) % tiles if i % 2 else (i - 1) % tiles) for i in range(tiles)]

    def neighbours(own):
        far = lax.ppermute(own, "tile", far_pairs)
        near = lax.ppermute(own, "tile", near_pairs)
        return near, far

    flat = mem_local * rows
    joined = (members, rows + 2 * slots, col_count)

    def route(even, own, weights, table, cell, count, frac, innov, prec):
        packed = call(lambda *refs: pack_kernel(tile_lead, *refs), (tiles, col_count), 0, 5)(
            cell[0].T, count, frac[0].transpose(0, 2, 1), innov[0].T, prec[0].T
        )
        packed = packed.reshape(tiles, 1, col_count)
        arrived = lax.all_to_all(
            packed, "tile", split_axis=0, concat_axis=0, tiled=True, axis_index_groups=tile_order
        )
        near, far = neighbours(own)
        partial = call(lambda *refs: partial_kernel(spread, *refs), (rows, col_count), 1, 5)(
            even, own, near, far, weights, table
        )
        return call(lambda *refs: join_kernel(slots, *refs), joined, 0, 2)(partial, arrived.reshape(tiles, col_count))

    def plain(even, own, weights, table, cell, count, frac, innov, prec):
        near, far = neighbours(own)
        return call(lambda *refs: partial_copies_kernel(spread, rows, *refs), joined, 1, 5)(
            even, own, near, far, weights, table
        )

    own = control.reshape(flat, col_count)
    weights = perturb.reshape(flat, col_count)
    partials = lax.cond(
        lax.axis_index("mem") == ROUTING_PLANE,
        route,
        plain,
        *(even, own, weights, table, obs_cell, obs_count, obs_frac, obs_innov, obs_prec),
    )
    partials = lax.all_to_all(
        partials, "mem", split_axis=0, concat_axis=0, tiled=True, axis_index_groups=member_order
    )
    source = (ROUTING_PLANE - MEMBER_LEAD) % members
    product = call(lambda *refs: obs_kernel(slots // 2, source, *refs), (flat, col_count), 0, 2)(partials, weights)
    near, far = neighbours(product)
    gradient = call(lambda *refs: final_kernel(spread, rows, *refs), (flat, col_count), 1, 5)(
        even, own, product, near, far, table
    )
    return gradient.reshape(control.shape)


def solution(mesh):
    return jax.shard_map(
        per_device,
        mesh=mesh,
        in_specs=(
            P("mem", None, None, "tile"),
            P("mem", None, None, "tile"),
            P("tile", None, None),
            P("tile", None),
            P("tile", None, None, None),
            P("tile", None, None),
            P("tile", None, None),
        ),
        out_specs=P("mem", None, None, "tile"),
        check_vma=False,
    )
```

time: 54.1 us -> 48.8 us (0.902)
  blocking collectives: 29.8 us -> 22.7 us
  starting transfers between devices: 16.8 us -> 19.3 us
  Pallas kernels: 4.3 us -> 3.35 us
  waiting for transfers between devices: 1.27 us -> 2.04 us
    all_to_all x2 -> x1, blocking collectives: 29.8 us -> 22.7 us  [per_device(): lax.all_to_all(partials, 'mem', split_axis=0, concat_axis=0, tiled=True,...]
    ppermute x2, starting transfers between devices: 8.04 us -> 9.45 us  [neighbours(): near = lax.ppermute(own, 'tile', near_pairs)]
    ppermute x2, starting transfers between devices: 8.72 us -> 9.87 us  [neighbours(): far = lax.ppermute(own, 'tile', far_pairs)]
    ppermute x2, waiting for transfers between devices: 0.91 us -> 2.03 us  [neighbours(): near = lax.ppermute(own, 'tile', near_pairs)]
    pallas_call x4 -> x3, Pallas kernels: 4.3 us -> 3.35 us  [the longest x1 1.48 us: plain(): call(lambda *refs: partial_copies_kernel(spread, rows, *refs), joined, 1, 5)]
  transfers between devices with their start and end apart: 4 -> 4, of which waited for: 2 -> 2; matrix products, arithmetic and copies ran while one was open for 0% -> 0% of each run, Pallas kernels for 2% -> 0%
where the time goes in v3:
time: 48.8 us; the launch traced here: 48.2 us
  blocking collectives  22.7 us (47%)
  starting transfers between devices  19.3 us (40%)
  Pallas kernels  3.35 us (7%)
  waiting for transfers between devices  2.04 us (4%)
  local copies, waits for them, and re-layouts  0.74 us (2%)
    all_to_all x1, blocking collectives, per_device(): lax.all_to_all(partials, 'mem', split_axis=0, concat_axis=0, tiled=True,...  22.7 us
    ppermute x2, starting transfers between devices, neighbours(): far = lax.ppermute(own, 'tile', far_pairs)  9.87 us
    ppermute x2, starting transfers between devices, neighbours(): near = lax.ppermute(own, 'tile', near_pairs)  9.45 us
    ppermute x2, waiting for transfers between devices, neighbours(): near = lax.ppermute(own, 'tile', near_pairs)  2.03 us
    pallas_call x1, Pallas kernels, plain(): call(lambda *refs: partial_copies_kernel(spread, rows, *refs), joined, 1, 5)  1.48 us
    pallas_call x1, Pallas kernels, per_device(): call(lambda *refs: final_kernel(spread, rows, *refs), (flat, col_count),...  1.12 us
  transfers between devices with their start and end apart: 4, of which 2 were waited for; matrix products, arithmetic and copies ran while one was open for 0% of the time, Pallas kernels for 0%

profile of v3, /device:TPU:1, one launch (start us, length us, event | category | flops | bytes accessed | tf_op | source)
XLA Modules:
  0.0 48.2 jit_solution(8873298850821101404)
XLA Ops:
  0.0 0.0 copy-start.9
  0.0 0.0 copy-start.8
  0.0 0.0 copy-start.5
  0.0 0.0 copy-start.7
  0.0 0.0 copy-start.6
  0.0 0.6 %copy-done.9 = s32[1,64]{1,0:T(1,128)S(1)} copy-done((s32[1,64]{1,0:T(1,128)S(1)}, s32[1,64]{1,0:T(1,128)}, u32[]{:S(2)}) %copy-start.9) | copy-done | bytes 280
  0.7 0.1 copy-done.8
  0.7 0.0 copy-done.5
  0.8 0.0 copy-done.7
  0.8 0.0 copy-done.6
  0.8 13.3 %conditional.1 = (f32[8,64,128]{2,1,0:T(8,128)S(1)}) conditional(s32[]{:T(128)} %convert_element_type.3, (f32[192,128]{1,0:T(8,128)}, s32[1]{0:T(128)}, bf16[192,128]{1,0:T(8,128)(2,1)}, bf16[832,128]{1,0:T(8,128)(2,1)}) %tuple.17, (f32[192,128]{1,0:T(8,128)}, s32[1]{0:T(128)}, bf16[192,128]{1,0:T(8,128)(2,1)}, bf16[832,128]{1,0:T(8,128)(2,1)}, ...), branch_computations={%region_0.1_spmd, %region_1.2_spmd} | conditional | bytes 1474736 | solution.py:240
  0.8 4.6 %collective-permute-start.1 = (f32[192,128]{1,0:T(8,128)}, f32[192,128]{1,0:T(8,128)S(1)}, u32[]{:S(2)}, u32[]{:S(2)}) collective-permute-start(f32[192,128]{1,0:T(8,128)} %get-tuple-element.35.refs_1_), channel_id=1, source_target_pairs={{0,504},{8,16},{16,8},{24,32},{32,24},{40,48},{48,40},{56,64},{64,... | collective-permute-start | bytes 294920 | tf_op jit(solution)/shard_map/cond/branch_0_fun/ppermute | solution.py:211
  5.4 6.1 %collective-permute-start = (f32[192,128]{1,0:T(8,128)}, f32[192,128]{1,0:T(8,128)S(1)}, u32[]{:S(2)}, u32[]{:S(2)}) collective-permute-start(f32[192,128]{1,0:T(8,128)} %get-tuple-element.35.refs_1_), channel_id=1, source_target_pairs={{0,8},{8,0},{16,24},{24,16},{32,40},{40,32},{48,56},{56,48},{64,72... | collective-permute-start | bytes 294920 | tf_op jit(solution)/shard_map/cond/branch_0_fun/ppermute | solution.py:212
  11.5 0.0 collective-permute-done.1.refs_3_
  11.5 1.1 %collective-permute-done.refs_2_ = f32[192,128]{1,0:T(8,128)S(1)} collective-permute-done((f32[192,128]{1,0:T(8,128)}, f32[192,128]{1,0:T(8,128)S(1)}, u32[]{:S(2)}, u32[]{:S(2)}) %collective-permute-start) | collective-permute-done | bytes 98336 | tf_op jit(solution)/shard_map/cond/branch_0_fun/ppermute | solution.py:212
  12.6 1.5 %branch_0_fun.1 = f32[8,64,128]{2,1,0:T(8,128)S(1)} custom-call(s32[1]{0:T(128)} %get-tuple-element.34.refs_0_, f32[192,128]{1,0:T(8,128)} %get-tuple-element.35.refs_1_, f32[192,128]{1,0:T(8,128)S(1)} %collective-permute-done.refs_2_, f32[192,128]{1,0:T(8,128)S(1)} %collective-permute-done.1.refs_3_, bf16[192,128]{1,0:T(8,128)(2,1)} %get-tuple-element.36.refs_4_, ...), custom_call_target="tpu_custom_call" | custom-call | tf_op jit(solution)/shard_map/cond/branch_0_fun/pallas_call | solution.py:234
  14.1 0.0 copy-start.3
  14.1 22.7 %all_to_all.9.refs_0_ = f32[8,64,128]{2,1,0:T(8,128)S(1)} all-to-all(f32[8,64,128]{2,1,0:T(8,128)S(1)} %get-tuple-element.57), channel_id=1, replica_groups={{6,7,0,1,2,3,4,5},{14,15,8,9,10,11,12,13},{22,23,16,17,18,19,20,21},{30..., dimensions={0} | all-to-all | bytes 524288 | tf_op jit(solution)/shard_map/all_to_all | solution.py:246
  36.8 0.0 copy-done.3
  36.8 0.0 copy-start
  36.8 0.0 copy-start.1
  36.8 0.7 %shard_map.87.refs_2_ = f32[192,128]{1,0:T(8,128)S(1)} custom-call(f32[8,64,128]{2,1,0:T(8,128)S(1)} %all_to_all.9.refs_0_, bf16[192,128]{1,0:T(8,128)(2,1)S(1)} %bitcast.26), custom_call_target="tpu_custom_call" | custom-call | tf_op jit(solution)/shard_map/pallas_call | solution.py:250
  37.5 5.3 %collective-permute-start.5 = (f32[192,128]{1,0:T(8,128)S(1)}, f32[192,128]{1,0:T(8,128)S(1)}, u32[]{:S(2)}, u32[]{:S(2)}) collective-permute-start(f32[192,128]{1,0:T(8,128)S(1)} %shard_map.87.refs_2_), channel_id=1, source_target_pairs={{0,504},{8,16},{16,8},{24,32},{32,24},{40,48},{48,40},{56,64},{64,... | collective-permute-start | bytes 294920 | tf_op jit(solution)/shard_map/ppermute | solution.py:211
  42.8 3.3 %collective-permute-start.4 = (f32[192,128]{1,0:T(8,128)S(1)}, f32[192,128]{1,0:T(8,128)S(1)}, u32[]{:S(2)}, u32[]{:S(2)}) collective-permute-start(f32[192,128]{1,0:T(8,128)S(1)} %shard_map.87.refs_2_), channel_id=1, source_target_pairs={{0,8},{8,0},{16,24},{24,16},{32,40},{40,32},{48,56},{56,48},{64,72... | collective-permute-start | bytes 294920 | tf_op jit(solution)/shard_map/ppermute | solution.py:212
  46.2 0.0 collective-permute-done.5.refs_4_
  46.2 0.9 %collective-permute-done.4.refs_3_ = f32[192,128]{1,0:T(8,128)S(1)} collective-permute-done((f32[192,128]{1,0:T(8,128)S(1)}, f32[192,128]{1,0:T(8,128)S(1)}, u32[]{:S(2)}, u32[]{:S(2)}) %collective-permute-start.4) | collective-permute-done | bytes 98336 | tf_op jit(solution)/shard_map/ppermute | solution.py:212
  47.1 0.0 copy-done
  47.1 0.0 copy-done.1
  47.1 1.1 %shard_map.88 = f32[192,128]{1,0:T(8,128)} custom-call(s32[1]{0:T(128)} %bitcast.16.refs_0_, f32[192,128]{1,0:T(8,128)S(1)} %bitcast.23, f32[192,128]{1,0:T(8,128)S(1)} %shard_map.87.refs_2_, f32[192,128]{1,0:T(8,128)S(1)} %collective-permute-done.4.refs_3_, f32[192,128]{1,0:T(8,128)S(1)} %collective-permute-done.5.refs_4_, bf16[832,128]{1,0:T(8,128)(2,1)S(1)} %copy-done), custom_call_target="tpu_custom_call" | custom-call | tf_op jit(solution)/shard_map/pallas_call | solution.py:252
Async XLA Ops:
  0.0 0.7 %copy-start.9 = (s32[1,64]{1,0:T(1,128)S(1)}, s32[1,64]{1,0:T(1,128)}, u32[]{:S(2)}) copy-start(s32[1,64]{1,0:T(1,128)} %param.13) | copy-start | bytes 772
  0.0 0.7 %copy-start.8 = (f32[1,64,16]{1,2,0:T(8,128)S(1)}, f32[1,64,16]{1,2,0:T(8,128)}, u32[]{:S(2)}) copy-start(f32[1,64,16]{1,2,0:T(8,128)} %param.16) | copy-start | bytes 12292
  0.0 0.7 %copy-start.5 = (f32[1,2,64,16]{2,3,1,0:T(8,128)S(1)}, f32[1,2,64,16]{2,3,1,0:T(8,128)}, u32[]{:S(2)}) copy-start(f32[1,2,64,16]{2,3,1,0:T(8,128)} %param.14) | copy-start | bytes 24580
  0.0 0.7 %copy-start.7 = (f32[1,64,16]{1,2,0:T(8,128)S(1)}, f32[1,64,16]{1,2,0:T(8,128)}, u32[]{:S(2)}) copy-start(f32[1,64,16]{1,2,0:T(8,128)} %param.15) | copy-start | bytes 12292
  0.0 0.7 %copy-start.6 = (s32[1,64,16]{1,2,0:T(8,128)S(1)}, s32[1,64,16]{1,2,0:T(8,128)}, u32[]{:S(2)}) copy-start(s32[1,64,16]{1,2,0:T(8,128)} %param.12) | copy-start | bytes 12292
  0.8 10.7 %collective-permute-start.1 = (f32[192,128]{1,0:T(8,128)}, f32[192,128]{1,0:T(8,128)S(1)}, u32[]{:S(2)}, u32[]{:S(2)}) collective-permute-start(f32[192,128]{1,0:T(8,128)} %get-tuple-element.35.refs_1_), channel_id=1, source_target_pairs={{0,504},{8,16},{16,8},{24,32},{32,24},{40,48},{48,40},{56,64},{64,... | collective-permute-start | bytes 294920 | tf_op jit(solution)/shard_map/cond/branch_0_fun/ppermute | solution.py:211
  5.4 7.3 %collective-permute-start = (f32[192,128]{1,0:T(8,128)}, f32[192,128]{1,0:T(8,128)S(1)}, u32[]{:S(2)}, u32[]{:S(2)}) collective-permute-start(f32[192,128]{1,0:T(8,128)} %get-tuple-element.35.refs_1_), channel_id=1, source_target_pairs={{0,8},{8,0},{16,24},{24,16},{32,40},{40,32},{48,56},{56,48},{64,72... | collective-permute-start | bytes 294920 | tf_op jit(solution)/shard_map/cond/branch_0_fun/ppermute | solution.py:212
  14.1 22.7 %copy-start.3 = (bf16[6,2,16,128]{3,2,1,0:T(8,128)(2,1)S(1)}, bf16[6,2,16,128]{3,2,1,0:T(8,128)(2,1)}, u32[]{:S(2)}) copy-start(bf16[6,2,16,128]{3,2,1,0:T(8,128)(2,1)} %param.10) | copy-start | bytes 147460
  36.8 10.3 %copy-start = (bf16[832,128]{1,0:T(8,128)(2,1)S(1)}, bf16[832,128]{1,0:T(8,128)(2,1)}, u32[]{:S(2)}) copy-start(bf16[832,128]{1,0:T(8,128)(2,1)} %constant.25.clone.refs_5_) | copy-start | bytes 638980
  36.8 10.3 %copy-start.1 = (f32[6,2,16,128]{3,2,1,0:T(8,128)S(1)}, f32[6,2,16,128]{3,2,1,0:T(8,128)}, u32[]{:S(2)}) copy-start(f32[6,2,16,128]{3,2,1,0:T(8,128)} %param.11) | copy-start | bytes 294916
  37.5 8.6 %collective-permute-start.5 = (f32[192,128]{1,0:T(8,128)S(1)}, f32[192,128]{1,0:T(8,128)S(1)}, u32[]{:S(2)}, u32[]{:S(2)}) collective-permute-start(f32[192,128]{1,0:T(8,128)S(1)} %shard_map.87.refs_2_), channel_id=1, source_target_pairs={{0,504},{8,16},{16,8},{24,32},{32,24},{40,48},{48,40},{56,64},{64,... | collective-permute-start | bytes 294920 | tf_op jit(solution)/shard_map/ppermute | solution.py:211
  42.8 4.3 %collective-permute-start.4 = (f32[192,128]{1,0:T(8,128)S(1)}, f32[192,128]{1,0:T(8,128)S(1)}, u32[]{:S(2)}, u32[]{:S(2)}) collective-permute-start(f32[192,128]{1,0:T(8,128)S(1)} %shard_map.87.refs_2_), channel_id=1, source_target_pairs={{0,8},{8,0},{16,24},{24,16},{32,40},{40,32},{48,56},{56,48},{64,72... | collective-permute-start | bytes 294920 | tf_op jit(solution)/shard_map/ppermute | solution.py:212

commit v4 on v3

--- a/solution.py
+++ b/solution.py
@@ -12,9 +12,9 @@
 YSCALE = 1
 F32 = jnp.float32
 BF16 = jnp.bfloat16
-ROUTING_PLANE = 1
-MEMBER_LEAD = 6
-TILE_LEAD = 40
+ROUTING_PLANES = (0, 1)
+TILE_BLOCKS = (5, 6, 7, 0, 1, 2, 3, 4)
+MEMBER_ORDER = (7, 6, 5, 4, 3, 2, 1, 0)
 
 
 def halves(table):
@@ -71,27 +71,31 @@
     return jnp.concatenate([left, own, right], axis=1)
 
 
-def pack_kernel(lead, cell_ref, count_ref, frac_ref, innov_ref, prec_ref, out_ref):
-    slots, tiles = innov_ref.shape
+def pack_kernel(blocks, part_ref, cell_ref, count_ref, frac_ref, innov_ref, prec_ref, out_ref):
+    tiles = innov_ref.shape[1]
+    slots = innov_ref.shape[0] // len(ROUTING_PLANES)
     cols = out_ref.shape[1]
-    slot = lax.broadcasted_iota(jnp.int32, (slots, tiles), 0)
+    start = pl.multiple_of(part_ref[0] * slots, slots)
+    mine = pl.ds(start, slots)
+    slot = start + lax.broadcasted_iota(jnp.int32, (slots, tiles), 0)
     live = jnp.where(slot < count_ref[...], 1.0, 0.0)
-    cell = cell_ref[...]
-    corner_row = cell // cols
-    corner_col = cell - corner_row * cols
+    cell = cell_ref[mine]
+    corner_row = lax.shift_right_logical(cell, int(math.log2(cols)))
+    corner_col = lax.bitwise_and(cell, cols - 1)
     packed = jnp.concatenate(
         [
-            corner_col.astype(F32) + frac_ref[0],
-            corner_row.astype(F32) + frac_ref[1],
-            innov_ref[...],
-            prec_ref[...] * live,
+            corner_col.astype(F32) + frac_ref[0, mine],
+            corner_row.astype(F32) + frac_ref[1, mine],
+            innov_ref[mine],
+            prec_ref[mine] * live,
             jnp.zeros((out_ref.shape[1] - 4 * slots, tiles), F32),
         ],
         axis=0,
     )
     turned = jnp.transpose(packed)
-    out_ref[: tiles - lead] = turned[lead:]
-    out_ref[tiles - lead :] = turned[:lead]
+    size = tiles // len(blocks)
+    for place, block in enumerate(blocks):
+        out_ref[place * size : (place + 1) * size] = turned[block * size : (block + 1) * size]
 
 
 def partial_sum(spread, rows, even, own_ref, near_ref, far_ref, perturb_ref, table_ref):
@@ -103,42 +107,49 @@
     return spread * total
 
 
-def partial_kernel(spread, even_ref, own_ref, near_ref, far_ref, perturb_ref, table_ref, out_ref):
+def partial_kernel(spread, even_ref, own_ref, near_ref, far_ref, perturb_ref, table_ref, out_ref, kept_ref):
     even = even_ref[0] == 1
+    kept_ref[...] = perturb_ref[...]
     out_ref[...] = partial_sum(spread, out_ref.shape[0], even, own_ref, near_ref, far_ref, perturb_ref, table_ref)
 
 
-def partial_copies_kernel(spread, rows, even_ref, own_ref, near_ref, far_ref, perturb_ref, table_ref, out_ref):
+def partial_copies_kernel(
+    spread, rows, even_ref, own_ref, near_ref, far_ref, perturb_ref, table_ref, out_ref, kept_ref
+):
     even = even_ref[0] == 1
+    kept_ref[...] = perturb_ref[...]
     total = partial_sum(spread, rows, even, own_ref, near_ref, far_ref, perturb_ref, table_ref)
     for copy in range(out_ref.shape[0]):
         out_ref[copy, :rows] = total
         out_ref[copy, rows:] = jnp.zeros((out_ref.shape[1] - rows, out_ref.shape[2]), F32)
 
 
-def join_kernel(slots, partial_ref, obs_ref, out_ref):
+def join_kernel(partial_ref, obs_ref, out_ref):
     rows = partial_ref.shape[0]
+    slots = (out_ref.shape[1] - rows) // 2
     total = partial_ref[...]
     turned = jnp.transpose(obs_ref[...])
-    half = slots // 2
-    quantities = []
-    for index in range(4):
-        first = turned[index * slots : index * slots + half]
-        second = turned[index * slots + half : (index + 1) * slots]
-        quantities.append(jnp.concatenate([first, second], axis=1))
+    places = jnp.concatenate([turned[:slots], turned[slots : 2 * slots]], axis=1)
+    values = jnp.concatenate([turned[2 * slots : 3 * slots], turned[3 * slots : 4 * slots]], axis=1)
     for copy in range(out_ref.shape[0]):
         out_ref[copy, :rows] = total
-        for index, quantity in enumerate(quantities):
-            out_ref[copy, rows + index * half : rows + (index + 1) * half] = quantity
-
-
-def obs_kernel(half, source, partial_ref, perturb_ref, out_ref):
-    rows = partial_ref.shape[1] - 4 * half
+        out_ref[copy, rows : rows + slots] = places
+        out_ref[copy, rows + slots :] = values
+
+
+def obs_kernel(half, sources, partial_ref, perturb_ref, out_ref):
+    rows = partial_ref.shape[1] - 2 * half
     field = partial_ref[0, :rows]
     for member in range(1, partial_ref.shape[0]):
         field = field + partial_ref[member, :rows]
     cols = field.shape[1]
-    at_x, at_y, innov, prec = (partial_ref[source, rows + i * half : rows + (i + 1) * half] for i in range(4))
+    tiles = cols // 2
+
+    def quantity(start, lane):
+        parts = [partial_ref[source, rows + start : rows + start + half] for source in sources]
+        return jnp.concatenate([part[:, lane : lane + tiles] for part in parts], axis=1)
+
+    at_x, at_y, innov, prec = quantity(0, 0), quantity(0, tiles), quantity(half, 0), quantity(half, tiles)
     corner_col, corner_row = at_x.astype(jnp.int32), at_y.astype(jnp.int32)
     frac_x, frac_y = at_x - corner_col.astype(F32), at_y - corner_row.astype(F32)
     lanes = at_x.shape[1]
@@ -181,15 +192,21 @@
     out_ref[...] = control_ref[...] + spread * localize(extended, table_ref, rows)
 
 
-def call(kernel, out_shape, scalars, arrays):
+def call(kernel, out_shapes, scalars, arrays, flops=None):
     specs = [pl.BlockSpec(memory_space=pltpu.SMEM)] * scalars + [pl.BlockSpec(memory_space=pltpu.VMEM)] * arrays
+    outs = [jax.ShapeDtypeStruct(shape, dtype) for shape, dtype in out_shapes]
     return pl.pallas_call(
         kernel,
-        out_shape=jax.ShapeDtypeStruct(out_shape, F32),
+        out_shape=outs,
         in_specs=specs,
-        out_specs=pl.BlockSpec(memory_space=pltpu.VMEM),
+        out_specs=[pl.BlockSpec(memory_space=pltpu.VMEM)] * len(outs),
         compiler_params=pltpu.CompilerParams(vmem_limit_bytes=24 * 1024 * 1024),
-    )
+        cost_estimate=flops and pl.CostEstimate(flops=flops, bytes_accessed=0, transcendentals=0),
+    )
+
+
+def in_hbm(array):
+    return pltpu.with_memory_space_constraint(array, pltpu.HBM)
 
 
 def per_device(perturb, control, obs_cell, obs_count, obs_frac, obs_innov, obs_prec):
@@ -201,9 +218,9 @@
     rows = levels * row_count
     table = jnp.asarray(tables(col_count, row_count, YSCALE, levels))
     even = (1 - lax.axis_index("tile") % 2).astype(jnp.int32).reshape(1)
-    tile_lead = TILE_LEAD
-    tile_order = [[(i + tile_lead) % tiles for i in range(tiles)]]
-    member_order = [[(i + MEMBER_LEAD) % members for i in range(members)]]
+    size = tiles // len(TILE_BLOCKS)
+    tile_order = [[block * size + i for block in TILE_BLOCKS for i in range(size)]]
+    member_order = [list(MEMBER_ORDER)]
     near_pairs = [(i, i ^ 1) for i in range(tiles)]
     far_pairs = [(i, (i + 1) % tiles if i % 2 else (i - 1) % tiles) for i in range(tiles)]
 
@@ -213,45 +230,47 @@
         return near, far
 
     flat = mem_local * rows
-    joined = (members, rows + 2 * slots, col_count)
-
-    def route(even, own, weights, table, cell, count, frac, innov, prec):
-        packed = call(lambda *refs: pack_kernel(tile_lead, *refs), (tiles, col_count), 0, 5)(
-            cell[0].T, count, frac[0].transpose(0, 2, 1), innov[0].T, prec[0].T
-        )
+    half = slots // len(ROUTING_PLANES)
+    joined = (members, rows + 2 * half, col_count)
+
+    kept = ((flat, col_count), BF16)
+
+    def route(part, even, own, weights, table, cell, count, frac, innov, prec):
+        obs = (cell[0].T, count, frac[0].transpose(0, 2, 1), innov[0].T, prec[0].T)
+        pack = call(lambda *refs: pack_kernel(TILE_BLOCKS, *refs), [((tiles, col_count), F32)], 1, 5, 10**9)
+        (packed,) = pack(part, *map(in_hbm, obs))
         packed = packed.reshape(tiles, 1, col_count)
         arrived = lax.all_to_all(
             packed, "tile", split_axis=0, concat_axis=0, tiled=True, axis_index_groups=tile_order
         )
         near, far = neighbours(own)
-        partial = call(lambda *refs: partial_kernel(spread, *refs), (rows, col_count), 1, 5)(
-            even, own, near, far, weights, table
-        )
-        return call(lambda *refs: join_kernel(slots, *refs), joined, 0, 2)(partial, arrived.reshape(tiles, col_count))
-
-    def plain(even, own, weights, table, cell, count, frac, innov, prec):
+        summing = call(lambda *refs: partial_kernel(spread, *refs), [((rows, col_count), F32), kept], 1, 5, 1000)
+        partial, weights = summing(even, own, near, far, in_hbm(weights), table)
+        (partials,) = call(join_kernel, [(joined, F32)], 0, 2)(partial, arrived.reshape(tiles, col_count))
+        return partials, weights
+
+    def plain(part, even, own, weights, table, cell, count, frac, innov, prec):
         near, far = neighbours(own)
-        return call(lambda *refs: partial_copies_kernel(spread, rows, *refs), joined, 1, 5)(
-            even, own, near, far, weights, table
-        )
+        summing = call(lambda *refs: partial_copies_kernel(spread, rows, *refs), [(joined, F32), kept], 1, 5)
+        return tuple(summing(even, own, near, far, in_hbm(weights), table))
 
     own = control.reshape(flat, col_count)
     weights = perturb.reshape(flat, col_count)
-    partials = lax.cond(
-        lax.axis_index("mem") == ROUTING_PLANE,
+    part = (lax.axis_index("mem") - ROUTING_PLANES[0]).astype(jnp.int32).reshape(1)
+    partials, weights = lax.cond(
+        (part[0] >= 0) & (part[0] < len(ROUTING_PLANES)),
         route,
         plain,
-        *(even, own, weights, table, obs_cell, obs_count, obs_frac, obs_innov, obs_prec),
+        *(part, even, own, weights, table, obs_cell, obs_count, obs_frac, obs_innov, obs_prec),
     )
     partials = lax.all_to_all(
         partials, "mem", split_axis=0, concat_axis=0, tiled=True, axis_index_groups=member_order
     )
-    source = (ROUTING_PLANE - MEMBER_LEAD) % members
-    product = call(lambda *refs: obs_kernel(slots // 2, source, *refs), (flat, col_count), 0, 2)(partials, weights)
+    sources = [MEMBER_ORDER.index(plane) for plane in ROUTING_PLANES]
+    (product,) = call(lambda *refs: obs_kernel(half, sources, *refs), [((flat, col_count), F32)], 0, 2)(partials, weights)
     near, far = neighbours(product)
-    gradient = call(lambda *refs: final_kernel(spread, rows, *refs), (flat, col_count), 1, 5)(
-        even, own, product, near, far, table
-    )
+    finish = call(lambda *refs: final_kernel(spread, rows, *refs), [((flat, col_count), F32)], 1, 5)
+    (gradient,) = finish(even, own, product, near, far, table)
     return gradient.reshape(control.shape)
 
 

time: 48.8 us -> 46.7 us (0.957)
  blocking collectives: 22.7 us -> 9.45 us
  starting transfers between devices: 19.3 us -> 30.4 us
  Pallas kernels: 3.35 us -> 4.74 us
  local copies, waits for them, and re-layouts: 0.74 us -> 0.02 us
    all_to_all x1, blocking collectives: 22.7 us -> 9.45 us  [per_device(): lax.all_to_all(partials, 'mem', split_axis=0, concat_axis=0, tiled=True,...]
    all_to_all x0 -> x1, starting transfers between devices: none -> 11.1 us  [route(): lax.all_to_all(packed, 'tile', split_axis=0, concat_axis=0, tiled=True, a...]
    pallas_call x3 -> x5, Pallas kernels: 3.35 us -> 4.74 us  [the longest x1 1.52 us: route(): packed, = pack(part, *map(in_hbm, obs))]
    ppermute x2, waiting for transfers between devices: 2.03 us -> 0.91 us  [neighbours(): near = lax.ppermute(own, 'tile', near_pairs)]
    all_to_all x0 -> x1, waiting for transfers between devices: none -> 0.75 us  [route(): lax.all_to_all(packed, 'tile', split_axis=0, concat_axis=0, tiled=True, a...]
    unnamed x16 -> x4, local copies, waits for them, and re-layouts: 0.74 us -> 0.01 us
  transfers between devices with their start and end apart: 4 -> 5, of which waited for: 2 -> 2; matrix products, arithmetic and copies ran while one was open for 0% -> 0% of each run, Pallas kernels for 0% -> 6%
where the time goes in v4:
time: 46.7 us; the launch traced here: 46.4 us
  starting transfers between devices  30.4 us (65%)
  blocking collectives  9.45 us (20%)
  Pallas kernels  4.74 us (10%)
  waiting for transfers between devices  1.67 us (4%)
    all_to_all x1, starting transfers between devices, route(): lax.all_to_all(packed, 'tile', split_axis=0, concat_axis=0, tiled=True, a...  11.1 us
    ppermute x2, starting transfers between devices, neighbours(): near = lax.ppermute(own, 'tile', near_pairs)  9.66 us
    ppermute x2, starting transfers between devices, neighbours(): far = lax.ppermute(own, 'tile', far_pairs)  9.6 us
    all_to_all x1, blocking collectives, per_device(): lax.all_to_all(partials, 'mem', split_axis=0, concat_axis=0, tiled=True,...  9.45 us
    pallas_call x1, Pallas kernels, route(): packed, = pack(part, *map(in_hbm, obs))  1.52 us
    pallas_call x1, Pallas kernels, route(): partial, weights = summing(even, own, near, far, in_hbm(weights), table)  1.27 us
    pallas_call x1, Pallas kernels, per_device(): gradient, = finish(even, own, product, near, far, table)  1.12 us
  transfers between devices with their start and end apart: 5, of which 2 were waited for; matrix products, arithmetic and copies ran while one was open for 0% of the time, Pallas kernels for 6%

profile of v4, /device:TPU:1, one launch (start us, length us, event | category | flops | bytes accessed | tf_op | source)
XLA Modules:
  0.0 46.4 jit_solution(3715148676480211419)
XLA Ops:
  0.0 25.6 %conditional.1 = ((f32[8,48,128]{2,1,0:T(8,128)S(1)}, bf16[192,128]{1,0:T(8,128)(2,1)S(1)})) conditional(s32[]{:T(128)} %convert_element_type.3, (f32[192,128]{1,0:T(8,128)}, s32[1]{0:T(128)}, bf16[192,128]{1,0:T(8,128)(2,1)}, bf16[832,128]{1,0:T(8,128)(2,1)}) %tuple.20, (f32[192,128]{1,0:T(8,128)}, s32[1]{0:T(128)}, bf16[192,128]{1,0:T(8,128)(2,1)}, ...), branch_computations={%region_0.1_spmd, %region_1.2_spmd} | conditional | flops 1000001024 | bytes 2130112 | solution.py:260
  0.0 4.6 %collective-permute-start.3 = (f32[192,128]{1,0:T(8,128)}, f32[192,128]{1,0:T(8,128)S(1)}, u32[]{:S(2)}, u32[]{:S(2)}) collective-permute-start(f32[192,128]{1,0:T(8,128)} %get-tuple-element.38.refs_1_), channel_id=1, source_target_pairs={{0,504},{8,16},{16,8},{24,32},{32,24},{40,48},{48,40},{56,64},{64,... | collective-permute-start | bytes 294920 | tf_op jit(solution)/shard_map/cond/branch_1_fun/ppermute | solution.py:228
  4.6 6.1 %collective-permute-start.2 = (f32[192,128]{1,0:T(8,128)}, f32[192,128]{1,0:T(8,128)S(1)}, u32[]{:S(2)}, u32[]{:S(2)}) collective-permute-start(f32[192,128]{1,0:T(8,128)} %get-tuple-element.38.refs_1_), channel_id=1, source_target_pairs={{0,8},{8,0},{16,24},{24,16},{32,40},{40,32},{48,56},{56,48},{64,72... | collective-permute-start | bytes 294920 | tf_op jit(solution)/shard_map/cond/branch_1_fun/ppermute | solution.py:229
  10.7 0.0 copy-start.1
  10.7 0.0 copy-start.3
  10.7 1.5 %branch_1_fun.4 = f32[64,128]{1,0:T(8,128)} custom-call(s32[1]{0:T(128)} %bitcast.refs_0_, s32[16,64]{1,0:T(8,128)} %bitcast.28, s32[1,64]{1,0:T(1,128)} %get-tuple-element.63.refs_2_, f32[2,16,64]{2,1,0:T(8,128)} %bitcast.27, f32[16,64]{1,0:T(8,128)} %bitcast.29, f32[16,64]{1,0:T(8,128)} %bitcast.30), custom_call_target="tpu_custom_call" | custom-call | flops 1000000000 | tf_op jit(solution)/shard_map/cond/branch_1_fun/pallas_call | solution.py:241
  12.3 11.1 %all-to-all-start = ((f32[64,1,128]{2,1,0:T(1,128)}), f32[64,1,128]{2,1,0:T(1,128)S(1)}, u32[]{:S(2)}, u32[]{:S(2)}) async-start(f32[64,1,128]{2,1,0:T(1,128)} %bitcast.10), calls=%async_computation | async-start | bytes 65536 | tf_op jit(solution)/shard_map/cond/branch_1_fun/all_to_all | solution.py:243
  23.4 0.0 collective-permute-done.3.refs_3_
  23.4 0.0 collective-permute-done.2.refs_2_
  23.4 0.0 copy-done.1
  23.4 0.0 copy-done.3
  23.4 1.3 %branch_1_fun.3 = (f32[32,128]{1,0:T(8,128)S(1)}, bf16[192,128]{1,0:T(8,128)(2,1)S(1)}) custom-call(s32[1]{0:T(128)} %get-tuple-element.37.refs_0_, f32[192,128]{1,0:T(8,128)S(1)} %copy-done.3, f32[192,128]{1,0:T(8,128)S(1)} %collective-permute-done.2.refs_2_, f32[192,128]{1,0:T(8,128)S(1)} %collective-permute-done.3.refs_3_, ...), custom_call_target="tpu_custom_call" | custom-call | flops 1000 | tf_op jit(solution)/shard_map/cond/branch_1_fun/pallas_call | solution.py:248
  24.7 0.7 %all-to-all-done = f32[64,1,128]{2,1,0:T(1,128)S(1)} async-done(((f32[64,1,128]{2,1,0:T(1,128)}), f32[64,1,128]{2,1,0:T(1,128)S(1)}, u32[]{:S(2)}, u32[]{:S(2)}) %all-to-all-start) | async-done | bytes 32800 | tf_op jit(solution)/shard_map/cond/branch_1_fun/all_to_all | solution.py:243
  25.5 0.1 branch_1_fun.5
  25.6 9.4 %all_to_all.9.refs_0_ = f32[8,48,128]{2,1,0:T(8,128)S(1)} all-to-all(f32[8,48,128]{2,1,0:T(8,128)S(1)} %get-tuple-element.51), channel_id=1, replica_groups={{7,6,5,4,3,2,1,0},{15,14,13,12,11,10,9,8},{23,22,21,20,19,18,17,16},{31..., dimensions={0} | all-to-all | bytes 393216 | tf_op jit(solution)/shard_map/all_to_all | solution.py:266
  35.0 0.0 copy-start
  35.0 0.0 copy-start.2
  35.0 0.7 %shard_map.87.refs_2_ = f32[192,128]{1,0:T(8,128)S(1)} custom-call(f32[8,48,128]{2,1,0:T(8,128)S(1)} %all_to_all.9.refs_0_, bf16[192,128]{1,0:T(8,128)(2,1)S(1)} %get-tuple-element.52.refs_1_), custom_call_target="tpu_custom_call" | custom-call | tf_op jit(solution)/shard_map/pallas_call | solution.py:270
  35.8 5.0 %collective-permute-start.5 = (f32[192,128]{1,0:T(8,128)S(1)}, f32[192,128]{1,0:T(8,128)S(1)}, u32[]{:S(2)}, u32[]{:S(2)}) collective-permute-start(f32[192,128]{1,0:T(8,128)S(1)} %shard_map.87.refs_2_), channel_id=1, source_target_pairs={{0,504},{8,16},{16,8},{24,32},{32,24},{40,48},{48,40},{56,64},{64,... | collective-permute-start | bytes 294920 | tf_op jit(solution)/shard_map/ppermute | solution.py:228
  40.8 3.5 %collective-permute-start.4 = (f32[192,128]{1,0:T(8,128)S(1)}, f32[192,128]{1,0:T(8,128)S(1)}, u32[]{:S(2)}, u32[]{:S(2)}) collective-permute-start(f32[192,128]{1,0:T(8,128)S(1)} %shard_map.87.refs_2_), channel_id=1, source_target_pairs={{0,8},{8,0},{16,24},{24,16},{32,40},{40,32},{48,56},{56,48},{64,72... | collective-permute-start | bytes 294920 | tf_op jit(solution)/shard_map/ppermute | solution.py:229
  44.3 0.0 collective-permute-done.5.refs_4_
  44.3 0.9 %collective-permute-done.4.refs_3_ = f32[192,128]{1,0:T(8,128)S(1)} collective-permute-done((f32[192,128]{1,0:T(8,128)S(1)}, f32[192,128]{1,0:T(8,128)S(1)}, u32[]{:S(2)}, u32[]{:S(2)}) %collective-permute-start.4) | collective-permute-done | bytes 98336 | tf_op jit(solution)/shard_map/ppermute | solution.py:229
  45.2 0.0 copy-done
  45.2 0.0 copy-done.2
  45.2 1.1 %shard_map.88 = f32[192,128]{1,0:T(8,128)} custom-call(s32[1]{0:T(128)} %bitcast.17.refs_0_, f32[192,128]{1,0:T(8,128)S(1)} %bitcast.24, f32[192,128]{1,0:T(8,128)S(1)} %shard_map.87.refs_2_, f32[192,128]{1,0:T(8,128)S(1)} %collective-permute-done.4.refs_3_, f32[192,128]{1,0:T(8,128)S(1)} %collective-permute-done.5.refs_4_, bf16[832,128]{1,0:T(8,128)(2,1)S(1)} %copy-done), custom_call_target="tpu_custom_call" | custom-call | tf_op jit(solution)/shard_map/pallas_call | solution.py:273
Async XLA Ops:
  0.0 23.4 %collective-permute-start.3 = (f32[192,128]{1,0:T(8,128)}, f32[192,128]{1,0:T(8,128)S(1)}, u32[]{:S(2)}, u32[]{:S(2)}) collective-permute-start(f32[192,128]{1,0:T(8,128)} %get-tuple-element.38.refs_1_), channel_id=1, source_target_pairs={{0,504},{8,16},{16,8},{24,32},{32,24},{40,48},{48,40},{56,64},{64,... | collective-permute-start | bytes 294920 | tf_op jit(solution)/shard_map/cond/branch_1_fun/ppermute | solution.py:228
  4.6 18.8 %collective-permute-start.2 = (f32[192,128]{1,0:T(8,128)}, f32[192,128]{1,0:T(8,128)S(1)}, u32[]{:S(2)}, u32[]{:S(2)}) collective-permute-start(f32[192,128]{1,0:T(8,128)} %get-tuple-element.38.refs_1_), channel_id=1, source_target_pairs={{0,8},{8,0},{16,24},{24,16},{32,40},{40,32},{48,56},{56,48},{64,72... | collective-permute-start | bytes 294920 | tf_op jit(solution)/shard_map/cond/branch_1_fun/ppermute | solution.py:229
  10.7 12.7 %copy-start.1 = (bf16[832,128]{1,0:T(8,128)(2,1)S(1)}, bf16[832,128]{1,0:T(8,128)(2,1)}, u32[]{:S(2)}) copy-start(bf16[832,128]{1,0:T(8,128)(2,1)} %get-tuple-element.40.refs_5_) | copy-start | bytes 638980 | tf_op jit(solution)/shard_map/cond
  10.7 12.7 %copy-start.3 = (f32[192,128]{1,0:T(8,128)S(1)}, f32[192,128]{1,0:T(8,128)}, u32[]{:S(2)}) copy-start(f32[192,128]{1,0:T(8,128)} %get-tuple-element.38.refs_1_) | copy-start | bytes 294916 | tf_op jit(solution)/shard_map/cond
  12.3 13.2 %all-to-all-start = ((f32[64,1,128]{2,1,0:T(1,128)}), f32[64,1,128]{2,1,0:T(1,128)S(1)}, u32[]{:S(2)}, u32[]{:S(2)}) async-start(f32[64,1,128]{2,1,0:T(1,128)} %bitcast.10), calls=%async_computation | async-start | bytes 65536 | tf_op jit(solution)/shard_map/cond/branch_1_fun/all_to_all | solution.py:243
  35.0 10.2 %copy-start = (bf16[832,128]{1,0:T(8,128)(2,1)S(1)}, bf16[832,128]{1,0:T(8,128)(2,1)}, u32[]{:S(2)}) copy-start(bf16[832,128]{1,0:T(8,128)(2,1)} %constant.26.clone.refs_5_) | copy-start | bytes 638980
  35.0 10.2 %copy-start.2 = (f32[6,2,16,128]{3,2,1,0:T(8,128)S(1)}, f32[6,2,16,128]{3,2,1,0:T(8,128)}, u32[]{:S(2)}) copy-start(f32[6,2,16,128]{3,2,1,0:T(8,128)} %param.11) | copy-start | bytes 294916
  35.8 8.6 %collective-permute-start.5 = (f32[192,128]{1,0:T(8,128)S(1)}, f32[192,128]{1,0:T(8,128)S(1)}, u32[]{:S(2)}, u32[]{:S(2)}) collective-permute-start(f32[192,128]{1,0:T(8,128)S(1)} %shard_map.87.refs_2_), channel_id=1, source_target_pairs={{0,504},{8,16},{16,8},{24,32},{32,24},{40,48},{48,40},{56,64},{64,... | collective-permute-start | bytes 294920 | tf_op jit(solution)/shard_map/ppermute | solution.py:228
  40.8 4.5 %collective-permute-start.4 = (f32[192,128]{1,0:T(8,128)S(1)}, f32[192,128]{1,0:T(8,128)S(1)}, u32[]{:S(2)}, u32[]{:S(2)}) collective-permute-start(f32[192,128]{1,0:T(8,128)S(1)} %shard_map.87.refs_2_), channel_id=1, source_target_pairs={{0,8},{8,0},{16,24},{24,16},{32,40},{40,32},{48,56},{56,48},{64,72... | collective-permute-start | bytes 294920 | tf_op jit(solution)/shard_map/ppermute | solution.py:229

commit v5 on v4

--- a/solution.py
+++ b/solution.py
@@ -1,3 +1,4 @@
+import functools
 import math
 
 import jax
@@ -13,8 +14,9 @@
 F32 = jnp.float32
 BF16 = jnp.bfloat16
 ROUTING_PLANES = (0, 1)
-TILE_BLOCKS = (5, 6, 7, 0, 1, 2, 3, 4)
-MEMBER_ORDER = (7, 6, 5, 4, 3, 2, 1, 0)
+FIRST_BLOCKS = (5, 6, 7, 0, 1, 2, 3, 4)
+SECOND_BLOCKS = (5, 6, 7, 0, 1, 2, 3, 4)
+MEMBER_ORDER = (7, 6, 4, 5, 1, 0, 3, 2)
 
 
 def halves(table):
@@ -41,8 +43,8 @@
     return high, (values - high.astype(F32)).astype(BF16)
 
 
-def localize(extended, table_ref, rows):
-    flat, depth = extended.shape
+def localize(high, low, table_ref, rows):
+    flat, depth = high.shape
     cols = table_ref.shape[1]
     row_block = lax.broadcasted_iota(jnp.int32, (flat, flat), 0) // rows
     same = row_block == lax.broadcasted_iota(jnp.int32, (flat, flat), 1) // rows
@@ -54,7 +56,6 @@
 
     mixed_high, mixed_low = mixing(2 * depth), mixing(2 * depth + rows)
     band_high, band_low = table_ref[:depth], table_ref[depth : 2 * depth]
-    high, low = split(extended)
     swept = jnp.dot(
         jnp.concatenate([high, low, high], axis=1),
         jnp.concatenate([band_high, band_high, band_low], axis=0),
@@ -71,13 +72,23 @@
     return jnp.concatenate([left, own, right], axis=1)
 
 
-def pack_kernel(blocks, part_ref, cell_ref, count_ref, frac_ref, innov_ref, prec_ref, out_ref):
+def payload_kernel(own_ref, perturb_ref, out_ref):
+    flat = own_ref.shape[0]
+    high, low = split(own_ref[...])
+    out_ref[:flat] = high
+    out_ref[flat : 2 * flat] = low
+    out_ref[2 * flat :] = perturb_ref[...]
+
+
+def pack_kernel(
+    blocks, part, own_ref, perturb_ref, cell_ref, count_ref, frac_ref, innov_ref, prec_ref, payload_ref, out_ref
+):
+    payload_kernel(own_ref, perturb_ref, payload_ref)
     tiles = innov_ref.shape[1]
     slots = innov_ref.shape[0] // len(ROUTING_PLANES)
     cols = out_ref.shape[1]
-    start = pl.multiple_of(part_ref[0] * slots, slots)
-    mine = pl.ds(start, slots)
-    slot = start + lax.broadcasted_iota(jnp.int32, (slots, tiles), 0)
+    mine = slice(part * slots, (part + 1) * slots)
+    slot = part * slots + lax.broadcasted_iota(jnp.int32, (slots, tiles), 0)
     live = jnp.where(slot < count_ref[...], 1.0, 0.0)
     cell = cell_ref[mine]
     corner_row = lax.shift_right_logical(cell, int(math.log2(cols)))
@@ -98,27 +109,28 @@
         out_ref[place * size : (place + 1) * size] = turned[block * size : (block + 1) * size]
 
 
-def partial_sum(spread, rows, even, own_ref, near_ref, far_ref, perturb_ref, table_ref):
-    extended = extend(even, own_ref[...], near_ref[...], far_ref[...])
-    product = perturb_ref[...].astype(F32) * localize(extended, table_ref, rows)
+def partial_sum(spread, rows, even, own_ref, near_ref, far_ref, table_ref, kept_ref):
+    flat = own_ref.shape[0] // 3
+    high, low, perturb = (
+        extend(even, *(ref[index * flat : (index + 1) * flat] for ref in (own_ref, near_ref, far_ref)))
+        for index in range(3)
+    )
+    kept_ref[...] = perturb
+    product = own_ref[2 * flat :].astype(F32) * localize(high, low, table_ref, rows)
     total = product[:rows]
-    for start in range(rows, product.shape[0], rows):
+    for start in range(rows, flat, rows):
         total = total + product[start : start + rows]
     return spread * total
 
 
-def partial_kernel(spread, even_ref, own_ref, near_ref, far_ref, perturb_ref, table_ref, out_ref, kept_ref):
+def partial_kernel(spread, even_ref, own_ref, near_ref, far_ref, table_ref, out_ref, kept_ref):
     even = even_ref[0] == 1
-    kept_ref[...] = perturb_ref[...]
-    out_ref[...] = partial_sum(spread, out_ref.shape[0], even, own_ref, near_ref, far_ref, perturb_ref, table_ref)
-
-
-def partial_copies_kernel(
-    spread, rows, even_ref, own_ref, near_ref, far_ref, perturb_ref, table_ref, out_ref, kept_ref
-):
+    out_ref[...] = partial_sum(spread, out_ref.shape[0], even, own_ref, near_ref, far_ref, table_ref, kept_ref)
+
+
+def partial_copies_kernel(spread, rows, even_ref, own_ref, near_ref, far_ref, table_ref, out_ref, kept_ref):
     even = even_ref[0] == 1
-    kept_ref[...] = perturb_ref[...]
-    total = partial_sum(spread, rows, even, own_ref, near_ref, far_ref, perturb_ref, table_ref)
+    total = partial_sum(spread, rows, even, own_ref, near_ref, far_ref, table_ref, kept_ref)
     for copy in range(out_ref.shape[0]):
         out_ref[copy, :rows] = total
         out_ref[copy, rows:] = jnp.zeros((out_ref.shape[1] - rows, out_ref.shape[2]), F32)
@@ -137,7 +149,7 @@
         out_ref[copy, rows + slots :] = values
 
 
-def obs_kernel(half, sources, partial_ref, perturb_ref, out_ref):
+def obs_kernel(half, sources, partial_ref, out_ref):
     rows = partial_ref.shape[1] - 2 * half
     field = partial_ref[0, :rows]
     for member in range(1, partial_ref.shape[0]):
@@ -176,20 +188,20 @@
     weighted = jnp.concatenate(weighted, axis=1)
     rows_high, rows_low = split(row_all * weighted)
     cols_high, cols_low = split(jnp.concatenate(col_parts, axis=1))
-    adjoint = lax.dot_general(
-        jnp.concatenate([rows_high, rows_low, rows_high], axis=1),
-        jnp.concatenate([cols_high, cols_high, cols_low], axis=1),
-        (((1,), (1,)), ((), ())),
-        preferred_element_type=F32,
-    )
-    for start in range(0, out_ref.shape[0], rows):
-        out_ref[start : start + rows] = perturb_ref[start : start + rows].astype(F32) * adjoint
-
-
-def final_kernel(spread, rows, even_ref, control_ref, own_ref, near_ref, far_ref, table_ref, out_ref):
+    contract = (((1,), (1,)), ((), ()))
+    both = jnp.concatenate([rows_high, rows_low], axis=0)
+    both = lax.dot_general(both, cols_high, contract, preferred_element_type=F32)
+    rest = lax.dot_general(rows_high, cols_low, contract, preferred_element_type=F32)
+    out_ref[...] = both[:rows] + both[rows:] + rest
+
+
+def final_kernel(spread, even_ref, control_ref, own_ref, near_ref, far_ref, kept_ref, table_ref, out_ref):
     even = even_ref[0] == 1
-    extended = extend(even, own_ref[...], near_ref[...], far_ref[...])
-    out_ref[...] = control_ref[...] + spread * localize(extended, table_ref, rows)
+    rows = own_ref.shape[0]
+    adjoint = extend(even, own_ref[...], near_ref[...], far_ref[...])
+    adjoint = jnp.concatenate([adjoint] * (out_ref.shape[0] // rows), axis=0)
+    high, low = split(kept_ref[...].astype(F32) * adjoint)
+    out_ref[...] = control_ref[...] + spread * localize(high, low, table_ref, rows)
 
 
 def call(kernel, out_shapes, scalars, arrays, flops=None):
@@ -218,59 +230,60 @@
     rows = levels * row_count
     table = jnp.asarray(tables(col_count, row_count, YSCALE, levels))
     even = (1 - lax.axis_index("tile") % 2).astype(jnp.int32).reshape(1)
-    size = tiles // len(TILE_BLOCKS)
-    tile_order = [[block * size + i for block in TILE_BLOCKS for i in range(size)]]
     member_order = [list(MEMBER_ORDER)]
     near_pairs = [(i, i ^ 1) for i in range(tiles)]
     far_pairs = [(i, (i + 1) % tiles if i % 2 else (i - 1) % tiles) for i in range(tiles)]
 
     def neighbours(own):
         far = lax.ppermute(own, "tile", far_pairs)
-        near = lax.ppermute(own, "tile", near_pairs)
-        return near, far
+        return lax.ppermute(own, "tile", near_pairs), far
 
     flat = mem_local * rows
     half = slots // len(ROUTING_PLANES)
     joined = (members, rows + 2 * half, col_count)
 
-    kept = ((flat, col_count), BF16)
-
-    def route(part, even, own, weights, table, cell, count, frac, innov, prec):
+    kept = ((flat, 3 * col_count), BF16)
+    payload = ((3 * flat, col_count), BF16)
+
+    def route(part, blocks, even, own, weights, table, cell, count, frac, innov, prec):
+        size = tiles // len(blocks)
+        tile_order = [[block * size + i for block in blocks for i in range(size)]]
         obs = (cell[0].T, count, frac[0].transpose(0, 2, 1), innov[0].T, prec[0].T)
-        pack = call(lambda *refs: pack_kernel(TILE_BLOCKS, *refs), [((tiles, col_count), F32)], 1, 5, 10**9)
-        (packed,) = pack(part, *map(in_hbm, obs))
+        packed = ((tiles, col_count), F32)
+        pack = call(lambda *refs: pack_kernel(blocks, part, *refs), [payload, packed], 0, 7, 10**9)
+        sent, packed = pack(*map(in_hbm, (own, weights, *obs)))
+        near, far = neighbours(sent)
         packed = packed.reshape(tiles, 1, col_count)
         arrived = lax.all_to_all(
             packed, "tile", split_axis=0, concat_axis=0, tiled=True, axis_index_groups=tile_order
         )
-        near, far = neighbours(own)
-        summing = call(lambda *refs: partial_kernel(spread, *refs), [((rows, col_count), F32), kept], 1, 5, 1000)
-        partial, weights = summing(even, own, near, far, in_hbm(weights), table)
+        summing = call(lambda *refs: partial_kernel(spread, *refs), [((rows, col_count), F32), kept], 1, 4, 1000)
+        partial, weights = summing(even, sent, near, far, table)
         (partials,) = call(join_kernel, [(joined, F32)], 0, 2)(partial, arrived.reshape(tiles, col_count))
         return partials, weights
 
-    def plain(part, even, own, weights, table, cell, count, frac, innov, prec):
-        near, far = neighbours(own)
-        summing = call(lambda *refs: partial_copies_kernel(spread, rows, *refs), [(joined, F32), kept], 1, 5)
-        return tuple(summing(even, own, near, far, in_hbm(weights), table))
+    def plain(even, own, weights, table, cell, count, frac, innov, prec):
+        (sent,) = call(payload_kernel, [payload], 0, 2, 10**9)(in_hbm(own), in_hbm(weights))
+        near, far = neighbours(sent)
+        summing = call(lambda *refs: partial_copies_kernel(spread, rows, *refs), [(joined, F32), kept], 1, 4)
+        return tuple(summing(even, sent, near, far, table))
 
     own = control.reshape(flat, col_count)
     weights = perturb.reshape(flat, col_count)
-    part = (lax.axis_index("mem") - ROUTING_PLANES[0]).astype(jnp.int32).reshape(1)
-    partials, weights = lax.cond(
-        (part[0] >= 0) & (part[0] < len(ROUTING_PLANES)),
-        route,
-        plain,
-        *(part, even, own, weights, table, obs_cell, obs_count, obs_frac, obs_innov, obs_prec),
+    plane = lax.axis_index("mem")
+    branches = [functools.partial(route, part, blocks) for part, blocks in enumerate((FIRST_BLOCKS, SECOND_BLOCKS))]
+    which = jnp.where(plane == ROUTING_PLANES[0], 0, jnp.where(plane == ROUTING_PLANES[1], 1, 2))
+    partials, weights = lax.switch(
+        which, [*branches, plain], even, own, weights, table, obs_cell, obs_count, obs_frac, obs_innov, obs_prec
     )
     partials = lax.all_to_all(
         partials, "mem", split_axis=0, concat_axis=0, tiled=True, axis_index_groups=member_order
     )
     sources = [MEMBER_ORDER.index(plane) for plane in ROUTING_PLANES]
-    (product,) = call(lambda *refs: obs_kernel(half, sources, *refs), [((flat, col_count), F32)], 0, 2)(partials, weights)
-    near, far = neighbours(product)
-    finish = call(lambda *refs: final_kernel(spread, rows, *refs), [((flat, col_count), F32)], 1, 5)
-    (gradient,) = finish(even, own, product, near, far, table)
+    (adjoint,) = call(lambda *refs: obs_kernel(half, sources, *refs), [((rows, col_count), F32)], 0, 1)(partials)
+    near, far = neighbours(adjoint)
+    finish = call(lambda *refs: final_kernel(spread, *refs), [((flat, col_count), F32)], 1, 6)
+    (gradient,) = finish(even, own, adjoint, near, far, weights, table)
     return gradient.reshape(control.shape)
 
 

time: 46.7 us -> 46.2 us (0.989)
  waiting for transfers between devices: 1.67 us -> 2.36 us
  Pallas kernels: 4.74 us -> 4.06 us
  blocking collectives: 9.45 us -> 8.95 us
    all_to_all x1, waiting for transfers between devices: 0.75 us -> 1.54 us  [route(): lax.all_to_all(packed, 'tile', split_axis=0, concat_axis=0, tiled=True, a...]
    pallas_call x4, Pallas kernels: 4.65 us -> 3.97 us  [the longest x1 1.71 us: route(): sent, packed = pack(*map(in_hbm, (own, weights, *obs)))]
    all_to_all x1, blocking collectives: 9.45 us -> 8.95 us  [per_device(): lax.all_to_all(partials, 'mem', split_axis=0, concat_axis=0, tiled=True,...]
  transfers between devices with their start and end apart: 5 -> 5, of which waited for: 2 -> 2; matrix products, arithmetic and copies ran while one was open for 0% -> 0% of each run, Pallas kernels for 6% -> 1%
where the time goes in v5:
time: 46.2 us; the launch traced here: 45.9 us
  starting transfers between devices  30.4 us (66%)
  blocking collectives  8.95 us (19%)
  Pallas kernels  4.06 us (9%)
  waiting for transfers between devices  2.36 us (5%)
    all_to_all x1, starting transfers between devices, route(): lax.all_to_all(packed, 'tile', split_axis=0, concat_axis=0, tiled=True, a...  11.1 us
    ppermute x2, starting transfers between devices, neighbours(): far = lax.ppermute(own, 'tile', far_pairs)  10 us
    ppermute x2, starting transfers between devices, neighbours(): return (lax.ppermute(own, 'tile', near_pairs), far)  9.23 us
    all_to_all x1, blocking collectives, per_device(): lax.all_to_all(partials, 'mem', split_axis=0, concat_axis=0, tiled=True,...  8.95 us
    pallas_call x1, Pallas kernels, route(): sent, packed = pack(*map(in_hbm, (own, weights, *obs)))  1.71 us
    all_to_all x1, waiting for transfers between devices, route(): lax.all_to_all(packed, 'tile', split_axis=0, concat_axis=0, tiled=True, a...  1.54 us
    pallas_call x1, Pallas kernels, per_device(): gradient, = finish(even, own, adjoint, near, far, weights, table)  1.13 us
  transfers between devices with their start and end apart: 5, of which 2 were waited for; matrix products, arithmetic and copies ran while one was open for 0% of the time, Pallas kernels for 1%

profile of v5, /device:TPU:1, one launch (start us, length us, event | category | flops | bytes accessed | tf_op | source)
XLA Modules:
  0.0 45.9 jit_solution(5344193331841583504)
XLA Ops:
  0.0 25.7 %conditional.1 = ((f32[8,48,128]{2,1,0:T(8,128)S(1)}, bf16[192,384]{1,0:T(8,128)(2,1)S(1)})) conditional(s32[]{:T(128)} %clamp.3, (s32[1,64,16]{1,2,0:T(8,128)}, f32[1,2,64,16]{2,3,1,0:T(8,128)}, f32[1,64,16]{1,2,0:T(8,128)}, f32[1,64,16]{1,2,0:T(8,128)}, f32[192,128]{1,0:T(8,128)}, /*index=5*/bf16[192,128]{1,0:T(8,128)(2,1)}, ...), branch_computations={%region_0.1_spmd, %region_1.2_spmd, %region_2.3_spmd} | conditional | flops 1000001024 | bytes 2130084 | solution.py:276
  0.0 0.0 copy-start.1
  0.0 1.7 %branch_0_fun.3 = (bf16[576,128]{1,0:T(8,128)(2,1)S(1)}, f32[64,128]{1,0:T(8,128)}) custom-call(f32[192,128]{1,0:T(8,128)} %get-tuple-element.50.refs_0_, bf16[192,128]{1,0:T(8,128)(2,1)} %get-tuple-element.51.refs_1_, s32[16,64]{1,0:T(8,128)} %bitcast.47, s32[1,64]{1,0:T(1,128)} %get-tuple-element.101.refs_3_, f32[2,16,64]{2,1,0:T(8,128)} %bitcast.45, ...), custom_call_target="tpu_custom_call" | custom-call | flops 1000000000 | tf_op jit(solution)/shard_map/cond/branch_0_fun/pallas_call | solution.py:254
  1.7 4.6 %collective-permute-start.1 = (bf16[576,128]{1,0:T(8,128)(2,1)S(1)}, bf16[576,128]{1,0:T(8,128)(2,1)S(1)}, u32[]{:S(2)}, u32[]{:S(2)}) collective-permute-start(bf16[576,128]{1,0:T(8,128)(2,1)S(1)} %get-tuple-element.57.refs_1_), channel_id=1, source_target_pairs={{0,504},{8,16},{16,8},{24,32},{32,24},{40,48},{48,40},{56,64},{64,... | collective-permute-start | bytes 442376 | tf_op jit(solution)/shard_map/cond/branch_0_fun/ppermute | solution.py:238
  6.3 6.1 %collective-permute-start = (bf16[576,128]{1,0:T(8,128)(2,1)S(1)}, bf16[576,128]{1,0:T(8,128)(2,1)S(1)}, u32[]{:S(2)}, u32[]{:S(2)}) collective-permute-start(bf16[576,128]{1,0:T(8,128)(2,1)S(1)} %get-tuple-element.57.refs_1_), channel_id=1, source_target_pairs={{0,8},{8,0},{16,24},{24,16},{32,40},{40,32},{48,56},{56,48},{64,72... | collective-permute-start | bytes 442376 | tf_op jit(solution)/shard_map/cond/branch_0_fun/ppermute | solution.py:239
  12.4 11.1 %all-to-all-start = ((f32[64,1,128]{2,1,0:T(1,128)}), f32[64,1,128]{2,1,0:T(1,128)S(1)}, u32[]{:S(2)}, u32[]{:S(2)}) async-start(f32[64,1,128]{2,1,0:T(1,128)} %bitcast.9), calls=%async_computation | async-start | bytes 65536 | tf_op jit(solution)/shard_map/cond/branch_0_fun/all_to_all | solution.py:257
  23.6 0.0 collective-permute-done.1.refs_3_
  23.6 0.0 collective-permute-done.refs_2_
  23.6 0.0 copy-done.1
  23.6 0.5 %branch_0_fun.4 = (f32[32,128]{1,0:T(8,128)S(1)}, bf16[192,384]{1,0:T(8,128)(2,1)S(1)}) custom-call(s32[1]{0:T(128)} %get-tuple-element.49.refs_0_, bf16[576,128]{1,0:T(8,128)(2,1)S(1)} %get-tuple-element.57.refs_1_, bf16[576,128]{1,0:T(8,128)(2,1)S(1)} %collective-permute-done.refs_2_, bf16[576,128]{1,0:T(8,128)(2,1)S(1)} %collective-permute-done.1.refs_3_, ...), custom_call_target="tpu_custom_call" | custom-call | flops 1000 | tf_op jit(solution)/shard_map/cond/branch_0_fun/pallas_call | solution.py:261
  24.1 1.5 %all-to-all-done = f32[64,1,128]{2,1,0:T(1,128)S(1)} async-done(((f32[64,1,128]{2,1,0:T(1,128)}), f32[64,1,128]{2,1,0:T(1,128)S(1)}, u32[]{:S(2)}, u32[]{:S(2)}) %all-to-all-start) | async-done | bytes 32800 | tf_op jit(solution)/shard_map/cond/branch_0_fun/all_to_all | solution.py:257
  25.6 0.1 branch_0_fun.5
  25.7 0.0 copy-start
  25.7 9.0 %all_to_all.13.refs_0_ = f32[8,48,128]{2,1,0:T(8,128)S(1)} all-to-all(f32[8,48,128]{2,1,0:T(8,128)S(1)} %get-tuple-element.81), channel_id=1, replica_groups={{7,6,4,5,1,0,3,2},{15,14,12,13,9,8,11,10},{23,22,20,21,17,16,19,18},{31..., dimensions={0} | all-to-all | bytes 393216 | tf_op jit(solution)/shard_map/all_to_all | solution.py:279
  34.7 0.0 copy-start.4
  34.7 0.6 %shard_map.92.refs_2_ = f32[32,128]{1,0:T(8,128)S(1)} custom-call(f32[8,48,128]{2,1,0:T(8,128)S(1)} %all_to_all.13.refs_0_), custom_call_target="tpu_custom_call" | custom-call | tf_op jit(solution)/shard_map/pallas_call | solution.py:283
  35.3 5.4 %collective-permute-start.7 = (f32[32,128]{1,0:T(8,128)S(1)}, f32[32,128]{1,0:T(8,128)S(1)}, u32[]{:S(2)}, u32[]{:S(2)}) collective-permute-start(f32[32,128]{1,0:T(8,128)S(1)} %shard_map.92.refs_2_), channel_id=1, source_target_pairs={{0,504},{8,16},{16,8},{24,32},{32,24},{40,48},{48,40},{56,64},{64,... | collective-permute-start | bytes 49160 | tf_op jit(solution)/shard_map/ppermute | solution.py:238
  40.8 3.1 %collective-permute-start.6 = (f32[32,128]{1,0:T(8,128)S(1)}, f32[32,128]{1,0:T(8,128)S(1)}, u32[]{:S(2)}, u32[]{:S(2)}) collective-permute-start(f32[32,128]{1,0:T(8,128)S(1)} %shard_map.92.refs_2_), channel_id=1, source_target_pairs={{0,8},{8,0},{16,24},{24,16},{32,40},{40,32},{48,56},{56,48},{64,72... | collective-permute-start | bytes 49160 | tf_op jit(solution)/shard_map/ppermute | solution.py:239
  43.9 0.0 collective-permute-done.7.refs_4_
  43.9 0.8 %collective-permute-done.6.refs_3_ = f32[32,128]{1,0:T(8,128)S(1)} collective-permute-done((f32[32,128]{1,0:T(8,128)S(1)}, f32[32,128]{1,0:T(8,128)S(1)}, u32[]{:S(2)}, u32[]{:S(2)}) %collective-permute-start.6) | collective-permute-done | bytes 16416 | tf_op jit(solution)/shard_map/ppermute | solution.py:239
  44.7 0.0 copy-done
  44.7 0.0 copy-done.4
  44.7 1.1 %shard_map.93 = f32[192,128]{1,0:T(8,128)} custom-call(s32[1]{0:T(128)} %bitcast.32.refs_0_, f32[192,128]{1,0:T(8,128)S(1)} %bitcast.41, f32[32,128]{1,0:T(8,128)S(1)} %shard_map.92.refs_2_, f32[32,128]{1,0:T(8,128)S(1)} %collective-permute-done.6.refs_3_, f32[32,128]{1,0:T(8,128)S(1)} %collective-permute-done.7.refs_4_, ...), custom_call_target="tpu_custom_call" | custom-call | tf_op jit(solution)/shard_map/pallas_call | solution.py:286
Async XLA Ops:
  0.0 23.6 %copy-start.1 = (bf16[832,128]{1,0:T(8,128)(2,1)S(1)}, bf16[832,128]{1,0:T(8,128)(2,1)}, u32[]{:S(2)}) copy-start(bf16[832,128]{1,0:T(8,128)(2,1)} %get-tuple-element.58.refs_4_) | copy-start | bytes 638980 | tf_op jit(solution)/shard_map/cond
  1.7 21.9 %collective-permute-start.1 = (bf16[576,128]{1,0:T(8,128)(2,1)S(1)}, bf16[576,128]{1,0:T(8,128)(2,1)S(1)}, u32[]{:S(2)}, u32[]{:S(2)}) collective-permute-start(bf16[576,128]{1,0:T(8,128)(2,1)S(1)} %get-tuple-element.57.refs_1_), channel_id=1, source_target_pairs={{0,504},{8,16},{16,8},{24,32},{32,24},{40,48},{48,40},{56,64},{64,... | collective-permute-start | bytes 442376 | tf_op jit(solution)/shard_map/cond/branch_0_fun/ppermute | solution.py:238
  6.3 17.3 %collective-permute-start = (bf16[576,128]{1,0:T(8,128)(2,1)S(1)}, bf16[576,128]{1,0:T(8,128)(2,1)S(1)}, u32[]{:S(2)}, u32[]{:S(2)}) collective-permute-start(bf16[576,128]{1,0:T(8,128)(2,1)S(1)} %get-tuple-element.57.refs_1_), channel_id=1, source_target_pairs={{0,8},{8,0},{16,24},{24,16},{32,40},{40,32},{48,56},{56,48},{64,72... | collective-permute-start | bytes 442376 | tf_op jit(solution)/shard_map/cond/branch_0_fun/ppermute | solution.py:239
  12.4 13.2 %all-to-all-start = ((f32[64,1,128]{2,1,0:T(1,128)}), f32[64,1,128]{2,1,0:T(1,128)S(1)}, u32[]{:S(2)}, u32[]{:S(2)}) async-start(f32[64,1,128]{2,1,0:T(1,128)} %bitcast.9), calls=%async_computation | async-start | bytes 65536 | tf_op jit(solution)/shard_map/cond/branch_0_fun/all_to_all | solution.py:257
  25.7 19.0 %copy-start = (bf16[832,128]{1,0:T(8,128)(2,1)S(1)}, bf16[832,128]{1,0:T(8,128)(2,1)}, u32[]{:S(2)}) copy-start(bf16[832,128]{1,0:T(8,128)(2,1)} %constant.26.clone.refs_6_) | copy-start | bytes 638980
  34.7 10.0 %copy-start.4 = (f32[6,2,16,128]{3,2,1,0:T(8,128)S(1)}, f32[6,2,16,128]{3,2,1,0:T(8,128)}, u32[]{:S(2)}) copy-start(f32[6,2,16,128]{3,2,1,0:T(8,128)} %param.12) | copy-start | bytes 294916
  35.3 8.6 %collective-permute-start.7 = (f32[32,128]{1,0:T(8,128)S(1)}, f32[32,128]{1,0:T(8,128)S(1)}, u32[]{:S(2)}, u32[]{:S(2)}) collective-permute-start(f32[32,128]{1,0:T(8,128)S(1)} %shard_map.92.refs_2_), channel_id=1, source_target_pairs={{0,504},{8,16},{16,8},{24,32},{32,24},{40,48},{48,40},{56,64},{64,... | collective-permute-start | bytes 49160 | tf_op jit(solution)/shard_map/ppermute | solution.py:238
  40.8 3.9 %collective-permute-start.6 = (f32[32,128]{1,0:T(8,128)S(1)}, f32[32,128]{1,0:T(8,128)S(1)}, u32[]{:S(2)}, u32[]{:S(2)}) collective-permute-start(f32[32,128]{1,0:T(8,128)S(1)} %shard_map.92.refs_2_), channel_id=1, source_target_pairs={{0,8},{8,0},{16,24},{24,16},{32,40},{40,32},{48,56},{56,48},{64,72... | collective-permute-start | bytes 49160 | tf_op jit(solution)/shard_map/ppermute | solution.py:239

commit v6 on v5

--- a/solution.py
+++ b/solution.py
@@ -16,6 +16,8 @@
 ROUTING_PLANES = (0, 1)
 FIRST_BLOCKS = (5, 6, 7, 0, 1, 2, 3, 4)
 SECOND_BLOCKS = (5, 6, 7, 0, 1, 2, 3, 4)
+WIDE = 3
+FAR_PAD = 400
 MEMBER_ORDER = (7, 6, 4, 5, 1, 0, 3, 2)
 
 
@@ -81,12 +83,15 @@
 
 
 def pack_kernel(
-    blocks, part, own_ref, perturb_ref, cell_ref, count_ref, frac_ref, innov_ref, prec_ref, payload_ref, out_ref
+    blocks, part, own_ref, perturb_ref, cell_ref, count_ref, frac_ref, innov_ref, prec_ref, payload_ref, wider_ref, out_ref
 ):
     payload_kernel(own_ref, perturb_ref, payload_ref)
+    length = payload_ref.shape[0]
+    wider_ref[:length] = payload_ref[...]
+    wider_ref[length:] = jnp.zeros((wider_ref.shape[0] - length, wider_ref.shape[1]), BF16)
     tiles = innov_ref.shape[1]
     slots = innov_ref.shape[0] // len(ROUTING_PLANES)
-    cols = out_ref.shape[1]
+    cols = payload_ref.shape[1]
     mine = slice(part * slots, (part + 1) * slots)
     slot = part * slots + lax.broadcasted_iota(jnp.int32, (slots, tiles), 0)
     live = jnp.where(slot < count_ref[...], 1.0, 0.0)
@@ -99,14 +104,15 @@
             corner_row.astype(F32) + frac_ref[1, mine],
             innov_ref[mine],
             prec_ref[mine] * live,
-            jnp.zeros((out_ref.shape[1] - 4 * slots, tiles), F32),
+            jnp.zeros((cols - 4 * slots, tiles), F32),
         ],
         axis=0,
     )
     turned = jnp.transpose(packed)
     size = tiles // len(blocks)
     for place, block in enumerate(blocks):
-        out_ref[place * size : (place + 1) * size] = turned[block * size : (block + 1) * size]
+        out_ref[place * size : (place + 1) * size, 0, :cols] = turned[block * size : (block + 1) * size]
+    out_ref[:, 0, cols:] = jnp.zeros((tiles, out_ref.shape[2] - cols), F32)
 
 
 def partial_sum(spread, rows, even, own_ref, near_ref, far_ref, table_ref, kept_ref):
@@ -140,7 +146,7 @@
     rows = partial_ref.shape[0]
     slots = (out_ref.shape[1] - rows) // 2
     total = partial_ref[...]
-    turned = jnp.transpose(obs_ref[...])
+    turned = jnp.transpose(obs_ref[:, 0, : partial_ref.shape[1]])
     places = jnp.concatenate([turned[:slots], turned[slots : 2 * slots]], axis=1)
     values = jnp.concatenate([turned[2 * slots : 3 * slots], turned[3 * slots : 4 * slots]], axis=1)
     for copy in range(out_ref.shape[0]):
@@ -249,17 +255,18 @@
         size = tiles // len(blocks)
         tile_order = [[block * size + i for block in blocks for i in range(size)]]
         obs = (cell[0].T, count, frac[0].transpose(0, 2, 1), innov[0].T, prec[0].T)
-        packed = ((tiles, col_count), F32)
-        pack = call(lambda *refs: pack_kernel(blocks, part, *refs), [payload, packed], 0, 7, 10**9)
-        sent, packed = pack(*map(in_hbm, (own, weights, *obs)))
-        near, far = neighbours(sent)
-        packed = packed.reshape(tiles, 1, col_count)
+        packed = ((tiles, 1, WIDE * col_count), F32)
+        wider = ((3 * flat + FAR_PAD, col_count), BF16)
+        pack = call(lambda *refs: pack_kernel(blocks, part, *refs), [payload, wider, packed], 0, 7, 10**9)
+        sent, sent_far, packed = pack(*map(in_hbm, (own, weights, *obs)))
+        far = lax.ppermute(sent_far, "tile", far_pairs)
+        near = lax.ppermute(sent, "tile", near_pairs)
         arrived = lax.all_to_all(
             packed, "tile", split_axis=0, concat_axis=0, tiled=True, axis_index_groups=tile_order
         )
         summing = call(lambda *refs: partial_kernel(spread, *refs), [((rows, col_count), F32), kept], 1, 4, 1000)
         partial, weights = summing(even, sent, near, far, table)
-        (partials,) = call(join_kernel, [(joined, F32)], 0, 2)(partial, arrived.reshape(tiles, col_count))
+        (partials,) = call(join_kernel, [(joined, F32)], 0, 2)(partial, arrived)
         return partials, weights
 
     def plain(even, own, weights, table, cell, count, frac, innov, prec):

time: 46.2 us -> 45.8 us (level)
  waiting for transfers between devices: 2.36 us -> 1.8 us
    ppermute x0 -> x2, starting transfers between devices: none -> 6.85 us  [the longest x1 4.58 us: route(): far = lax.ppermute(sent_far, 'tile', far_pairs)]
    ppermute x2 -> x1, starting transfers between devices: 9.23 us -> 3.32 us  [neighbours(): return (lax.ppermute(own, 'tile', near_pairs), far)]
    ppermute x2 -> x1, starting transfers between devices: 10 us -> 5.07 us  [neighbours(): far = lax.ppermute(own, 'tile', far_pairs)]
    all_to_all x1, starting transfers between devices: 11.1 us -> 14.9 us  [route(): lax.all_to_all(packed, 'tile', split_axis=0, concat_axis=0, tiled=True, a...]
    all_to_all x1, waiting for transfers between devices: 1.54 us -> 0.01 us  [route(): lax.all_to_all(packed, 'tile', split_axis=0, concat_axis=0, tiled=True, a...]
    ppermute x0 -> x2, waiting for transfers between devices: none -> 0.99 us  [the longest x1 0.99 us: route(): near = lax.ppermute(sent, 'tile', near_pairs)]
where the time goes in v6:
time: 45.8 us; the launch traced here: 45.5 us
  starting transfers between devices  30.2 us (66%)
  blocking collectives  9.26 us (20%)
  Pallas kernels  4.15 us (9%)
  waiting for transfers between devices  1.8 us (4%)
    all_to_all x1, starting transfers between devices, route(): lax.all_to_all(packed, 'tile', split_axis=0, concat_axis=0, tiled=True, a...  14.9 us
    all_to_all x1, blocking collectives, per_device(): lax.all_to_all(partials, 'mem', split_axis=0, concat_axis=0, tiled=True,...  9.26 us
    ppermute x1, starting transfers between devices, neighbours(): far = lax.ppermute(own, 'tile', far_pairs)  5.07 us
    ppermute x1, starting transfers between devices, route(): far = lax.ppermute(sent_far, 'tile', far_pairs)  4.58 us
    ppermute x1, starting transfers between devices, neighbours(): return (lax.ppermute(own, 'tile', near_pairs), far)  3.32 us
    ppermute x1, starting transfers between devices, route(): near = lax.ppermute(sent, 'tile', near_pairs)  2.27 us
    pallas_call x1, Pallas kernels, route(): sent, sent_far, packed = pack(*map(in_hbm, (own, weights, *obs)))  1.78 us
    pallas_call x1, Pallas kernels, per_device(): gradient, = finish(even, own, adjoint, near, far, weights, table)  1.13 us
  transfers between devices with their start and end apart: 5, of which 2 were waited for; matrix products, arithmetic and copies ran while one was open for 0% of the time, Pallas kernels for 1%

profile of v6, /device:TPU:1, one launch (start us, length us, event | category | flops | bytes accessed | tf_op | source)
XLA Modules:
  0.0 45.5 jit_solution(13776820792351501869)
XLA Ops:
  0.0 25.2 %conditional.1 = ((f32[8,48,128]{2,1,0:T(8,128)S(1)}, bf16[192,384]{1,0:T(8,128)(2,1)S(1)})) conditional(s32[]{:T(128)} %clamp.3, (s32[1,64,16]{1,2,0:T(8,128)}, f32[1,2,64,16]{2,3,1,0:T(8,128)}, f32[1,64,16]{1,2,0:T(8,128)}, f32[1,64,16]{1,2,0:T(8,128)}, f32[192,128]{1,0:T(8,128)}, /*index=5*/bf16[192,128]{1,0:T(8,128)(2,1)}, ...), branch_computations={%region_0.1_spmd, %region_1.2_spmd, %region_2.3_spmd} | conditional | flops 1000001024 | bytes 2736292 | solution.py:283
  0.0 0.0 copy-start.1
  0.0 1.8 %branch_0_fun.3 = (bf16[576,128]{1,0:T(8,128)(2,1)S(1)}, bf16[976,128]{1,0:T(8,128)(2,1)S(1)}, f32[64,1,384]{2,1,0:T(1,128)}) custom-call(f32[192,128]{1,0:T(8,128)} %get-tuple-element.50.refs_0_, bf16[192,128]{1,0:T(8,128)(2,1)} %get-tuple-element.51.refs_1_, s32[16,64]{1,0:T(8,128)} %bitcast.37, s32[1,64]{1,0:T(1,128)} %get-tuple-element.103.refs_3_, ...), custom_call_target="tpu_custom_call" | custom-call | flops 1000000000 | tf_op jit(solution)/shard_map/cond/branch_0_fun/pallas_call | solution.py:261
  1.8 4.6 %collective-permute-start.1 = (bf16[976,128]{1,0:T(8,128)(2,1)S(1)}, bf16[976,128]{1,0:T(8,128)(2,1)S(1)}, u32[]{:S(2)}, u32[]{:S(2)}) collective-permute-start(bf16[976,128]{1,0:T(8,128)(2,1)S(1)} %get-tuple-element.58), channel_id=1, source_target_pairs={{0,504},{8,16},{16,8},{24,32},{32,24},{40,48},{48,40},{56,64},{64,... | collective-permute-start | bytes 749576 | tf_op jit(solution)/shard_map/cond/branch_0_fun/ppermute | solution.py:262
  6.4 14.9 %all-to-all-start = ((f32[64,1,384]{2,1,0:T(1,128)}), f32[64,1,384]{2,1,0:T(1,128)S(1)}, u32[]{:S(2)}, u32[]{:S(2)}) async-start(f32[64,1,384]{2,1,0:T(1,128)} %get-tuple-element.61), calls=%async_computation | async-start | bytes 196608 | tf_op jit(solution)/shard_map/cond/branch_0_fun/all_to_all | solution.py:264
  21.3 2.3 %collective-permute-start = (bf16[576,128]{1,0:T(8,128)(2,1)S(1)}, bf16[576,128]{1,0:T(8,128)(2,1)S(1)}, u32[]{:S(2)}, u32[]{:S(2)}) collective-permute-start(bf16[576,128]{1,0:T(8,128)(2,1)S(1)} %get-tuple-element.57.refs_1_), channel_id=1, source_target_pairs={{0,8},{8,0},{16,24},{24,16},{32,40},{40,32},{48,56},{56,48},{64,72... | collective-permute-start | bytes 442376 | tf_op jit(solution)/shard_map/cond/branch_0_fun/ppermute | solution.py:263
  23.6 1.0 %collective-permute-done.refs_2_ = bf16[576,128]{1,0:T(8,128)(2,1)S(1)} collective-permute-done((bf16[576,128]{1,0:T(8,128)(2,1)S(1)}, bf16[576,128]{1,0:T(8,128)(2,1)S(1)}, u32[]{:S(2)}, u32[]{:S(2)}) %collective-permute-start) | collective-permute-done | bytes 147488 | tf_op jit(solution)/shard_map/cond/branch_0_fun/ppermute | solution.py:263
  24.6 0.0 collective-permute-done.1.refs_3_
  24.6 0.0 copy-done.1
  24.6 0.5 %branch_0_fun.4 = (f32[32,128]{1,0:T(8,128)S(1)}, bf16[192,384]{1,0:T(8,128)(2,1)S(1)}) custom-call(s32[1]{0:T(128)} %get-tuple-element.49.refs_0_, bf16[576,128]{1,0:T(8,128)(2,1)S(1)} %get-tuple-element.57.refs_1_, bf16[576,128]{1,0:T(8,128)(2,1)S(1)} %collective-permute-done.refs_2_, bf16[976,128]{1,0:T(8,128)(2,1)S(1)} %collective-permute-done.1.refs_3_, ...), custom_call_target="tpu_custom_call" | custom-call | flops 1000 | tf_op jit(solution)/shard_map/cond/branch_0_fun/pallas_call | solution.py:268
  25.1 0.0 all-to-all-done.obs_ref
  25.1 0.1 branch_0_fun.5
  25.2 0.0 copy-start
  25.2 9.3 %all_to_all.13.refs_0_ = f32[8,48,128]{2,1,0:T(8,128)S(1)} all-to-all(f32[8,48,128]{2,1,0:T(8,128)S(1)} %get-tuple-element.83), channel_id=1, replica_groups={{7,6,4,5,1,0,3,2},{15,14,12,13,9,8,11,10},{23,22,20,21,17,16,19,18},{31..., dimensions={0} | all-to-all | bytes 393216 | tf_op jit(solution)/shard_map/all_to_all | solution.py:286
  34.5 0.0 copy-start.4
  34.5 0.6 %shard_map.92.refs_2_ = f32[32,128]{1,0:T(8,128)S(1)} custom-call(f32[8,48,128]{2,1,0:T(8,128)S(1)} %all_to_all.13.refs_0_), custom_call_target="tpu_custom_call" | custom-call | tf_op jit(solution)/shard_map/pallas_call | solution.py:290
  35.1 5.1 %collective-permute-start.7 = (f32[32,128]{1,0:T(8,128)S(1)}, f32[32,128]{1,0:T(8,128)S(1)}, u32[]{:S(2)}, u32[]{:S(2)}) collective-permute-start(f32[32,128]{1,0:T(8,128)S(1)} %shard_map.92.refs_2_), channel_id=1, source_target_pairs={{0,504},{8,16},{16,8},{24,32},{32,24},{40,48},{48,40},{56,64},{64,... | collective-permute-start | bytes 49160 | tf_op jit(solution)/shard_map/ppermute | solution.py:244
  40.2 3.3 %collective-permute-start.6 = (f32[32,128]{1,0:T(8,128)S(1)}, f32[32,128]{1,0:T(8,128)S(1)}, u32[]{:S(2)}, u32[]{:S(2)}) collective-permute-start(f32[32,128]{1,0:T(8,128)S(1)} %shard_map.92.refs_2_), channel_id=1, source_target_pairs={{0,8},{8,0},{16,24},{24,16},{32,40},{40,32},{48,56},{56,48},{64,72... | collective-permute-start | bytes 49160 | tf_op jit(solution)/shard_map/ppermute | solution.py:245
  43.5 0.0 collective-permute-done.7.refs_4_
  43.5 0.8 %collective-permute-done.6.refs_3_ = f32[32,128]{1,0:T(8,128)S(1)} collective-permute-done((f32[32,128]{1,0:T(8,128)S(1)}, f32[32,128]{1,0:T(8,128)S(1)}, u32[]{:S(2)}, u32[]{:S(2)}) %collective-permute-start.6) | collective-permute-done | bytes 16416 | tf_op jit(solution)/shard_map/ppermute | solution.py:245
  44.3 0.0 copy-done
  44.3 0.0 copy-done.4
  44.3 1.1 %shard_map.93 = f32[192,128]{1,0:T(8,128)} custom-call(s32[1]{0:T(128)} %bitcast.24.refs_0_, f32[192,128]{1,0:T(8,128)S(1)} %bitcast.31, f32[32,128]{1,0:T(8,128)S(1)} %shard_map.92.refs_2_, f32[32,128]{1,0:T(8,128)S(1)} %collective-permute-done.6.refs_3_, f32[32,128]{1,0:T(8,128)S(1)} %collective-permute-done.7.refs_4_, ...), custom_call_target="tpu_custom_call" | custom-call | tf_op jit(solution)/shard_map/pallas_call | solution.py:293
Async XLA Ops:
  0.0 24.6 %copy-start.1 = (bf16[832,128]{1,0:T(8,128)(2,1)S(1)}, bf16[832,128]{1,0:T(8,128)(2,1)}, u32[]{:S(2)}) copy-start(bf16[832,128]{1,0:T(8,128)(2,1)} %get-tuple-element.59.refs_4_) | copy-start | bytes 638980 | tf_op jit(solution)/shard_map/cond
  1.8 22.8 %collective-permute-start.1 = (bf16[976,128]{1,0:T(8,128)(2,1)S(1)}, bf16[976,128]{1,0:T(8,128)(2,1)S(1)}, u32[]{:S(2)}, u32[]{:S(2)}) collective-permute-start(bf16[976,128]{1,0:T(8,128)(2,1)S(1)} %get-tuple-element.58), channel_id=1, source_target_pairs={{0,504},{8,16},{16,8},{24,32},{32,24},{40,48},{48,40},{56,64},{64,... | collective-permute-start | bytes 749576 | tf_op jit(solution)/shard_map/cond/branch_0_fun/ppermute | solution.py:262
  6.4 18.7 %all-to-all-start = ((f32[64,1,384]{2,1,0:T(1,128)}), f32[64,1,384]{2,1,0:T(1,128)S(1)}, u32[]{:S(2)}, u32[]{:S(2)}) async-start(f32[64,1,384]{2,1,0:T(1,128)} %get-tuple-element.61), calls=%async_computation | async-start | bytes 196608 | tf_op jit(solution)/shard_map/cond/branch_0_fun/all_to_all | solution.py:264
  21.3 3.3 %collective-permute-start = (bf16[576,128]{1,0:T(8,128)(2,1)S(1)}, bf16[576,128]{1,0:T(8,128)(2,1)S(1)}, u32[]{:S(2)}, u32[]{:S(2)}) collective-permute-start(bf16[576,128]{1,0:T(8,128)(2,1)S(1)} %get-tuple-element.57.refs_1_), channel_id=1, source_target_pairs={{0,8},{8,0},{16,24},{24,16},{32,40},{40,32},{48,56},{56,48},{64,72... | collective-permute-start | bytes 442376 | tf_op jit(solution)/shard_map/cond/branch_0_fun/ppermute | solution.py:263
  25.2 19.1 %copy-start = (bf16[832,128]{1,0:T(8,128)(2,1)S(1)}, bf16[832,128]{1,0:T(8,128)(2,1)}, u32[]{:S(2)}) copy-start(bf16[832,128]{1,0:T(8,128)(2,1)} %constant.26.clone.refs_6_) | copy-start | bytes 638980
  34.5 9.9 %copy-start.4 = (f32[6,2,16,128]{3,2,1,0:T(8,128)S(1)}, f32[6,2,16,128]{3,2,1,0:T(8,128)}, u32[]{:S(2)}) copy-start(f32[6,2,16,128]{3,2,1,0:T(8,128)} %param.12) | copy-start | bytes 294916
  35.1 8.4 %collective-permute-start.7 = (f32[32,128]{1,0:T(8,128)S(1)}, f32[32,128]{1,0:T(8,128)S(1)}, u32[]{:S(2)}, u32[]{:S(2)}) collective-permute-start(f32[32,128]{1,0:T(8,128)S(1)} %shard_map.92.refs_2_), channel_id=1, source_target_pairs={{0,504},{8,16},{16,8},{24,32},{32,24},{40,48},{48,40},{56,64},{64,... | collective-permute-start | bytes 49160 | tf_op jit(solution)/shard_map/ppermute | solution.py:244
  40.2 4.1 %collective-permute-start.6 = (f32[32,128]{1,0:T(8,128)S(1)}, f32[32,128]{1,0:T(8,128)S(1)}, u32[]{:S(2)}, u32[]{:S(2)}) collective-permute-start(f32[32,128]{1,0:T(8,128)S(1)} %shard_map.92.refs_2_), channel_id=1, source_target_pairs={{0,8},{8,0},{16,24},{24,16},{32,40},{40,32},{48,56},{56,48},{64,72... | collective-permute-start | bytes 49160 | tf_op jit(solution)/shard_map/ppermute | solution.py:245

commit v7 on v6

--- a/solution.py
+++ b/solution.py
@@ -14,8 +14,8 @@
 F32 = jnp.float32
 BF16 = jnp.bfloat16
 ROUTING_PLANES = (0, 1)
-FIRST_BLOCKS = (5, 6, 7, 0, 1, 2, 3, 4)
-SECOND_BLOCKS = (5, 6, 7, 0, 1, 2, 3, 4)
+FIRST_BLOCKS = (5, 0, 7, 6, 1, 2, 3, 4)
+SECOND_BLOCKS = (5, 0, 7, 6, 1, 2, 3, 4)
 WIDE = 3
 FAR_PAD = 400
 MEMBER_ORDER = (7, 6, 4, 5, 1, 0, 3, 2)

time: 45.8 us -> 45.7 us (level)
  starting transfers between devices: 30.2 us -> 29.7 us
    ppermute x1, starting transfers between devices: 3.32 us -> 2.81 us  [neighbours(): return (lax.ppermute(own, 'tile', near_pairs), far)]
where the time goes in v7:
time: 45.7 us; the launch traced here: 45 us
  starting transfers between devices  29.7 us (65%)
  blocking collectives  9.26 us (20%)
  Pallas kernels  4.15 us (9%)
  waiting for transfers between devices  1.8 us (4%)
    all_to_all x1, starting transfers between devices, route(): lax.all_to_all(packed, 'tile', split_axis=0, concat_axis=0, tiled=True, a...  14.9 us
    all_to_all x1, blocking collectives, per_device(): lax.all_to_all(partials, 'mem', split_axis=0, concat_axis=0, tiled=True,...  9.26 us
    ppermute x1, starting transfers between devices, neighbours(): far = lax.ppermute(own, 'tile', far_pairs)  5.18 us
    ppermute x1, starting transfers between devices, route(): far = lax.ppermute(sent_far, 'tile', far_pairs)  4.58 us
    ppermute x1, starting transfers between devices, neighbours(): return (lax.ppermute(own, 'tile', near_pairs), far)  2.81 us
    ppermute x1, starting transfers between devices, route(): near = lax.ppermute(sent, 'tile', near_pairs)  2.27 us
    pallas_call x1, Pallas kernels, route(): sent, sent_far, packed = pack(*map(in_hbm, (own, weights, *obs)))  1.78 us
    pallas_call x1, Pallas kernels, per_device(): gradient, = finish(even, own, adjoint, near, far, weights, table)  1.13 us
  transfers between devices with their start and end apart: 5, of which 2 were waited for; matrix products, arithmetic and copies ran while one was open for 0% of the time, Pallas kernels for 1%

profile of v7, /device:TPU:1, one launch (start us, length us, event | category | flops | bytes accessed | tf_op | source)
XLA Modules:
  0.0 45.0 jit_solution(187124160014603932)
XLA Ops:
  0.0 25.2 %conditional.1 = ((f32[8,48,128]{2,1,0:T(8,128)S(1)}, bf16[192,384]{1,0:T(8,128)(2,1)S(1)})) conditional(s32[]{:T(128)} %clamp.3, (s32[1,64,16]{1,2,0:T(8,128)}, f32[1,2,64,16]{2,3,1,0:T(8,128)}, f32[1,64,16]{1,2,0:T(8,128)}, f32[1,64,16]{1,2,0:T(8,128)}, f32[192,128]{1,0:T(8,128)}, /*index=5*/bf16[192,128]{1,0:T(8,128)(2,1)}, ...), branch_computations={%region_0.1_spmd, %region_1.2_spmd, %region_2.3_spmd} | conditional | flops 1000001024 | bytes 2736292 | solution.py:283
  0.0 0.0 copy-start.1
  0.0 1.8 %branch_0_fun.3 = (bf16[576,128]{1,0:T(8,128)(2,1)S(1)}, bf16[976,128]{1,0:T(8,128)(2,1)S(1)}, f32[64,1,384]{2,1,0:T(1,128)}) custom-call(f32[192,128]{1,0:T(8,128)} %get-tuple-element.50.refs_0_, bf16[192,128]{1,0:T(8,128)(2,1)} %get-tuple-element.51.refs_1_, s32[16,64]{1,0:T(8,128)} %bitcast.37, s32[1,64]{1,0:T(1,128)} %get-tuple-element.103.refs_3_, ...), custom_call_target="tpu_custom_call" | custom-call | flops 1000000000 | tf_op jit(solution)/shard_map/cond/branch_0_fun/pallas_call | solution.py:261
  1.8 4.6 %collective-permute-start.1 = (bf16[976,128]{1,0:T(8,128)(2,1)S(1)}, bf16[976,128]{1,0:T(8,128)(2,1)S(1)}, u32[]{:S(2)}, u32[]{:S(2)}) collective-permute-start(bf16[976,128]{1,0:T(8,128)(2,1)S(1)} %get-tuple-element.58), channel_id=1, source_target_pairs={{0,504},{8,16},{16,8},{24,32},{32,24},{40,48},{48,40},{56,64},{64,... | collective-permute-start | bytes 749576 | tf_op jit(solution)/shard_map/cond/branch_0_fun/ppermute | solution.py:262
  6.4 14.9 %all-to-all-start = ((f32[64,1,384]{2,1,0:T(1,128)}), f32[64,1,384]{2,1,0:T(1,128)S(1)}, u32[]{:S(2)}, u32[]{:S(2)}) async-start(f32[64,1,384]{2,1,0:T(1,128)} %get-tuple-element.61), calls=%async_computation | async-start | bytes 196608 | tf_op jit(solution)/shard_map/cond/branch_0_fun/all_to_all | solution.py:264
  21.3 2.3 %collective-permute-start = (bf16[576,128]{1,0:T(8,128)(2,1)S(1)}, bf16[576,128]{1,0:T(8,128)(2,1)S(1)}, u32[]{:S(2)}, u32[]{:S(2)}) collective-permute-start(bf16[576,128]{1,0:T(8,128)(2,1)S(1)} %get-tuple-element.57.refs_1_), channel_id=1, source_target_pairs={{0,8},{8,0},{16,24},{24,16},{32,40},{40,32},{48,56},{56,48},{64,72... | collective-permute-start | bytes 442376 | tf_op jit(solution)/shard_map/cond/branch_0_fun/ppermute | solution.py:263
  23.6 1.0 %collective-permute-done.refs_2_ = bf16[576,128]{1,0:T(8,128)(2,1)S(1)} collective-permute-done((bf16[576,128]{1,0:T(8,128)(2,1)S(1)}, bf16[576,128]{1,0:T(8,128)(2,1)S(1)}, u32[]{:S(2)}, u32[]{:S(2)}) %collective-permute-start) | collective-permute-done | bytes 147488 | tf_op jit(solution)/shard_map/cond/branch_0_fun/ppermute | solution.py:263
  24.6 0.0 collective-permute-done.1.refs_3_
  24.6 0.0 copy-done.1
  24.6 0.5 %branch_0_fun.4 = (f32[32,128]{1,0:T(8,128)S(1)}, bf16[192,384]{1,0:T(8,128)(2,1)S(1)}) custom-call(s32[1]{0:T(128)} %get-tuple-element.49.refs_0_, bf16[576,128]{1,0:T(8,128)(2,1)S(1)} %get-tuple-element.57.refs_1_, bf16[576,128]{1,0:T(8,128)(2,1)S(1)} %collective-permute-done.refs_2_, bf16[976,128]{1,0:T(8,128)(2,1)S(1)} %collective-permute-done.1.refs_3_, ...), custom_call_target="tpu_custom_call" | custom-call | flops 1000 | tf_op jit(solution)/shard_map/cond/branch_0_fun/pallas_call | solution.py:268
  25.1 0.0 all-to-all-done.obs_ref
  25.1 0.1 branch_0_fun.5
  25.2 0.0 copy-start
  25.2 9.3 %all_to_all.13.refs_0_ = f32[8,48,128]{2,1,0:T(8,128)S(1)} all-to-all(f32[8,48,128]{2,1,0:T(8,128)S(1)} %get-tuple-element.83), channel_id=1, replica_groups={{7,6,4,5,1,0,3,2},{15,14,12,13,9,8,11,10},{23,22,20,21,17,16,19,18},{31..., dimensions={0} | all-to-all | bytes 393216 | tf_op jit(solution)/shard_map/all_to_all | solution.py:286
  34.4 0.0 copy-start.4
  34.4 0.6 %shard_map.92.refs_2_ = f32[32,128]{1,0:T(8,128)S(1)} custom-call(f32[8,48,128]{2,1,0:T(8,128)S(1)} %all_to_all.13.refs_0_), custom_call_target="tpu_custom_call" | custom-call | tf_op jit(solution)/shard_map/pallas_call | solution.py:290
  35.1 5.2 %collective-permute-start.7 = (f32[32,128]{1,0:T(8,128)S(1)}, f32[32,128]{1,0:T(8,128)S(1)}, u32[]{:S(2)}, u32[]{:S(2)}) collective-permute-start(f32[32,128]{1,0:T(8,128)S(1)} %shard_map.92.refs_2_), channel_id=1, source_target_pairs={{0,504},{8,16},{16,8},{24,32},{32,24},{40,48},{48,40},{56,64},{64,... | collective-permute-start | bytes 49160 | tf_op jit(solution)/shard_map/ppermute | solution.py:244
  40.3 2.8 %collective-permute-start.6 = (f32[32,128]{1,0:T(8,128)S(1)}, f32[32,128]{1,0:T(8,128)S(1)}, u32[]{:S(2)}, u32[]{:S(2)}) collective-permute-start(f32[32,128]{1,0:T(8,128)S(1)} %shard_map.92.refs_2_), channel_id=1, source_target_pairs={{0,8},{8,0},{16,24},{24,16},{32,40},{40,32},{48,56},{56,48},{64,72... | collective-permute-start | bytes 49160 | tf_op jit(solution)/shard_map/ppermute | solution.py:245
  43.1 0.0 collective-permute-done.7.refs_4_
  43.1 0.8 %collective-permute-done.6.refs_3_ = f32[32,128]{1,0:T(8,128)S(1)} collective-permute-done((f32[32,128]{1,0:T(8,128)S(1)}, f32[32,128]{1,0:T(8,128)S(1)}, u32[]{:S(2)}, u32[]{:S(2)}) %collective-permute-start.6) | collective-permute-done | bytes 16416 | tf_op jit(solution)/shard_map/ppermute | solution.py:245
  43.9 0.0 copy-done
  43.9 0.0 copy-done.4
  43.9 1.1 %shard_map.93 = f32[192,128]{1,0:T(8,128)} custom-call(s32[1]{0:T(128)} %bitcast.24.refs_0_, f32[192,128]{1,0:T(8,128)S(1)} %bitcast.31, f32[32,128]{1,0:T(8,128)S(1)} %shard_map.92.refs_2_, f32[32,128]{1,0:T(8,128)S(1)} %collective-permute-done.6.refs_3_, f32[32,128]{1,0:T(8,128)S(1)} %collective-permute-done.7.refs_4_, ...), custom_call_target="tpu_custom_call" | custom-call | tf_op jit(solution)/shard_map/pallas_call | solution.py:293
Async XLA Ops:
  0.0 24.6 %copy-start.1 = (bf16[832,128]{1,0:T(8,128)(2,1)S(1)}, bf16[832,128]{1,0:T(8,128)(2,1)}, u32[]{:S(2)}) copy-start(bf16[832,128]{1,0:T(8,128)(2,1)} %get-tuple-element.59.refs_4_) | copy-start | bytes 638980 | tf_op jit(solution)/shard_map/cond
  1.8 22.8 %collective-permute-start.1 = (bf16[976,128]{1,0:T(8,128)(2,1)S(1)}, bf16[976,128]{1,0:T(8,128)(2,1)S(1)}, u32[]{:S(2)}, u32[]{:S(2)}) collective-permute-start(bf16[976,128]{1,0:T(8,128)(2,1)S(1)} %get-tuple-element.58), channel_id=1, source_target_pairs={{0,504},{8,16},{16,8},{24,32},{32,24},{40,48},{48,40},{56,64},{64,... | collective-permute-start | bytes 749576 | tf_op jit(solution)/shard_map/cond/branch_0_fun/ppermute | solution.py:262
  6.4 18.7 %all-to-all-start = ((f32[64,1,384]{2,1,0:T(1,128)}), f32[64,1,384]{2,1,0:T(1,128)S(1)}, u32[]{:S(2)}, u32[]{:S(2)}) async-start(f32[64,1,384]{2,1,0:T(1,128)} %get-tuple-element.61), calls=%async_computation | async-start | bytes 196608 | tf_op jit(solution)/shard_map/cond/branch_0_fun/all_to_all | solution.py:264
  21.3 3.3 %collective-permute-start = (bf16[576,128]{1,0:T(8,128)(2,1)S(1)}, bf16[576,128]{1,0:T(8,128)(2,1)S(1)}, u32[]{:S(2)}, u32[]{:S(2)}) collective-permute-start(bf16[576,128]{1,0:T(8,128)(2,1)S(1)} %get-tuple-element.57.refs_1_), channel_id=1, source_target_pairs={{0,8},{8,0},{16,24},{24,16},{32,40},{40,32},{48,56},{56,48},{64,72... | collective-permute-start | bytes 442376 | tf_op jit(solution)/shard_map/cond/branch_0_fun/ppermute | solution.py:263
  25.2 18.7 %copy-start = (bf16[832,128]{1,0:T(8,128)(2,1)S(1)}, bf16[832,128]{1,0:T(8,128)(2,1)}, u32[]{:S(2)}) copy-start(bf16[832,128]{1,0:T(8,128)(2,1)} %constant.26.clone.refs_6_) | copy-start | bytes 638980
  34.4 9.5 %copy-start.4 = (f32[6,2,16,128]{3,2,1,0:T(8,128)S(1)}, f32[6,2,16,128]{3,2,1,0:T(8,128)}, u32[]{:S(2)}) copy-start(f32[6,2,16,128]{3,2,1,0:T(8,128)} %param.12) | copy-start | bytes 294916
  35.1 8.0 %collective-permute-start.7 = (f32[32,128]{1,0:T(8,128)S(1)}, f32[32,128]{1,0:T(8,128)S(1)}, u32[]{:S(2)}, u32[]{:S(2)}) collective-permute-start(f32[32,128]{1,0:T(8,128)S(1)} %shard_map.92.refs_2_), channel_id=1, source_target_pairs={{0,504},{8,16},{16,8},{24,32},{32,24},{40,48},{48,40},{56,64},{64,... | collective-permute-start | bytes 49160 | tf_op jit(solution)/shard_map/ppermute | solution.py:244
  40.3 3.6 %collective-permute-start.6 = (f32[32,128]{1,0:T(8,128)S(1)}, f32[32,128]{1,0:T(8,128)S(1)}, u32[]{:S(2)}, u32[]{:S(2)}) collective-permute-start(f32[32,128]{1,0:T(8,128)S(1)} %shard_map.92.refs_2_), channel_id=1, source_target_pairs={{0,8},{8,0},{16,24},{24,16},{32,40},{40,32},{48,56},{56,48},{64,72... | collective-permute-start | bytes 49160 | tf_op jit(solution)/shard_map/ppermute | solution.py:245

commit v8 on v7

--- a/solution.py
+++ b/solution.py
@@ -14,8 +14,8 @@
 F32 = jnp.float32
 BF16 = jnp.bfloat16
 ROUTING_PLANES = (0, 1)
-FIRST_BLOCKS = (5, 0, 7, 6, 1, 2, 3, 4)
-SECOND_BLOCKS = (5, 0, 7, 6, 1, 2, 3, 4)
+FIRST_BLOCKS = (5, 0, 7, 1, 2, 6, 3, 4)
+SECOND_BLOCKS = (5, 0, 7, 1, 2, 6, 3, 4)
 WIDE = 3
 FAR_PAD = 400
 MEMBER_ORDER = (7, 6, 4, 5, 1, 0, 3, 2)

time: 45.7 us -> 45.7 us (level)
  no operation moved by 1% of the time
where the time goes in v8:
time: 45.7 us; the launch traced here: 45.1 us
  starting transfers between devices  29.8 us (65%)
  blocking collectives  9.26 us (20%)
  Pallas kernels  4.15 us (9%)
  waiting for transfers between devices  1.8 us (4%)
    all_to_all x1, starting transfers between devices, route(): lax.all_to_all(packed, 'tile', split_axis=0, concat_axis=0, tiled=True, a...  14.9 us
    all_to_all x1, blocking collectives, per_device(): lax.all_to_all(partials, 'mem', split_axis=0, concat_axis=0, tiled=True,...  9.26 us
    ppermute x1, starting transfers between devices, neighbours(): far = lax.ppermute(own, 'tile', far_pairs)  5.18 us
    ppermute x1, starting transfers between devices, route(): far = lax.ppermute(sent_far, 'tile', far_pairs)  4.58 us
    ppermute x1, starting transfers between devices, neighbours(): return (lax.ppermute(own, 'tile', near_pairs), far)  2.88 us
    ppermute x1, starting transfers between devices, route(): near = lax.ppermute(sent, 'tile', near_pairs)  2.27 us
    pallas_call x1, Pallas kernels, route(): sent, sent_far, packed = pack(*map(in_hbm, (own, weights, *obs)))  1.78 us
    pallas_call x1, Pallas kernels, per_device(): gradient, = finish(even, own, adjoint, near, far, weights, table)  1.13 us
  transfers between devices with their start and end apart: 5, of which 2 were waited for; matrix products, arithmetic and copies ran while one was open for 0% of the time, Pallas kernels for 1%

profile of v8, /device:TPU:1, one launch (start us, length us, event | category | flops | bytes accessed | tf_op | source)
XLA Modules:
  0.0 45.1 jit_solution(1422967565625041521)
XLA Ops:
  0.0 25.2 %conditional.1 = ((f32[8,48,128]{2,1,0:T(8,128)S(1)}, bf16[192,384]{1,0:T(8,128)(2,1)S(1)})) conditional(s32[]{:T(128)} %clamp.3, (s32[1,64,16]{1,2,0:T(8,128)}, f32[1,2,64,16]{2,3,1,0:T(8,128)}, f32[1,64,16]{1,2,0:T(8,128)}, f32[1,64,16]{1,2,0:T(8,128)}, f32[192,128]{1,0:T(8,128)}, /*index=5*/bf16[192,128]{1,0:T(8,128)(2,1)}, ...), branch_computations={%region_0.1_spmd, %region_1.2_spmd, %region_2.3_spmd} | conditional | flops 1000001024 | bytes 2736292 | solution.py:283
  0.0 0.0 copy-start.1
  0.0 1.8 %branch_0_fun.3 = (bf16[576,128]{1,0:T(8,128)(2,1)S(1)}, bf16[976,128]{1,0:T(8,128)(2,1)S(1)}, f32[64,1,384]{2,1,0:T(1,128)}) custom-call(f32[192,128]{1,0:T(8,128)} %get-tuple-element.50.refs_0_, bf16[192,128]{1,0:T(8,128)(2,1)} %get-tuple-element.51.refs_1_, s32[16,64]{1,0:T(8,128)} %bitcast.37, s32[1,64]{1,0:T(1,128)} %get-tuple-element.103.refs_3_, ...), custom_call_target="tpu_custom_call" | custom-call | flops 1000000000 | tf_op jit(solution)/shard_map/cond/branch_0_fun/pallas_call | solution.py:261
  1.8 4.6 %collective-permute-start.1 = (bf16[976,128]{1,0:T(8,128)(2,1)S(1)}, bf16[976,128]{1,0:T(8,128)(2,1)S(1)}, u32[]{:S(2)}, u32[]{:S(2)}) collective-permute-start(bf16[976,128]{1,0:T(8,128)(2,1)S(1)} %get-tuple-element.58), channel_id=1, source_target_pairs={{0,504},{8,16},{16,8},{24,32},{32,24},{40,48},{48,40},{56,64},{64,... | collective-permute-start | bytes 749576 | tf_op jit(solution)/shard_map/cond/branch_0_fun/ppermute | solution.py:262
  6.4 14.9 %all-to-all-start = ((f32[64,1,384]{2,1,0:T(1,128)}), f32[64,1,384]{2,1,0:T(1,128)S(1)}, u32[]{:S(2)}, u32[]{:S(2)}) async-start(f32[64,1,384]{2,1,0:T(1,128)} %get-tuple-element.61), calls=%async_computation | async-start | bytes 196608 | tf_op jit(solution)/shard_map/cond/branch_0_fun/all_to_all | solution.py:264
  21.3 2.3 %collective-permute-start = (bf16[576,128]{1,0:T(8,128)(2,1)S(1)}, bf16[576,128]{1,0:T(8,128)(2,1)S(1)}, u32[]{:S(2)}, u32[]{:S(2)}) collective-permute-start(bf16[576,128]{1,0:T(8,128)(2,1)S(1)} %get-tuple-element.57.refs_1_), channel_id=1, source_target_pairs={{0,8},{8,0},{16,24},{24,16},{32,40},{40,32},{48,56},{56,48},{64,72... | collective-permute-start | bytes 442376 | tf_op jit(solution)/shard_map/cond/branch_0_fun/ppermute | solution.py:263
  23.6 1.0 %collective-permute-done.refs_2_ = bf16[576,128]{1,0:T(8,128)(2,1)S(1)} collective-permute-done((bf16[576,128]{1,0:T(8,128)(2,1)S(1)}, bf16[576,128]{1,0:T(8,128)(2,1)S(1)}, u32[]{:S(2)}, u32[]{:S(2)}) %collective-permute-start) | collective-permute-done | bytes 147488 | tf_op jit(solution)/shard_map/cond/branch_0_fun/ppermute | solution.py:263
  24.6 0.0 collective-permute-done.1.refs_3_
  24.6 0.0 copy-done.1
  24.6 0.5 %branch_0_fun.4 = (f32[32,128]{1,0:T(8,128)S(1)}, bf16[192,384]{1,0:T(8,128)(2,1)S(1)}) custom-call(s32[1]{0:T(128)} %get-tuple-element.49.refs_0_, bf16[576,128]{1,0:T(8,128)(2,1)S(1)} %get-tuple-element.57.refs_1_, bf16[576,128]{1,0:T(8,128)(2,1)S(1)} %collective-permute-done.refs_2_, bf16[976,128]{1,0:T(8,128)(2,1)S(1)} %collective-permute-done.1.refs_3_, ...), custom_call_target="tpu_custom_call" | custom-call | flops 1000 | tf_op jit(solution)/shard_map/cond/branch_0_fun/pallas_call | solution.py:268
  25.1 0.0 all-to-all-done.obs_ref
  25.1 0.1 branch_0_fun.5
  25.2 0.0 copy-start
  25.2 9.3 %all_to_all.13.refs_0_ = f32[8,48,128]{2,1,0:T(8,128)S(1)} all-to-all(f32[8,48,128]{2,1,0:T(8,128)S(1)} %get-tuple-element.83), channel_id=1, replica_groups={{7,6,4,5,1,0,3,2},{15,14,12,13,9,8,11,10},{23,22,20,21,17,16,19,18},{31..., dimensions={0} | all-to-all | bytes 393216 | tf_op jit(solution)/shard_map/all_to_all | solution.py:286
  34.4 0.0 copy-start.4
  34.4 0.6 %shard_map.92.refs_2_ = f32[32,128]{1,0:T(8,128)S(1)} custom-call(f32[8,48,128]{2,1,0:T(8,128)S(1)} %all_to_all.13.refs_0_), custom_call_target="tpu_custom_call" | custom-call | tf_op jit(solution)/shard_map/pallas_call | solution.py:290
  35.1 5.2 %collective-permute-start.7 = (f32[32,128]{1,0:T(8,128)S(1)}, f32[32,128]{1,0:T(8,128)S(1)}, u32[]{:S(2)}, u32[]{:S(2)}) collective-permute-start(f32[32,128]{1,0:T(8,128)S(1)} %shard_map.92.refs_2_), channel_id=1, source_target_pairs={{0,504},{8,16},{16,8},{24,32},{32,24},{40,48},{48,40},{56,64},{64,... | collective-permute-start | bytes 49160 | tf_op jit(solution)/shard_map/ppermute | solution.py:244
  40.3 2.9 %collective-permute-start.6 = (f32[32,128]{1,0:T(8,128)S(1)}, f32[32,128]{1,0:T(8,128)S(1)}, u32[]{:S(2)}, u32[]{:S(2)}) collective-permute-start(f32[32,128]{1,0:T(8,128)S(1)} %shard_map.92.refs_2_), channel_id=1, source_target_pairs={{0,8},{8,0},{16,24},{24,16},{32,40},{40,32},{48,56},{56,48},{64,72... | collective-permute-start | bytes 49160 | tf_op jit(solution)/shard_map/ppermute | solution.py:245
  43.2 0.0 collective-permute-done.7.refs_4_
  43.2 0.8 %collective-permute-done.6.refs_3_ = f32[32,128]{1,0:T(8,128)S(1)} collective-permute-done((f32[32,128]{1,0:T(8,128)S(1)}, f32[32,128]{1,0:T(8,128)S(1)}, u32[]{:S(2)}, u32[]{:S(2)}) %collective-permute-start.6) | collective-permute-done | bytes 16416 | tf_op jit(solution)/shard_map/ppermute | solution.py:245
  44.0 0.0 copy-done
  44.0 0.0 copy-done.4
  44.0 1.1 %shard_map.93 = f32[192,128]{1,0:T(8,128)} custom-call(s32[1]{0:T(128)} %bitcast.24.refs_0_, f32[192,128]{1,0:T(8,128)S(1)} %bitcast.31, f32[32,128]{1,0:T(8,128)S(1)} %shard_map.92.refs_2_, f32[32,128]{1,0:T(8,128)S(1)} %collective-permute-done.6.refs_3_, f32[32,128]{1,0:T(8,128)S(1)} %collective-permute-done.7.refs_4_, ...), custom_call_target="tpu_custom_call" | custom-call | tf_op jit(solution)/shard_map/pallas_call | solution.py:293
Async XLA Ops:
  0.0 24.6 %copy-start.1 = (bf16[832,128]{1,0:T(8,128)(2,1)S(1)}, bf16[832,128]{1,0:T(8,128)(2,1)}, u32[]{:S(2)}) copy-start(bf16[832,128]{1,0:T(8,128)(2,1)} %get-tuple-element.59.refs_4_) | copy-start | bytes 638980 | tf_op jit(solution)/shard_map/cond
  1.8 22.8 %collective-permute-start.1 = (bf16[976,128]{1,0:T(8,128)(2,1)S(1)}, bf16[976,128]{1,0:T(8,128)(2,1)S(1)}, u32[]{:S(2)}, u32[]{:S(2)}) collective-permute-start(bf16[976,128]{1,0:T(8,128)(2,1)S(1)} %get-tuple-element.58), channel_id=1, source_target_pairs={{0,504},{8,16},{16,8},{24,32},{32,24},{40,48},{48,40},{56,64},{64,... | collective-permute-start | bytes 749576 | tf_op jit(solution)/shard_map/cond/branch_0_fun/ppermute | solution.py:262
  6.4 18.7 %all-to-all-start = ((f32[64,1,384]{2,1,0:T(1,128)}), f32[64,1,384]{2,1,0:T(1,128)S(1)}, u32[]{:S(2)}, u32[]{:S(2)}) async-start(f32[64,1,384]{2,1,0:T(1,128)} %get-tuple-element.61), calls=%async_computation | async-start | bytes 196608 | tf_op jit(solution)/shard_map/cond/branch_0_fun/all_to_all | solution.py:264
  21.3 3.3 %collective-permute-start = (bf16[576,128]{1,0:T(8,128)(2,1)S(1)}, bf16[576,128]{1,0:T(8,128)(2,1)S(1)}, u32[]{:S(2)}, u32[]{:S(2)}) collective-permute-start(bf16[576,128]{1,0:T(8,128)(2,1)S(1)} %get-tuple-element.57.refs_1_), channel_id=1, source_target_pairs={{0,8},{8,0},{16,24},{24,16},{32,40},{40,32},{48,56},{56,48},{64,72... | collective-permute-start | bytes 442376 | tf_op jit(solution)/shard_map/cond/branch_0_fun/ppermute | solution.py:263
  25.2 18.8 %copy-start = (bf16[832,128]{1,0:T(8,128)(2,1)S(1)}, bf16[832,128]{1,0:T(8,128)(2,1)}, u32[]{:S(2)}) copy-start(bf16[832,128]{1,0:T(8,128)(2,1)} %constant.26.clone.refs_6_) | copy-start | bytes 638980
  34.4 9.5 %copy-start.4 = (f32[6,2,16,128]{3,2,1,0:T(8,128)S(1)}, f32[6,2,16,128]{3,2,1,0:T(8,128)}, u32[]{:S(2)}) copy-start(f32[6,2,16,128]{3,2,1,0:T(8,128)} %param.12) | copy-start | bytes 294916
  35.1 8.1 %collective-permute-start.7 = (f32[32,128]{1,0:T(8,128)S(1)}, f32[32,128]{1,0:T(8,128)S(1)}, u32[]{:S(2)}, u32[]{:S(2)}) collective-permute-start(f32[32,128]{1,0:T(8,128)S(1)} %shard_map.92.refs_2_), channel_id=1, source_target_pairs={{0,504},{8,16},{16,8},{24,32},{32,24},{40,48},{48,40},{56,64},{64,... | collective-permute-start | bytes 49160 | tf_op jit(solution)/shard_map/ppermute | solution.py:244
  40.3 3.7 %collective-permute-start.6 = (f32[32,128]{1,0:T(8,128)S(1)}, f32[32,128]{1,0:T(8,128)S(1)}, u32[]{:S(2)}, u32[]{:S(2)}) collective-permute-start(f32[32,128]{1,0:T(8,128)S(1)} %shard_map.92.refs_2_), channel_id=1, source_target_pairs={{0,8},{8,0},{16,24},{24,16},{32,40},{40,32},{48,56},{56,48},{64,72... | collective-permute-start | bytes 49160 | tf_op jit(solution)/shard_map/ppermute | solution.py:245

commit v9 on v8

--- a/solution.py
+++ b/solution.py
@@ -14,8 +14,8 @@
 F32 = jnp.float32
 BF16 = jnp.bfloat16
 ROUTING_PLANES = (0, 1)
-FIRST_BLOCKS = (5, 0, 7, 1, 2, 6, 3, 4)
-SECOND_BLOCKS = (5, 0, 7, 1, 2, 6, 3, 4)
+FIRST_BLOCKS = (5, 0, 1, 2, 3, 4, 6, 7)
+SECOND_BLOCKS = (5, 0, 7, 2, 4, 6, 1, 3)
 WIDE = 3
 FAR_PAD = 400
 MEMBER_ORDER = (7, 6, 4, 5, 1, 0, 3, 2)

time: 45.7 us -> 45.7 us (level)
  no operation moved by 1% of the time
where the time goes in v9:
time: 45.7 us; the launch traced here: 45.1 us
  starting transfers between devices  29.8 us (65%)
  blocking collectives  9.26 us (20%)
  Pallas kernels  4.15 us (9%)
  waiting for transfers between devices  1.8 us (4%)
    all_to_all x1, starting transfers between devices, route(): lax.all_to_all(packed, 'tile', split_axis=0, concat_axis=0, tiled=True, a...  14.9 us
    all_to_all x1, blocking collectives, per_device(): lax.all_to_all(partials, 'mem', split_axis=0, concat_axis=0, tiled=True,...  9.26 us
    ppermute x1, starting transfers between devices, neighbours(): far = lax.ppermute(own, 'tile', far_pairs)  5.07 us
    ppermute x1, starting transfers between devices, route(): far = lax.ppermute(sent_far, 'tile', far_pairs)  4.58 us
    ppermute x1, starting transfers between devices, neighbours(): return (lax.ppermute(own, 'tile', near_pairs), far)  2.95 us
    ppermute x1, starting transfers between devices, route(): near = lax.ppermute(sent, 'tile', near_pairs)  2.27 us
    pallas_call x1, Pallas kernels, route(): sent, sent_far, packed = pack(*map(in_hbm, (own, weights, *obs)))  1.78 us
    pallas_call x1, Pallas kernels, per_device(): gradient, = finish(even, own, adjoint, near, far, weights, table)  1.13 us
  transfers between devices with their start and end apart: 5, of which 2 were waited for; matrix products, arithmetic and copies ran while one was open for 0% of the time, Pallas kernels for 1%

profile of v9, /device:TPU:1, one launch (start us, length us, event | category | flops | bytes accessed | tf_op | source)
XLA Modules:
  0.0 45.1 jit_solution(16897833959129987069)
XLA Ops:
  0.0 25.2 %conditional.1 = ((f32[8,48,128]{2,1,0:T(8,128)S(1)}, bf16[192,384]{1,0:T(8,128)(2,1)S(1)})) conditional(s32[]{:T(128)} %clamp.3, (s32[1,64,16]{1,2,0:T(8,128)}, f32[1,2,64,16]{2,3,1,0:T(8,128)}, f32[1,64,16]{1,2,0:T(8,128)}, f32[1,64,16]{1,2,0:T(8,128)}, f32[192,128]{1,0:T(8,128)}, /*index=5*/bf16[192,128]{1,0:T(8,128)(2,1)}, ...), branch_computations={%region_0.1_spmd, %region_1.2_spmd, %region_2.3_spmd} | conditional | flops 1000001024 | bytes 2736292 | solution.py:283
  0.0 0.0 copy-start.1
  0.0 1.8 %branch_0_fun.3 = (bf16[576,128]{1,0:T(8,128)(2,1)S(1)}, bf16[976,128]{1,0:T(8,128)(2,1)S(1)}, f32[64,1,384]{2,1,0:T(1,128)}) custom-call(f32[192,128]{1,0:T(8,128)} %get-tuple-element.50.refs_0_, bf16[192,128]{1,0:T(8,128)(2,1)} %get-tuple-element.51.refs_1_, s32[16,64]{1,0:T(8,128)} %bitcast.37, s32[1,64]{1,0:T(1,128)} %get-tuple-element.103.refs_3_, ...), custom_call_target="tpu_custom_call" | custom-call | flops 1000000000 | tf_op jit(solution)/shard_map/cond/branch_0_fun/pallas_call | solution.py:261
  1.8 4.6 %collective-permute-start.1 = (bf16[976,128]{1,0:T(8,128)(2,1)S(1)}, bf16[976,128]{1,0:T(8,128)(2,1)S(1)}, u32[]{:S(2)}, u32[]{:S(2)}) collective-permute-start(bf16[976,128]{1,0:T(8,128)(2,1)S(1)} %get-tuple-element.58), channel_id=1, source_target_pairs={{0,504},{8,16},{16,8},{24,32},{32,24},{40,48},{48,40},{56,64},{64,... | collective-permute-start | bytes 749576 | tf_op jit(solution)/shard_map/cond/branch_0_fun/ppermute | solution.py:262
  6.4 14.9 %all-to-all-start = ((f32[64,1,384]{2,1,0:T(1,128)}), f32[64,1,384]{2,1,0:T(1,128)S(1)}, u32[]{:S(2)}, u32[]{:S(2)}) async-start(f32[64,1,384]{2,1,0:T(1,128)} %get-tuple-element.61), calls=%async_computation | async-start | bytes 196608 | tf_op jit(solution)/shard_map/cond/branch_0_fun/all_to_all | solution.py:264
  21.3 2.3 %collective-permute-start = (bf16[576,128]{1,0:T(8,128)(2,1)S(1)}, bf16[576,128]{1,0:T(8,128)(2,1)S(1)}, u32[]{:S(2)}, u32[]{:S(2)}) collective-permute-start(bf16[576,128]{1,0:T(8,128)(2,1)S(1)} %get-tuple-element.57.refs_1_), channel_id=1, source_target_pairs={{0,8},{8,0},{16,24},{24,16},{32,40},{40,32},{48,56},{56,48},{64,72... | collective-permute-start | bytes 442376 | tf_op jit(solution)/shard_map/cond/branch_0_fun/ppermute | solution.py:263
  23.6 1.0 %collective-permute-done.refs_2_ = bf16[576,128]{1,0:T(8,128)(2,1)S(1)} collective-permute-done((bf16[576,128]{1,0:T(8,128)(2,1)S(1)}, bf16[576,128]{1,0:T(8,128)(2,1)S(1)}, u32[]{:S(2)}, u32[]{:S(2)}) %collective-permute-start) | collective-permute-done | bytes 147488 | tf_op jit(solution)/shard_map/cond/branch_0_fun/ppermute | solution.py:263
  24.6 0.0 collective-permute-done.1.refs_3_
  24.6 0.0 copy-done.1
  24.6 0.5 %branch_0_fun.4 = (f32[32,128]{1,0:T(8,128)S(1)}, bf16[192,384]{1,0:T(8,128)(2,1)S(1)}) custom-call(s32[1]{0:T(128)} %get-tuple-element.49.refs_0_, bf16[576,128]{1,0:T(8,128)(2,1)S(1)} %get-tuple-element.57.refs_1_, bf16[576,128]{1,0:T(8,128)(2,1)S(1)} %collective-permute-done.refs_2_, bf16[976,128]{1,0:T(8,128)(2,1)S(1)} %collective-permute-done.1.refs_3_, ...), custom_call_target="tpu_custom_call" | custom-call | flops 1000 | tf_op jit(solution)/shard_map/cond/branch_0_fun/pallas_call | solution.py:268
  25.1 0.0 all-to-all-done.obs_ref
  25.1 0.1 branch_0_fun.5
  25.2 0.0 copy-start
  25.2 9.3 %all_to_all.13.refs_0_ = f32[8,48,128]{2,1,0:T(8,128)S(1)} all-to-all(f32[8,48,128]{2,1,0:T(8,128)S(1)} %get-tuple-element.83), channel_id=1, replica_groups={{7,6,4,5,1,0,3,2},{15,14,12,13,9,8,11,10},{23,22,20,21,17,16,19,18},{31..., dimensions={0} | all-to-all | bytes 393216 | tf_op jit(solution)/shard_map/all_to_all | solution.py:286
  34.4 0.0 copy-start.4
  34.4 0.6 %shard_map.92.refs_2_ = f32[32,128]{1,0:T(8,128)S(1)} custom-call(f32[8,48,128]{2,1,0:T(8,128)S(1)} %all_to_all.13.refs_0_), custom_call_target="tpu_custom_call" | custom-call | tf_op jit(solution)/shard_map/pallas_call | solution.py:290
  35.1 5.1 %collective-permute-start.7 = (f32[32,128]{1,0:T(8,128)S(1)}, f32[32,128]{1,0:T(8,128)S(1)}, u32[]{:S(2)}, u32[]{:S(2)}) collective-permute-start(f32[32,128]{1,0:T(8,128)S(1)} %shard_map.92.refs_2_), channel_id=1, source_target_pairs={{0,504},{8,16},{16,8},{24,32},{32,24},{40,48},{48,40},{56,64},{64,... | collective-permute-start | bytes 49160 | tf_op jit(solution)/shard_map/ppermute | solution.py:244
  40.2 2.9 %collective-permute-start.6 = (f32[32,128]{1,0:T(8,128)S(1)}, f32[32,128]{1,0:T(8,128)S(1)}, u32[]{:S(2)}, u32[]{:S(2)}) collective-permute-start(f32[32,128]{1,0:T(8,128)S(1)} %shard_map.92.refs_2_), channel_id=1, source_target_pairs={{0,8},{8,0},{16,24},{24,16},{32,40},{40,32},{48,56},{56,48},{64,72... | collective-permute-start | bytes 49160 | tf_op jit(solution)/shard_map/ppermute | solution.py:245
  43.1 0.0 collective-permute-done.7.refs_4_
  43.1 0.8 %collective-permute-done.6.refs_3_ = f32[32,128]{1,0:T(8,128)S(1)} collective-permute-done((f32[32,128]{1,0:T(8,128)S(1)}, f32[32,128]{1,0:T(8,128)S(1)}, u32[]{:S(2)}, u32[]{:S(2)}) %collective-permute-start.6) | collective-permute-done | bytes 16416 | tf_op jit(solution)/shard_map/ppermute | solution.py:245
  43.9 0.0 copy-done
  43.9 0.0 copy-done.4
  43.9 1.1 %shard_map.93 = f32[192,128]{1,0:T(8,128)} custom-call(s32[1]{0:T(128)} %bitcast.24.refs_0_, f32[192,128]{1,0:T(8,128)S(1)} %bitcast.31, f32[32,128]{1,0:T(8,128)S(1)} %shard_map.92.refs_2_, f32[32,128]{1,0:T(8,128)S(1)} %collective-permute-done.6.refs_3_, f32[32,128]{1,0:T(8,128)S(1)} %collective-permute-done.7.refs_4_, ...), custom_call_target="tpu_custom_call" | custom-call | tf_op jit(solution)/shard_map/pallas_call | solution.py:293
Async XLA Ops:
  0.0 24.6 %copy-start.1 = (bf16[832,128]{1,0:T(8,128)(2,1)S(1)}, bf16[832,128]{1,0:T(8,128)(2,1)}, u32[]{:S(2)}) copy-start(bf16[832,128]{1,0:T(8,128)(2,1)} %get-tuple-element.59.refs_4_) | copy-start | bytes 638980 | tf_op jit(solution)/shard_map/cond
  1.8 22.8 %collective-permute-start.1 = (bf16[976,128]{1,0:T(8,128)(2,1)S(1)}, bf16[976,128]{1,0:T(8,128)(2,1)S(1)}, u32[]{:S(2)}, u32[]{:S(2)}) collective-permute-start(bf16[976,128]{1,0:T(8,128)(2,1)S(1)} %get-tuple-element.58), channel_id=1, source_target_pairs={{0,504},{8,16},{16,8},{24,32},{32,24},{40,48},{48,40},{56,64},{64,... | collective-permute-start | bytes 749576 | tf_op jit(solution)/shard_map/cond/branch_0_fun/ppermute | solution.py:262
  6.4 18.7 %all-to-all-start = ((f32[64,1,384]{2,1,0:T(1,128)}), f32[64,1,384]{2,1,0:T(1,128)S(1)}, u32[]{:S(2)}, u32[]{:S(2)}) async-start(f32[64,1,384]{2,1,0:T(1,128)} %get-tuple-element.61), calls=%async_computation | async-start | bytes 196608 | tf_op jit(solution)/shard_map/cond/branch_0_fun/all_to_all | solution.py:264
  21.3 3.3 %collective-permute-start = (bf16[576,128]{1,0:T(8,128)(2,1)S(1)}, bf16[576,128]{1,0:T(8,128)(2,1)S(1)}, u32[]{:S(2)}, u32[]{:S(2)}) collective-permute-start(bf16[576,128]{1,0:T(8,128)(2,1)S(1)} %get-tuple-element.57.refs_1_), channel_id=1, source_target_pairs={{0,8},{8,0},{16,24},{24,16},{32,40},{40,32},{48,56},{56,48},{64,72... | collective-permute-start | bytes 442376 | tf_op jit(solution)/shard_map/cond/branch_0_fun/ppermute | solution.py:263
  25.2 18.8 %copy-start = (bf16[832,128]{1,0:T(8,128)(2,1)S(1)}, bf16[832,128]{1,0:T(8,128)(2,1)}, u32[]{:S(2)}) copy-start(bf16[832,128]{1,0:T(8,128)(2,1)} %constant.26.clone.refs_6_) | copy-start | bytes 638980
  34.4 9.5 %copy-start.4 = (f32[6,2,16,128]{3,2,1,0:T(8,128)S(1)}, f32[6,2,16,128]{3,2,1,0:T(8,128)}, u32[]{:S(2)}) copy-start(f32[6,2,16,128]{3,2,1,0:T(8,128)} %param.12) | copy-start | bytes 294916
  35.1 8.0 %collective-permute-start.7 = (f32[32,128]{1,0:T(8,128)S(1)}, f32[32,128]{1,0:T(8,128)S(1)}, u32[]{:S(2)}, u32[]{:S(2)}) collective-permute-start(f32[32,128]{1,0:T(8,128)S(1)} %shard_map.92.refs_2_), channel_id=1, source_target_pairs={{0,504},{8,16},{16,8},{24,32},{32,24},{40,48},{48,40},{56,64},{64,... | collective-permute-start | bytes 49160 | tf_op jit(solution)/shard_map/ppermute | solution.py:244
  40.2 3.8 %collective-permute-start.6 = (f32[32,128]{1,0:T(8,128)S(1)}, f32[32,128]{1,0:T(8,128)S(1)}, u32[]{:S(2)}, u32[]{:S(2)}) collective-permute-start(f32[32,128]{1,0:T(8,128)S(1)} %shard_map.92.refs_2_), channel_id=1, source_target_pairs={{0,8},{8,0},{16,24},{24,16},{32,40},{40,32},{48,56},{56,48},{64,72... | collective-permute-start | bytes 49160 | tf_op jit(solution)/shard_map/ppermute | solution.py:245
